TPU v7x, 128 devices: a whole 4x4x4 slice. The times are simulated.
128 devices in a mesh: grp: 2 (over y_hi), dev: 64 (over z, x, y_lo, core).
Axes of the slice: x: 4, y: 4 (y_hi: 2, y_lo: 2; y = y_hi * 2 + y_lo), z: 4, core: 2. Of those that a mesh axis runs over, the one named last changes fastest.
Arguments:
- hidden: bfloat16 [512, 7168], P(('grp', 'dev')), may hold values from -6 to 6
- queries: bfloat16 [512, 16384], P(('grp', 'dev')), may hold values from -120 to 120
- new_key: bfloat16 [512, 256], P(('grp', 'dev')), may hold values from -6 to 6
- new_value: bfloat16 [512, 256], P(('grp', 'dev')), may hold values from -6 to 6
- cache_keys: bfloat16 [512, 2048, 256], P(('grp', 'dev')), may hold values from -6 to 6
- cache_values: bfloat16 [512, 2048, 256], P(('grp', 'dev')), may hold values from -6 to 6
- lengths: int32 [512], P(('grp', 'dev')), may hold values from 2 to 2048, as said below
- out_weight: bfloat16 [16384, 7168], P(None, 'dev'), may hold values from -0.375 to 0.375
- ffn_gain: float32 [7168], replicated, may hold values from 0.5 to 1.5
- gate_weight: bfloat16 [7168, 40960], P(None, ('grp', 'dev')), may hold values from -0.0625 to 0.0625
- up_weight: bfloat16 [7168, 40960], P(None, ('grp', 'dev')), may hold values from -0.0625 to 0.0625
- down_weight: bfloat16 [40960, 7168], P(('grp', 'dev')), may hold values from -0.078125 to 0.078125
- routes: int32 [512, 3], P(('grp', 'dev')), may hold values from 0 to 7, as said below
- route_gates: int32 [512, 3], P(('grp', 'dev')), may hold values from 1 to 255
Outputs:
- layer_out: bfloat16 [512, 7168], P(('grp', 'dev'))
Inputs may be any that keep to these rules, and one draw needn't show every extreme that they name: `lengths`: some row has all 2048 positions filled. `routes`: each row names 3 different experts; among the rows of one device no expert is named by more than 2 rows, and one expert, the same for all devices and drawn afresh, is named by exactly 2 rows of every device.
All inputs are finite; a program needn't handle non-finite values.
Results may differ from a plain program's by a relative error of at most 0.0095.
Values may be sent and summed in bfloat16 or wider, within the bound.
No kernel may reach another device: no remote copies, remote signals or barrier semaphores. Data moves between devices by JAX's collectives and lax.ppermute only.
A program may use at most 128 MiB of HBM per device.

v0:
```python
import math

import jax
import jax.numpy as jnp
from jax import lax
from jax.sharding import PartitionSpec as P

HID = 5120
EXPERTS = 8


def attend(queries, new_key, new_value, cache_keys, cache_values, lengths):
    row_count = queries.shape[0]
    head_size = new_key.shape[1]
    head_count = queries.shape[1] // head_size
    context = cache_keys.shape[1]
    queried = queries.reshape(row_count, head_count, head_size)
    scaling = 1.0 / math.sqrt(head_size)
    cached = (
        jnp.einsum("rhd,rpd->rhp", queried, cache_keys, preferred_element_type=jnp.float32)
        * scaling
    )
    itself = (
        jnp.einsum("rhd,rd->rh", queried, new_key, preferred_element_type=jnp.float32) * scaling
    )
    position = lax.broadcasted_iota(jnp.int32, (1, 1, context), 2)
    cached = jnp.where(position < lengths[:, None, None], cached, -jnp.inf)
    highest = jnp.maximum(jnp.max(cached, axis=2), itself)
    cached_exp = jnp.exp(cached - highest[:, :, None])
    itself_exp = jnp.exp(itself - highest)
    totals = jnp.sum(cached_exp, axis=2) + itself_exp
    cached_probs = (cached_exp / totals[:, :, None]).astype(jnp.bfloat16)
    itself_probs = (itself_exp / totals).astype(jnp.bfloat16)
    mixture = jnp.einsum(
        "rhp,rpd->rhd", cached_probs, cache_values, preferred_element_type=jnp.float32
    )
    mixture = (
        mixture
        + itself_probs.astype(jnp.float32)[:, :, None] * new_value.astype(jnp.float32)[:, None, :]
    )
    return mixture.astype(jnp.bfloat16).reshape(row_count, head_count * head_size)


def expert_rows(normed_rows, gate_weight, up_weight, down_weight):
    gated = jnp.dot(normed_rows, gate_weight, preferred_element_type=jnp.float32)
    upward = jnp.dot(normed_rows, up_weight, preferred_element_type=jnp.float32)
    activated = (jax.nn.silu(gated) * upward).astype(jnp.bfloat16)
    return jnp.dot(activated, down_weight, preferred_element_type=jnp.float32)


def expert_term(normed_rows, gate_table, gate_weight, up_weight, down_weight, expert_index):
    table = gate_table.astype(jnp.float32)
    expert_ids = lax.broadcasted_iota(jnp.int32, (1, table.shape[1]), 1)
    mine = jnp.sum(jnp.where(expert_ids == expert_index, table, 0.0), axis=-1)
    chosen = mine / jnp.sum(table, axis=-1)
    return chosen[:, None] * expert_rows(normed_rows, gate_weight, up_weight, down_weight)


def per_device(
    hidden,
    queries,
    new_key,
    new_value,
    cache_keys,
    cache_values,
    lengths,
    out_weight,
    ffn_gain,
    gate_weight,
    up_weight,
    down_weight,
    routes,
    route_gates,
):
    attended = attend(queries, new_key, new_value, cache_keys, cache_values, lengths)
    columns = jnp.dot(
        lax.all_gather(attended, "dev", axis=0, tiled=True),
        out_weight,
        preferred_element_type=jnp.float32,
    )
    projected = lax.all_to_all(columns, "dev", split_axis=0, concat_axis=1, tiled=True)
    mixed = (hidden.astype(jnp.float32) + projected).astype(jnp.bfloat16)
    widened = lax.optimization_barrier(mixed).astype(jnp.float32)
    mean_square = jnp.mean(widened * widened, axis=-1, keepdims=True)
    normed = (widened * lax.rsqrt(mean_square + 1e-05) * ffn_gain).astype(jnp.bfloat16)
    shards_per = HID // gate_weight.shape[1]
    flat_index = lax.axis_index("grp") * lax.axis_size("dev") + lax.axis_index("dev")
    expert_index = flat_index // shards_per
    expert_ids = lax.broadcasted_iota(jnp.int32, (1, 1, EXPERTS), 2)
    named = routes[:, :, None] == expert_ids
    gate_table = jnp.sum(jnp.where(named, route_gates[:, :, None], 0), axis=1).astype(jnp.bfloat16)
    all_normed, all_table = (
        lax.all_gather(normed, ("grp", "dev"), axis=0, tiled=True),
        lax.all_gather(gate_table, ("grp", "dev"), axis=0, tiled=True),
    )
    combined = lax.psum_scatter(
        expert_term(all_normed, all_table, gate_weight, up_weight, down_weight, expert_index),
        ("grp", "dev"),
        scatter_dimension=0,
        tiled=True,
    )
    return (widened + combined).astype(jnp.bfloat16)


def solution(mesh):
    return jax.shard_map(
        per_device,
        mesh=mesh,
        in_specs=(
            P(("grp", "dev"), None),
            P(("grp", "dev"), None),
            P(("grp", "dev"), None),
            P(("grp", "dev"), None),
            P(("grp", "dev"), None, None),
            P(("grp", "dev"), None, None),
            P(("grp", "dev")),
            P(None, "dev"),
            P(),
            P(None, ("grp", "dev")),
            P(None, ("grp", "dev")),
            P(("grp", "dev"), None),
            P(("grp", "dev"), None),
            P(("grp", "dev"), None),
        ),
        out_specs=P(("grp", "dev"), None),
        check_vma=False,
    )
```

profile of v0, /device:TPU:0, one launch (start us, length us, event | category | flops | bytes accessed | tf_op | source)
XLA Modules:
  0.0 582.4 jit_solution(1219727923698923569)
XLA Ops:
  6.5 0.9 iota_compare_fusion
  7.4 0.0 copy-done
  7.4 1.4 fusion.6
  8.9 3.8 fusion.20
  12.6 0.4 fusion.1
  13.1 0.9 fusion.3
  14.0 0.7 reshape.57
  14.7 0.0 all-gather.6.cloned.1.call-update
  14.7 0.0 all-gather.8.cloned.1.call-start
  14.8 114.2 %all-gather.6.cloned.1.call-done = bf16[64,4,16384]{2,1,0:T(4,128)(2,1)} async-done(((bf16[1,4,16384]{2,1,0:T(4,128)(2,1)}), bf16[64,4,16384]{2,1,0:T(4,128)(2,1)}) %all-gather.6.cloned.1.call-update) | async-done | bytes 8388624 | tf_op jit(solution)/shard_map/all_gather | solution.py:77
  129.0 12.5 %reshape.58 = bf16[256,16384]{1,0:T(8,128)(2,1)} reshape(bf16[64,4,16384]{2,1,0:T(4,128)(2,1)} %all-gather.6.cloned.1.call-done) | data formatting | bytes 16777216
  141.5 6.8 %fusion.21 = f32[256,112]{1,0:T(8,128)S(1)} fusion(bf16[256,16384]{1,0:T(8,128)(2,1)} %reshape.58, bf16[16384,112]{0,1:T(8,128)(2,1)} %param.21), kind=kOutput, calls=%fused_computation.42 | convolution fusion | flops 939524096 | bytes 12173312 | tf_op jit(solution)/shard_map/dot_general | solution.py:76
  148.3 14.3 %all_to_all.19 = f32[64,4,112]{2,1,0:T(4,128)S(1)} all-to-all(f32[64,4,112]{2,1,0:T(4,128)S(1)} %bitcast.30), channel_id=1, replica_groups=mesh['grp'=2,'dev'=64] {'dev'}, dimensions={0} | all-to-all | bytes 229376 | tf_op jit(solution)/shard_map/all_to_all | solution.py:81
  162.6 0.2 all_to_all.17
  162.8 0.2 fusion.11
  163.0 0.7 fusion.15
  163.7 0.0 all-gather.8.cloned.1.call-update
  163.7 0.0 all-reduce.3.cloned.1.call-start
  163.8 0.1 copy.23
  163.9 0.1 copy.24
  164.0 0.1 select_reduce_fusion.1
  164.1 173.6 %all-gather.1 = bf16[128,4,8]{2,1,0:T(4,128)(2,1)S(1)} all-gather(bf16[1,4,8]{2,1,0:T(4,128)(2,1)S(1)} %convert_bitcast_fusion), channel_id=1, replica_groups=mesh['grp'=2,'dev'=64] {'grp','dev'}, dimensions={0}, use_global_device_ids=true | all-gather | bytes 8256 | tf_op jit(solution)/shard_map/all_gather | solution.py:94
  337.7 0.2 convert_reduce_fusion
  337.9 0.1 reshape.65
  338.1 0.1 select_reduce_fusion
  338.2 25.7 %all-gather.8.cloned.1.call-done = bf16[128,4,7168]{2,1,0:T(4,128)(2,1)} async-done(((bf16[1,4,7168]{2,1,0:T(4,128)(2,1)}), bf16[128,4,7168]{2,1,0:T(4,128)(2,1)}) %all-gather.8.cloned.1.call-update) | async-done | bytes 7340048 | tf_op jit(solution)/shard_map/all_gather | solution.py:93
  363.9 12.1 %reshape.62 = bf16[512,7168]{1,0:T(8,128)(2,1)} reshape(bf16[128,4,7168]{2,1,0:T(4,128)(2,1)} %all-gather.8.cloned.1.call-done) | data formatting | bytes 14680064
  376.0 6.9 %fusion.22 = f32[512,320]{0,1:T(8,128)S(1)} fusion(bf16[512,7168]{1,0:T(8,128)(2,1)} %reshape.62, bf16[7168,320]{0,1:T(8,128)(2,1)} %param.23), kind=kOutput, calls=%fused_computation.43 | convolution fusion | flops 2348810240 | bytes 12582912 | tf_op jit(solution)/shard_map/dot_general | solution.py:45
  382.9 19.5 %convolution_multiply_fusion = f32[512,7168]{1,0:T(8,128)} fusion(bf16[320,7168]{1,0:T(8,128)(2,1)} %param.25, f32[512]{0:T(512)S(1)} %div.39, bf16[512,7168]{1,0:T(8,128)(2,1)} %reshape.62, bf16[7168,320]{0,1:T(8,128)(2,1)} %param.24, f32[512,320]{0,1:T(8,128)S(1)} %fusion.22), kind=kOutput, calls=%fused_computation | convolution fusion | flops 4702273536 | bytes 31852544 | tf_op jit(solution)/shard_map/dot_general | solution.py:48
  402.4 0.0 all-reduce.3.cloned.1.call-update
  402.4 171.8 %all-reduce.3.cloned.1.call-done = f32[512,7168]{1,0:T(8,128)} async-done(((f32[512,7168]{1,0:T(8,128)}), f32[512,7168]{1,0:T(8,128)}) %all-reduce.3.cloned.1.call-update) | async-done | bytes 14680080
  574.2 1.6 fusion.14
  (25 shorter events, 0.1 us)
Async XLA Ops:
  6.5 0.9 copy-start
  6.5 6.6 %copy-start.4 = (bf16[4,256]{1,0:T(4,128)(2,1)S(1)}, bf16[4,256]{1,0:T(4,128)(2,1)}, u32[]{:S(2)}) copy-start(bf16[4,256]{1,0:T(4,128)(2,1)} %param.17) | copy-start | bytes 6148
  6.5 122.5 %all-gather.6.cloned.1.call-start = ((), (), s32[]{:S(2)}) async-start(), calls=%async_computation.1 | async-start | bytes 8519680 | tf_op jit(solution)/shard_map/all_gather | solution.py:77
  6.5 6.6 %copy-start.7 = (bf16[4,2048,256]{2,1,0:T(8,128)(2,1)S(1)}, bf16[4,2048,256]{2,1,0:T(8,128)(2,1)}, u32[]{:S(2)}) copy-start(bf16[4,2048,256]{2,1,0:T(8,128)(2,1)} %param.19) | copy-start | bytes 12582916
  14.7 349.1 %all-gather.8.cloned.1.call-start = ((), (), s32[]{:S(2)}) async-start(), calls=%async_computation.2 | async-start | bytes 7397376 | tf_op jit(solution)/shard_map/all_gather | solution.py:93
  141.5 21.2 %copy-start.2 = (bf16[4,7168]{1,0:T(4,128)(2,1)S(1)}, bf16[4,7168]{1,0:T(4,128)(2,1)}, u32[]{:S(2)}) copy-start(bf16[4,7168]{1,0:T(4,128)(2,1)} %param.14) | copy-start | bytes 172036
  141.5 21.5 %copy-start.3 = (f32[7168]{0:T(1024)S(1)}, f32[7168]{0:T(1024)}, u32[]{:S(2)}) copy-start(f32[7168]{0:T(1024)} %param.22) | copy-start | bytes 86020
  141.5 22.3 %copy-start.5 = (s32[4,3]{1,0:T(4,128)S(1)}, s32[4,3]{1,0:T(4,128)}, u32[]{:S(2)}) copy-start(s32[4,3]{1,0:T(4,128)} %param.26) | copy-start | bytes 148
  141.5 22.4 %copy-start.6 = (s32[4,3]{1,0:T(4,128)S(1)}, s32[4,3]{1,0:T(4,128)}, u32[]{:S(2)}) copy-start(s32[4,3]{1,0:T(4,128)} %param.27) | copy-start | bytes 148
  163.7 410.5 %all-reduce.3.cloned.1.call-start = ((), (), s32[]{:S(2)}) async-start(), calls=%async_computation.3 | async-start | bytes 29360128
  402.4 173.4 %copy-start.1 = (bf16[4,256]{1,0:T(4,128)(2,1)S(1)}, bf16[4,256]{1,0:T(4,128)(2,1)}, u32[]{:S(2)}) copy-start(bf16[4,256]{1,0:T(4,128)(2,1)} %param.16) | copy-start | bytes 6148
Sparse Core Ops, SparseCore 0:
  14.9 114.0 all-gather.5
  163.9 199.9 all-gather.7
  402.6 171.6 all-reduce.2
where the time goes:
time: 584 us; the launch traced here: 582 us
  waiting for transfers between devices  312 us (53%)
  blocking collectives  188 us (32%)
  matrix products  39.2 us (7%)
  local copies, waits for them, and re-layouts  25.9 us (4%)
  between operations  13.3 us (2%)
    all_gather x1, blocking collectives, per_device(): lax.all_gather(gate_table, ('grp', 'dev'), axis=0, tiled=True)  174 us
    unnamed x4, waiting for transfers between devices  172 us
    all_gather x1, waiting for transfers between devices, per_device(): lax.all_gather(attended, 'dev', axis=0, tiled=True)  114 us
    all_gather x1, waiting for transfers between devices, per_device(): lax.all_gather(normed, ('grp', 'dev'), axis=0, tiled=True)  25.7 us
    unnamed x21, local copies, waits for them, and re-layouts  25.6 us
    dot_general x1, matrix products, expert_rows(): return jnp.dot(activated, down_weight, preferred_element_type=jnp.float32)  19.5 us
    all_to_all x1, blocking collectives, per_device(): lax.all_to_all(columns, 'dev', split_axis=0, concat_axis=1, tiled=True)  14.3 us
  transfers between devices with their start and end apart: 3, of which 3 were waited for; matrix products, arithmetic and copies ran while one was open for 0% of the time, Pallas kernels for 0%

commit v1 on v0

v1 whole, which is shorter than its diff:
```python
import math

import jax
import jax.numpy as jnp
from jax import lax
from jax.experimental import pallas as pl
from jax.experimental.pallas import tpu as pltpu
from jax.sharding import Mesh, PartitionSpec as P

D = 7168
HEAD = 256
KALL = 16384
KHALF = KALL // 2
KQ = KHALF // 2
KE = KQ // 2
HID_DEV = 320
COLS = 112
EXPERTS = 8
BF = jnp.bfloat16
F32 = jnp.float32
SIZES = {"g": 2, "z": 4, "x": 4, "y": 2, "c": 2}
ALL = ("g", "z", "x", "y", "c")
SECTION = ("z", "x", "y", "c")


def shift(array, axis, step=1):
    n = SIZES[axis]
    return lax.ppermute(array, axis, [(i, (i + step) % n) for i in range(n)])


def others4(array, axis):
    return [shift(array, axis, 1), shift(array, axis, 2), shift(array, axis, 3)]


def ring_gy(array, step):
    return lax.ppermute(array, ("g", "y"), [(i, (i + step) % 4) for i in range(4)])


def pair_ordered(own, other, mine):
    return jnp.where(
        mine == 0, jnp.stack([own, other]), jnp.stack([other, own])
    )


def attend(queries, new_key, new_value, cache_keys, cache_values, lengths):
    row_count = queries.shape[0]
    head_size = new_key.shape[1]
    head_count = queries.shape[1] // head_size
    context = cache_keys.shape[1]
    queried = queries.reshape(row_count, head_count, head_size)
    scaling = 1.0 / math.sqrt(head_size)
    cached = (
        jnp.einsum("rhd,rpd->rhp", queried, cache_keys, preferred_element_type=F32) * scaling
    )
    itself = jnp.einsum("rhd,rd->rh", queried, new_key, preferred_element_type=F32) * scaling
    position = lax.broadcasted_iota(jnp.int32, (1, 1, context), 2)
    cached = jnp.where(position < lengths[:, None, None], cached, -jnp.inf)
    highest = jnp.maximum(jnp.max(cached, axis=2), itself)
    cached_exp = jnp.exp(cached - highest[:, :, None])
    itself_exp = jnp.exp(itself - highest)
    totals = jnp.sum(cached_exp, axis=2) + itself_exp
    cached_probs = (cached_exp / totals[:, :, None]).astype(BF)
    itself_probs = (itself_exp / totals).astype(BF)
    mixture = jnp.einsum("rhp,rpd->rhd", cached_probs, cache_values, preferred_element_type=F32)
    mixture = (
        mixture + itself_probs.astype(F32)[:, :, None] * new_value.astype(F32)[:, None, :]
    )
    return mixture.astype(BF)


VMEM = pl.BlockSpec(memory_space=pltpu.VMEM)
SMEM = pl.BlockSpec(memory_space=pltpu.SMEM)
HBM = pl.BlockSpec(memory_space=pl.ANY)


def at16(index):
    return pl.multiple_of(index, 16)


def project_kernel(place, a0, a1, a2, a3, b0, b1, b2, b3, w, sent, kept, tail, rows):
    z, x = place[0], place[1]
    for k, a in enumerate((a0, a1, a2, a3)):
        for i in range(4):
            row = at16((z - i + 4) % 4 * 64 + (x - k + 4) % 4 * 16)
            rows[pl.ds(row, 16), :KE] = a[16 * i : 16 * i + 16, :KE]
            tail[pl.ds(row, 16), :128] = a[16 * i : 16 * i + 16, KE:]
    for k, b in enumerate((b0, b1, b2, b3)):
        for i in range(4):
            row = at16((z - k + 4) % 4 * 64 + (x - i + 4) % 4 * 16)
            rows[pl.ds(row, 16), KE:] = b[16 * i : 16 * i + 16, :KE]
            tail[pl.ds(row, 16), 128:] = b[16 * i : 16 * i + 16, KE:]
    product = lax.dot_general(
        w[...], rows[...], (((1,), (1,)), ((), ())), preferred_element_type=F32
    )
    kept[...] = product[: 2 * COLS]
    sent[...] = product[2 * COLS :].astype(BF)


def project(place, firsts, seconds, weights):
    return pl.pallas_call(
        project_kernel,
        out_shape=(
            jax.ShapeDtypeStruct((2 * COLS, 256), BF),
            jax.ShapeDtypeStruct((2 * COLS, 256), F32),
            jax.ShapeDtypeStruct((256, 256), BF),
        ),
        in_specs=[SMEM] + [VMEM] * 9,
        out_specs=(VMEM,) * 3,
        scratch_shapes=[pltpu.VMEM((256, KQ), BF)],
        compiler_params=pltpu.CompilerParams(vmem_limit_bytes=24 << 20),
        name="project",
    )(place, *firsts, *seconds, weights)


def mix_kernel(kept, near, other, gain, tail, dispatched):
    projected = kept[...] + near[...].astype(F32) + other[...]
    back = tail[:, :128].astype(F32).T[:COLS]
    widened = (back + projected).astype(BF).astype(F32)
    carried = (widened * gain[...]).astype(BF)
    position = lax.broadcasted_iota(jnp.int32, (256, 128), 0)
    slot = lax.broadcasted_iota(jnp.int32, (256, 128), 1)
    z, x, y, c = position // 64, position // 16 % 4, position // 8 % 2, position // 4 % 2
    here = ((c * 4 + z) * 4 + x) * 2 + y == slot // 2
    rank = (slot % 2 + 1).astype(F32)
    ranks = tail[:, 128:].astype(F32)
    for e in range(EXPERTS):
        pick = jnp.where(here & (ranks[:, e : e + 1] == rank), 1.0, 0.0).astype(BF)
        block = jnp.dot(carried, pick, preferred_element_type=F32).astype(BF)
        for device in range(8):
            dispatched[8 * e + device] = block


def mix(kept, near, other, gain, tail):
    return pl.pallas_call(
        mix_kernel,
        out_shape=jax.ShapeDtypeStruct((64, COLS, 128), BF),
        in_specs=[VMEM] * 5,
        out_specs=VMEM,
        compiler_params=pltpu.CompilerParams(vmem_limit_bytes=12 << 20),
        name="mix",
    )(kept, near, other, gain, tail)


def square_kernel(arrived, inverse, out):
    for g in range(2):
        total = jnp.zeros((8, 128), F32)
        for i in range(32):
            value = arrived[32 * g + i].astype(F32) * inverse[i]
            total = total + jnp.sum((value * value).reshape(14, 8, 128), axis=0)
        out[:, 128 * g : 128 * g + 128] = total


def squares_of(arrived, inverse):
    return pl.pallas_call(
        square_kernel,
        out_shape=jax.ShapeDtypeStruct((8, 256), F32),
        in_specs=[VMEM] * 2,
        out_specs=VMEM,
        compiler_params=pltpu.CompilerParams(vmem_limit_bytes=12 << 20),
        name="squares",
    )(arrived, inverse)


DEPTH = 1024


def expert_kernel(
    place, own, other, own_squares, other_squares, gate, up, sent, kept, resid,
    columns, gates, ups, act, sems,
):
    x, y, c = place[1], place[2], place[3]
    copies = []
    for k in range(D // DEPTH):
        lanes = pl.ds(k * DEPTH, DEPTH)
        copies.append((
            pltpu.make_async_copy(gate.at[:, lanes], gates.at[:, lanes], sems.at[2 * k]),
            pltpu.make_async_copy(up.at[:, lanes], ups.at[:, lanes], sems.at[2 * k + 1]),
        ))
    for pair in copies:
        for copy in pair:
            copy.start()

    for ref, of_c in ((own, c), (other, 1 - c)):
        for i in range(32):
            row = at16((2 * i + of_c) * COLS)
            columns[pl.ds(row, COLS), :128] = ref[i]
            columns[pl.ds(row, COLS), 128:] = ref[32 + i]
    squares = own_squares[...] + other_squares[...]
    scale = lax.rsqrt(jnp.sum(squares, axis=0, keepdims=True) / D + 1e-05)

    gated = jnp.zeros((HID_DEV, 256), F32)
    upward = jnp.zeros((HID_DEV, 256), F32)
    for k, pair in enumerate(copies):
        for copy in pair:
            copy.wait()
        lanes = slice(k * DEPTH, (k + 1) * DEPTH)
        part = columns[lanes, :]
        gated = gated + jnp.dot(gates[:, lanes], part, preferred_element_type=F32)
        upward = upward + jnp.dot(ups[:, lanes], part, preferred_element_type=F32)
    gated = gated * scale
    upward = upward * scale
    activated = gated / (1.0 + jnp.exp(-gated)) * upward
    act[...] = activated.T.astype(BF)
    for g in range(2):
        sent[g * 64 : g * 64 + 64, :] = act[pl.ds(at16(g * 128 + (1 - c) * 64), 64), :]
        kept[g * 64 : g * 64 + 64, :] = act[pl.ds(at16(g * 128 + c * 64), 64), :]
    row = lax.broadcasted_iota(jnp.int32, (128, 256), 0)
    lane = lax.broadcasted_iota(jnp.int32, (128, 256), 1)
    mine = (row // 2 % 8 == x * 2 + y) & (lane == row // 64 * 128 + c * 64 + row % 64)
    resid[...] = lax.dot_general(
        jnp.where(mine, 1.0, 0.0).astype(BF), columns[...],
        (((1,), (1,)), ((), ())), preferred_element_type=F32,
    ).astype(BF)


def expert(place, own, other, own_squares, other_squares, gate, up):
    return pl.pallas_call(
        expert_kernel,
        out_shape=(
            jax.ShapeDtypeStruct((128, HID_DEV), BF),
            jax.ShapeDtypeStruct((128, HID_DEV), BF),
            jax.ShapeDtypeStruct((128, D), BF),
        ),
        in_specs=[SMEM] + [VMEM] * 4 + [HBM] * 2,
        out_specs=(VMEM,) * 3,
        scratch_shapes=[
            pltpu.VMEM((D, 256), BF),
            pltpu.VMEM((HID_DEV, D), BF),
            pltpu.VMEM((HID_DEV, D), BF),
            pltpu.VMEM((256, HID_DEV), BF),
            pltpu.SemaphoreType.DMA((2 * (D // DEPTH),)),
        ],
        compiler_params=pltpu.CompilerParams(vmem_limit_bytes=32 << 20),
        name="expert",
    )(place, own, other, own_squares, other_squares, gate, up)


def lower_kernel(own, other, down, other_down, resid, inverse, out):
    width = D // 4
    for k in range(4):
        lanes = slice(k * width, (k + 1) * width)
        part = jnp.dot(own[...], down[:, lanes], preferred_element_type=F32)
        part = part + jnp.dot(other[...], other_down[:, lanes], preferred_element_type=F32)
        out[:, lanes] = (part + resid[:, lanes].astype(F32) * inverse[:, lanes]).astype(BF)


def lower(own, other, down, other_down, resid, inverse):
    return pl.pallas_call(
        lower_kernel,
        out_shape=jax.ShapeDtypeStruct((128, D), BF),
        in_specs=[VMEM] * 6,
        out_specs=VMEM,
        compiler_params=pltpu.CompilerParams(vmem_limit_bytes=24 << 20),
        name="lower",
    )(own, other, down, other_down, resid, inverse)


def per_device(
    hidden,
    queries,
    new_key,
    new_value,
    cache_keys,
    cache_values,
    lengths,
    out_weight,
    ffn_gain,
    gate_weight,
    up_weight,
    down_weight,
    routes,
    route_gates,
):
    z, x, y, c = (lax.axis_index(a) for a in SECTION)
    chunk = ((z * 4 + x) * 2 + y) * 2 + c
    place = jnp.stack([z, x, y, c]).astype(jnp.int32)

    turned = out_weight.T

    def quarter(of_c, of_y):
        return lax.dynamic_slice_in_dim(turned, of_c * KHALF + of_y * KQ, KQ, 1)

    away = (quarter(0, 1 - y), quarter(1, 1 - y))
    queries, away = lax.optimization_barrier((queries, away))
    far_low = ring_gy(away[0], 1)
    far_high = ring_gy(away[1], -1)
    near = quarter(c, y)
    near_other = shift(quarter(1 - c, y), "c")
    other_down = shift(down_weight, "c")

    expert_ids = lax.broadcasted_iota(jnp.int32, (1, 1, EXPERTS), 2)
    named = routes[:, :, None] == expert_ids
    names = jnp.any(named, axis=1).astype(jnp.int32)
    before = jnp.concatenate(
        [jnp.zeros((1, EXPERTS), jnp.int32), jnp.cumsum(names, axis=0)[:-1]], axis=0
    )
    slot_table = names * (before + 1)
    gate_table = jnp.sum(jnp.where(named, route_gates[:, :, None], 0), axis=1).astype(F32)
    shares = gate_table / jnp.sum(route_gates, axis=1, keepdims=True).astype(F32)
    slot_lanes = jnp.pad(slot_table.astype(BF), ((0, 0), (0, 128 - EXPERTS)))

    hidden_lanes = jnp.pad(
        hidden.reshape(4, 4, 4, 2, 2, COLS).transpose(4, 3, 0, 1, 2, 5),
        ((0, 0),) * 5 + ((0, 128 - COLS),),
    ).reshape(2, 2, 4, 4 * 4 * 128)

    def pick(array, index, dim):
        return lax.dynamic_index_in_dim(array, index, dim, keepdims=False)

    attended = attend(queries, new_key, new_value, cache_keys, cache_values, lengths)
    halves = attended.reshape(4, 2, KHALF)

    def for_core(of_c):
        of_hidden = pick(hidden_lanes, of_c, 0)
        return jnp.concatenate(
            [pick(halves, of_c, 1), slot_lanes, of_hidden[0], of_hidden[1]], axis=1
        )

    block = pair_ordered(for_core(c), shift(for_core(1 - c), "c"), c)
    block = block.reshape(8, KHALF + 128 + 4096)

    def for_y(of_y):
        return jnp.concatenate(
            [
                lax.dynamic_slice_in_dim(block, of_y * KQ, KQ, 1),
                block[:, KHALF : KHALF + 128],
                lax.dynamic_slice_in_dim(block, KHALF + 128 + of_y * 2048, 2048, 1),
            ],
            axis=1,
        )

    block = pair_ordered(for_y(y), shift(for_y(1 - y), "y"), y).reshape(16, KQ + 128 + 2048)
    first, second = block[:, :KE], block[:, KE : KQ + 128]
    tails = block[:, KQ + 128 :]

    def with_tail(of_z):
        own = lax.dynamic_slice_in_dim(tails, of_z % 4 * 512, 512, 1)
        return jnp.concatenate([first, own], axis=1)

    firsts = [with_tail(z)] + [shift(with_tail(z + k), "z", k) for k in (1, 2, 3)]
    firsts, seconds, far_low, far_high = lax.optimization_barrier(
        (firsts, [second] + others4(second, "x"), far_low, far_high)
    )
    far = jnp.where(c == 0, far_low, far_high)
    far_other = shift(jnp.where(c == 0, far_high, far_low), "c")
    weights = jnp.concatenate([near, near_other, far, far_other], axis=0)
    first = jnp.concatenate(firsts, axis=0)
    second = jnp.concatenate(seconds, axis=0)
    tails = first[:, KE:]
    first = first[:, :KE]

    def with_column(of_x):
        own = lax.dynamic_slice_in_dim(tails, of_x % 4 * 128, 128, 1)
        return jnp.concatenate([first, own], axis=1)

    firsts = [with_column(x)] + [shift(with_column(x + k), "x", k) for k in (1, 2, 3)]
    seconds = [second] + others4(second, "z")
    sent, kept, tail = project(place, firsts, seconds, weights)
    near_sum = shift(sent, "y")
    gain = lax.dynamic_slice_in_dim(ffn_gain, chunk * COLS, COLS, 0).reshape(COLS, 1)
    crossing = kept[COLS:] + near_sum[COLS:].astype(F32)
    dispatched = mix(kept[:COLS], near_sum[:COLS], shift(crossing, "c"), gain, tail)
    arrived = lax.all_to_all(dispatched, ("g", "z", "x", "y"), 0, 0, tiled=True)
    other = shift(arrived, "c")
    inverse = 1.0 / ffn_gain
    own_inverse = pick(inverse.reshape(32, 2, COLS), c, 1).reshape(32, COLS, 1)
    own_squares = squares_of(arrived, own_inverse)
    sent, kept, resid = expert(
        place, arrived, other, own_squares, shift(own_squares, "c"),
        gate_weight.T, up_weight.T,
    )
    summed = lower(kept, shift(sent, "c"), down_weight, other_down, resid, inverse.reshape(1, D))
    returned = lax.all_to_all(
        summed.reshape(64, 2, D), ("g", "z", "x", "y"), 0, 0, tiled=True
    )
    returned = jnp.sum(returned.reshape(8, 8, 2, D).astype(F32), axis=1)
    ranks = lax.broadcasted_iota(jnp.int32, (1, 1, 2), 2) + 1
    parts = jnp.where(slot_table[:, :, None] == ranks, shares[:, :, None], 0.0)
    return jnp.sum(parts.reshape(4, 16, 1) * returned.reshape(1, 16, D), axis=1).astype(BF)


def solution(mesh):
    fine = Mesh(mesh.devices.reshape(*SIZES.values()), ALL)
    rows = P(ALL, None)
    return jax.shard_map(
        per_device,
        mesh=fine,
        in_specs=(
            rows,
            rows,
            rows,
            rows,
            P(ALL, None, None),
            P(ALL, None, None),
            P(ALL),
            P(None, SECTION),
            P(),
            P(None, ALL),
            P(None, ALL),
            rows,
            rows,
            rows,
        ),
        out_specs=rows,
        check_vma=False,
    )
```

time: 584 us -> 174 us (0.30)
  waiting for transfers between devices: 312 us -> 57.8 us
  blocking collectives: 188 us -> 34.4 us
  starting transfers between devices: 0.09 us -> 39.1 us
  matrix products: 39.2 us -> 2.47 us
  Pallas kernels: 0 us -> 14.8 us
  between operations: 13.3 us -> 0.51 us
  local copies, waits for them, and re-layouts: 25.9 us -> 18 us
    all_gather x1 -> x0, blocking collectives: 174 us -> none  [per_device(): lax.all_gather(gate_table, ('grp', 'dev'), axis=0, tiled=True)]
    unnamed x4 -> x0, waiting for transfers between devices: 172 us -> none
    all_gather x2 -> x0, waiting for transfers between devices: 140 us -> none  [the longest x1 114 us: per_device(): lax.all_gather(attended, 'dev', axis=0, tiled=True)]
    dot_general x5 -> x2, matrix products: 38.4 us -> 1.62 us  [the longest x1 1.49 us: attend(): jnp.einsum('rhd,rpd->rhp', queried, cache_keys, preferred_element_type=F32)]
    ppermute x0 -> x24, starting transfers between devices: none -> 32.7 us  [the longest x22 29.5 us: shift(): return lax.ppermute(array, axis, [(i, (i + step) % n) for i in range(n)])]
    ppermute x0 -> x24, waiting for transfers between devices: none -> 31.9 us  [the longest x22 27.9 us: shift(): return lax.ppermute(array, axis, [(i, (i + step) % n) for i in range(n)])]
    all_to_all x0 -> x1, waiting for transfers between devices: none -> 25.9 us  [per_device(): lax.all_to_all(summed.reshape(64, 2, D), ('g', 'z', 'x', 'y'), 0, 0, tile...]
    all_to_all x1, blocking collectives: 14.3 us -> 34.4 us  [per_device(): arrived = lax.all_to_all(dispatched, ('g', 'z', 'x', 'y'), 0, 0, tiled=True)]
  transfers between devices with their start and end apart: 3 -> 25, of which waited for: 3 -> 15; matrix products, arithmetic and copies ran while one was open for 0% -> 3% of each run, Pallas kernels for 0% -> 6%
where the time goes in v1:
time: 174 us; the launch traced here: 173 us
  waiting for transfers between devices  57.8 us (33%)
  starting transfers between devices  39.1 us (22%)
  blocking collectives  34.4 us (20%)
  local copies, waits for them, and re-layouts  18 us (10%)
  Pallas kernels  14.8 us (9%)
  other arithmetic  6.26 us (4%)
  matrix products  2.47 us (1%)
    all_to_all x1, blocking collectives, per_device(): arrived = lax.all_to_all(dispatched, ('g', 'z', 'x', 'y'), 0, 0, tiled=True)  34.4 us
    ppermute x22, starting transfers between devices, shift(): return lax.ppermute(array, axis, [(i, (i + step) % n) for i in range(n)])  29.5 us
    ppermute x22, waiting for transfers between devices, shift(): return lax.ppermute(array, axis, [(i, (i + step) % n) for i in range(n)])  27.9 us
    all_to_all x1, waiting for transfers between devices, per_device(): lax.all_to_all(summed.reshape(64, 2, D), ('g', 'z', 'x', 'y'), 0, 0, tile...  25.9 us
    unnamed x38, local copies, waits for them, and re-layouts  8.93 us
    pallas_call x1, Pallas kernels, expert(): pl.pallas_call(expert_kernel, out_shape=(jax.ShapeDtypeStruct((128, HID_D...  7 us
    all_to_all x1, starting transfers between devices, per_device(): lax.all_to_all(summed.reshape(64, 2, D), ('g', 'z', 'x', 'y'), 0, 0, tile...  6.41 us
    pallas_call x1, Pallas kernels, lower(): pl.pallas_call(lower_kernel, out_shape=jax.ShapeDtypeStruct((128, D), BF)...  4.42 us
  transfers between devices with their start and end apart: 25, of which 15 were waited for; matrix products, arithmetic and copies ran while one was open for 3% of the time, Pallas kernels for 6%

profile of v1, /device:TPU:0, one launch (start us, length us, event | category | flops | bytes accessed | tf_op | source)
XLA Modules:
  0.0 173.3 jit_solution(8361256312759064416)
XLA Ops:
  0.0 3.5 %dynamic-slice_bitcast_fusion.1 = (bf16[112,4096]{1,0:T(8,128)(2,1)S(1)}, bf16[112,4096]{1,0:T(8,128)(2,1)S(1)}, bf16[112,4096]{1,0:T(8,128)(2,1)}, bf16[112,4096]{1,0:T(8,128)(2,1)S(1)}) fusion(bf16[16384,112]{0,1:T(8,128)(2,1)} %param.21, s32[]{:T(128)S(6)} %select_n.183, s32[]{:T(128)S(6)} %select_n.155, s32[]{:T(128)S(6)} %select_n.154, s32[]{:T(128)S(6)} %select_n.184), kind=kLoop, calls=%fused_computation.12 | loop fusion | bytes 7340048 | tf_op jit(solution)/shard_map/dynamic_slice | solution.py:281
  9.7 1.7 %collective-permute-start.1 = (bf16[8,6272]{1,0:T(8,128)(2,1)S(1)}, bf16[8,6272]{1,0:T(8,128)(2,1)S(1)}, u32[]{:S(2)}, u32[]{:S(2)}) collective-permute-start(bf16[8,6272]{1,0:T(8,128)(2,1)S(1)} %get-tuple-element.84), channel_id=1, source_target_pairs={{0,2},{2,0},{1,3},{3,1},{4,6},{6,4},{5,7},{7,5},{8,10},{10,8},{9,1... | collective-permute-start | bytes 301064 | tf_op jit(solution)/shard_map/ppermute | solution.py:28
  11.8 2.9 %collective-permute-start.9 = (bf16[112,4096]{1,0:T(8,128)(2,1)S(1)}, bf16[112,4096]{1,0:T(8,128)(2,1)}, u32[]{:S(2)}, u32[]{:S(2)}) collective-permute-start(bf16[112,4096]{1,0:T(8,128)(2,1)S(1)} %get-tuple-element.26), channel_id=1, source_target_pairs={{0,66},{2,0},{64,2},{66,64},{1,67},{3,1},{65,3},{67,65},{4,70},{6,... | collective-permute-start | bytes 2752520 | tf_op jit(solution)/shard_map/ppermute | solution.py:36
  14.8 1.6 collective-permute-start.5
  16.4 2.7 %collective-permute-start.6 = (bf16[16,2176]{1,0:T(8,128)(2,1)S(1)}, bf16[16,2176]{1,0:T(8,128)(2,1)S(1)}, u32[]{:S(2)}, u32[]{:S(2)}) collective-permute-start(bf16[16,2176]{1,0:T(8,128)(2,1)S(1)} %slice.68), channel_id=1, source_target_pairs={{0,8},{4,12},{8,0},{12,4},{1,9},{5,13},{9,1},{13,5},{2,10},{6,14},... | collective-permute-start | bytes 208904 | tf_op jit(solution)/shard_map/ppermute | solution.py:28
  21.1 2.0 %collective-permute-start.2 = (bf16[16,2560]{1,0:T(8,128)(2,1)S(1)}, bf16[16,2560]{1,0:T(8,128)(2,1)S(1)}, u32[]{:S(2)}, u32[]{:S(2)}) collective-permute-start(bf16[16,2560]{1,0:T(8,128)(2,1)S(1)} %get-tuple-element.70), channel_id=1, source_target_pairs={{0,16},{16,32},{32,48},{48,0},{1,17},{17,33},{33,49},{49,1},{2,18}... | collective-permute-start | bytes 245768 | tf_op jit(solution)/shard_map/ppermute | solution.py:28
  23.1 3.6 %collective-permute-start.3 = (bf16[16,2560]{1,0:T(8,128)(2,1)S(1)}, bf16[16,2560]{1,0:T(8,128)(2,1)S(1)}, u32[]{:S(2)}, u32[]{:S(2)}) collective-permute-start(bf16[16,2560]{1,0:T(8,128)(2,1)S(1)} %get-tuple-element.71), channel_id=1, source_target_pairs={{0,32},{16,48},{32,0},{48,16},{1,33},{17,49},{33,1},{49,17},{2,34}... | collective-permute-start | bytes 245768 | tf_op jit(solution)/shard_map/ppermute | solution.py:28
  27.9 2.1 %collective-permute-done.3 = bf16[16,2560]{1,0:T(8,128)(2,1)S(1)} collective-permute-done((bf16[16,2560]{1,0:T(8,128)(2,1)S(1)}, bf16[16,2560]{1,0:T(8,128)(2,1)S(1)}, u32[]{:S(2)}, u32[]{:S(2)}) %collective-permute-start.3) | collective-permute-done | bytes 81952 | tf_op jit(solution)/shard_map/ppermute | solution.py:28
  31.2 4.0 %collective-permute-done.8 = bf16[112,4096]{1,0:T(8,128)(2,1)} collective-permute-done((bf16[112,4096]{1,0:T(8,128)(2,1)}, bf16[112,4096]{1,0:T(8,128)(2,1)}, u32[]{:S(2)}, u32[]{:S(2)}) %collective-permute-start.8) | collective-permute-done | bytes 917536 | tf_op jit(solution)/shard_map/ppermute | solution.py:36
  35.2 2.0 %collective-permute-start.13 = (bf16[64,2176]{1,0:T(8,128)(2,1)S(1)}, bf16[64,2176]{1,0:T(8,128)(2,1)S(1)}, u32[]{:S(2)}, u32[]{:S(2)}) collective-permute-start(bf16[64,2176]{1,0:T(8,128)(2,1)S(1)} %constant_dynamic-update-slice_fusion.4.b0), channel_id=1, source_target_pairs={{0,16},{16,32},{32,48},{48,0},{1,17},{17,33},{33,49},{49,1},{2,18}... | collective-permute-start | bytes 835592 | tf_op jit(solution)/shard_map/ppermute | solution.py:28
  37.2 3.6 %collective-permute-start.14 = (bf16[64,2176]{1,0:T(8,128)(2,1)S(1)}, bf16[64,2176]{1,0:T(8,128)(2,1)S(1)}, u32[]{:S(2)}, u32[]{:S(2)}) collective-permute-start(bf16[64,2176]{1,0:T(8,128)(2,1)S(1)} %constant_dynamic-update-slice_fusion.4.b0), channel_id=1, source_target_pairs={{0,32},{16,48},{32,0},{48,16},{1,33},{17,49},{33,1},{49,17},{2,34}... | collective-permute-start | bytes 835592 | tf_op jit(solution)/shard_map/ppermute | solution.py:28
  40.8 1.6 broadcast_select_fusion.1
  43.8 2.2 %collective-permute-done.13.b1 = bf16[64,2176]{1,0:T(8,128)(2,1)S(1)} collective-permute-done((bf16[64,2176]{1,0:T(8,128)(2,1)S(1)}, bf16[64,2176]{1,0:T(8,128)(2,1)S(1)}, u32[]{:S(2)}, u32[]{:S(2)}) %collective-permute-start.13) | collective-permute-done | bytes 278560 | tf_op jit(solution)/shard_map/ppermute | solution.py:28
  47.5 4.8 %collective-permute-done.14.b2 = bf16[64,2176]{1,0:T(8,128)(2,1)S(1)} collective-permute-done((bf16[64,2176]{1,0:T(8,128)(2,1)S(1)}, bf16[64,2176]{1,0:T(8,128)(2,1)S(1)}, u32[]{:S(2)}, u32[]{:S(2)}) %collective-permute-start.14) | collective-permute-done | bytes 278560 | tf_op jit(solution)/shard_map/ppermute | solution.py:28
  52.3 3.0 %collective-permute-start.11 = (bf16[64,2176]{1,0:T(8,128)(2,1)S(1)}, bf16[64,2176]{1,0:T(8,128)(2,1)S(1)}, u32[]{:S(2)}, u32[]{:S(2)}) collective-permute-start(bf16[64,2176]{1,0:T(8,128)(2,1)S(1)} %get-tuple-element.53), channel_id=1, source_target_pairs={{0,8},{4,12},{8,0},{12,4},{1,9},{5,13},{9,1},{13,5},{2,10},{6,14},... | collective-permute-start | bytes 835592 | tf_op jit(solution)/shard_map/ppermute | solution.py:28
  56.9 3.8 %collective-permute-done.11.a2 = bf16[64,2176]{1,0:T(8,128)(2,1)S(1)} collective-permute-done((bf16[64,2176]{1,0:T(8,128)(2,1)S(1)}, bf16[64,2176]{1,0:T(8,128)(2,1)S(1)}, u32[]{:S(2)}, u32[]{:S(2)}) %collective-permute-start.11) | collective-permute-done | bytes 278560 | tf_op jit(solution)/shard_map/ppermute | solution.py:28
  60.7 5.8 %collective-permute-done.12.a3 = bf16[64,2176]{1,0:T(8,128)(2,1)S(1)} collective-permute-done((bf16[64,2176]{1,0:T(8,128)(2,1)S(1)}, bf16[64,2176]{1,0:T(8,128)(2,1)S(1)}, u32[]{:S(2)}, u32[]{:S(2)}) %collective-permute-start.12) | collective-permute-done | bytes 278560 | tf_op jit(solution)/shard_map/ppermute | solution.py:28
  66.5 1.9 %project.1 = (bf16[224,256]{1,0:T(8,128)(2,1)S(1)}, f32[224,256]{1,0:T(8,128)S(1)}, bf16[256,256]{1,0:T(8,128)(2,1)S(1)}) custom-call(s32[4]{0:T(128)S(1)} %pad_add_fusion.place, bf16[64,2176]{1,0:T(8,128)(2,1)S(1)} %get-tuple-element.54.a0, bf16[64,2176]{1,0:T(8,128)(2,1)S(1)} %collective-permute-done.10.a1, ...), custom_call_target="tpu_custom_call" | custom-call | tf_op jit(solution)/shard_map/project/pallas_call | solution.py:100
  68.4 1.8 %collective-permute-start.18 = (bf16[224,256]{1,0:T(8,128)(2,1)S(1)}, bf16[224,256]{1,0:T(8,128)(2,1)S(1)}, u32[]{:S(2)}, u32[]{:S(2)}) collective-permute-start(bf16[224,256]{1,0:T(8,128)(2,1)S(1)} %get-tuple-element.38), channel_id=1, source_target_pairs={{0,2},{2,0},{1,3},{3,1},{4,6},{6,4},{5,7},{7,5},{8,10},{10,8},{9,1... | collective-permute-start | bytes 344072 | tf_op jit(solution)/shard_map/ppermute | solution.py:28
  70.2 3.3 %collective-permute-done.18 = bf16[224,256]{1,0:T(8,128)(2,1)S(1)} collective-permute-done((bf16[224,256]{1,0:T(8,128)(2,1)S(1)}, bf16[224,256]{1,0:T(8,128)(2,1)S(1)}, u32[]{:S(2)}, u32[]{:S(2)}) %collective-permute-start.18) | collective-permute-done | bytes 114720 | tf_op jit(solution)/shard_map/ppermute | solution.py:28
  75.4 34.4 %all_to_all.10.arrived.own = bf16[64,112,128]{2,1,0:T(8,128)(2,1)S(1)} all-to-all(bf16[64,112,128]{2,1,0:T(8,128)(2,1)S(1)} %mix.1), channel_id=1, replica_groups=mesh['g'=2,'z'=4,'x'=4,'y'=2,'c'=2] {'g','z','x','y'}, dimensions={0} | all-to-all | bytes 3670016 | tf_op jit(solution)/shard_map/all_to_all | solution.py:363
  109.9 1.9 %copy.35.inverse = f32[32,112,1]{2,1,0:T(8,128)} copy(f32[32,112,1]{1,0,2:T(8,128)S(1)} %bitcast.69) | data formatting | bytes 28672 | tf_op jit(solution)/shard_map/reshape | solution.py:366
  111.8 1.5 copy-done.2
  115.8 2.3 %copy-done.3 = bf16[7168,320]{0,1:T(8,128)(2,1)S(1)} copy-done((bf16[7168,320]{0,1:T(8,128)(2,1)S(1)}, bf16[7168,320]{0,1:T(8,128)(2,1)}, u32[]{:S(2)}) %copy-start.3) | copy-done | bytes 4587544
  118.1 2.3 %copy-done.4 = bf16[7168,320]{0,1:T(8,128)(2,1)S(1)} copy-done((bf16[7168,320]{0,1:T(8,128)(2,1)S(1)}, bf16[7168,320]{0,1:T(8,128)(2,1)}, u32[]{:S(2)}) %copy-start.4) | copy-done | bytes 4587544
  120.4 7.0 %expert.1 = (bf16[128,320]{1,0:T(8,128)(2,1)S(1)}, bf16[128,320]{1,0:T(8,128)(2,1)S(1)}, bf16[128,7168]{1,0:T(8,128)(2,1)S(1)}) custom-call(s32[4]{0:T(128)S(1)} %pad_add_fusion.place, bf16[64,112,128]{2,1,0:T(8,128)(2,1)S(1)} %all_to_all.10.arrived.own, bf16[64,112,128]{2,1,0:T(8,128)(2,1)} %collective-permute-done.20.other, ...), custom_call_target="tpu_custom_call" | custom-call | tf_op jit(solution)/shard_map/expert/pallas_call | solution.py:217
  128.8 2.3 %copy-done.5 = bf16[320,7168]{1,0:T(8,128)(2,1)S(1)} copy-done((bf16[320,7168]{1,0:T(8,128)(2,1)S(1)}, bf16[320,7168]{1,0:T(8,128)(2,1)}, u32[]{:S(2)}) %copy-start.5) | copy-done | bytes 4587544
  131.1 4.4 %lower.1 = bf16[128,7168]{1,0:T(8,128)(2,1)S(1)} custom-call(bf16[128,320]{1,0:T(8,128)(2,1)S(1)} %get-tuple-element.40.own, bf16[128,320]{1,0:T(8,128)(2,1)S(1)} %collective-permute-done.22.other, bf16[320,7168]{1,0:T(8,128)(2,1)S(1)} %copy-done.5, bf16[320,7168]{1,0:T(8,128)(2,1)} %collective-permute-done.23.other_down, ...), custom_call_target="tpu_custom_call" | custom-call | tf_op jit(solution)/shard_map/lower/pallas_call | solution.py:248
  135.5 1.7 reshape.136
  137.2 6.4 %all-to-all-start.1 = ((bf16[64,2,7168]{2,1,0:T(2,128)(2,1)}), bf16[64,2,7168]{2,1,0:T(2,128)(2,1)S(1)}, u32[]{:S(2)}, u32[]{:S(2)}) async-start(bf16[64,2,7168]{2,1,0:T(2,128)(2,1)} %reshape.136), calls=%async_computation.1 | async-start | bytes 3670016 | tf_op jit(solution)/shard_map/all_to_all | solution.py:373
  144.4 25.9 %all-to-all-done.1 = bf16[64,2,7168]{2,1,0:T(2,128)(2,1)S(1)} async-done(((bf16[64,2,7168]{2,1,0:T(2,128)(2,1)}), bf16[64,2,7168]{2,1,0:T(2,128)(2,1)S(1)}, u32[]{:S(2)}, u32[]{:S(2)}) %all-to-all-start.1) | async-done | bytes 1835040 | tf_op jit(solution)/shard_map/all_to_all | solution.py:373
  170.3 1.6 convert_reduce_fusion
  (129 shorter events, 23.2 us)
Async XLA Ops:
  0.0 3.6 %copy-start = (bf16[4,256]{1,0:T(4,128)(2,1)S(1)}, bf16[4,256]{1,0:T(4,128)(2,1)}, u32[]{:S(2)}) copy-start(bf16[4,256]{1,0:T(4,128)(2,1)} %param.16) | copy-start | bytes 6148
  0.0 3.6 %copy-start.13 = (s32[4]{0:T(128)S(1)}, s32[4]{0:T(128)}, u32[]{:S(2)}) copy-start(s32[4]{0:T(128)} %param.20) | copy-start | bytes 52
  0.0 3.7 %copy-start.7 = (bf16[4,16384]{1,0:T(4,128)(2,1)S(1)}, bf16[4,16384]{1,0:T(4,128)(2,1)}, u32[]{:S(2)}) copy-start(bf16[4,16384]{1,0:T(4,128)(2,1)} %param.15) | copy-start | bytes 393220
  0.0 3.8 %copy-start.6 = (bf16[4,2048,256]{2,1,0:T(8,128)(2,1)S(1)}, bf16[4,2048,256]{2,1,0:T(8,128)(2,1)}, u32[]{:S(2)}) copy-start(bf16[4,2048,256]{2,1,0:T(8,128)(2,1)} %param.18) | copy-start | bytes 12582916
  8.0 1.4 collective-permute-start
  9.7 5.0 %collective-permute-start.1 = (bf16[8,6272]{1,0:T(8,128)(2,1)S(1)}, bf16[8,6272]{1,0:T(8,128)(2,1)S(1)}, u32[]{:S(2)}, u32[]{:S(2)}) collective-permute-start(bf16[8,6272]{1,0:T(8,128)(2,1)S(1)} %get-tuple-element.84), channel_id=1, source_target_pairs={{0,2},{2,0},{1,3},{3,1},{4,6},{6,4},{5,7},{7,5},{8,10},{10,8},{9,1... | collective-permute-start | bytes 301064 | tf_op jit(solution)/shard_map/ppermute | solution.py:28
  11.5 23.7 %collective-permute-start.8 = (bf16[112,4096]{1,0:T(8,128)(2,1)}, bf16[112,4096]{1,0:T(8,128)(2,1)}, u32[]{:S(2)}, u32[]{:S(2)}) collective-permute-start(bf16[112,4096]{1,0:T(8,128)(2,1)} %get-tuple-element.25), channel_id=1, source_target_pairs={{0,2},{2,64},{64,66},{66,0},{1,3},{3,65},{65,67},{67,1},{4,6},{6,6... | collective-permute-start | bytes 2752520 | tf_op jit(solution)/shard_map/ppermute | solution.py:36
  11.8 23.3 %collective-permute-start.9 = (bf16[112,4096]{1,0:T(8,128)(2,1)S(1)}, bf16[112,4096]{1,0:T(8,128)(2,1)}, u32[]{:S(2)}, u32[]{:S(2)}) collective-permute-start(bf16[112,4096]{1,0:T(8,128)(2,1)S(1)} %get-tuple-element.26), channel_id=1, source_target_pairs={{0,66},{2,0},{64,2},{66,64},{1,67},{3,1},{65,3},{67,65},{4,70},{6,... | collective-permute-start | bytes 2752520 | tf_op jit(solution)/shard_map/ppermute | solution.py:36
  14.8 6.3 %collective-permute-start.5 = (bf16[16,2176]{1,0:T(8,128)(2,1)S(1)}, bf16[16,2176]{1,0:T(8,128)(2,1)S(1)}, u32[]{:S(2)}, u32[]{:S(2)}) collective-permute-start(bf16[16,2176]{1,0:T(8,128)(2,1)S(1)} %slice.68), channel_id=1, source_target_pairs={{0,4},{4,8},{8,12},{12,0},{1,5},{5,9},{9,13},{13,1},{2,6},{6,10},{... | collective-permute-start | bytes 208904 | tf_op jit(solution)/shard_map/ppermute | solution.py:28
  16.4 6.7 %collective-permute-start.6 = (bf16[16,2176]{1,0:T(8,128)(2,1)S(1)}, bf16[16,2176]{1,0:T(8,128)(2,1)S(1)}, u32[]{:S(2)}, u32[]{:S(2)}) collective-permute-start(bf16[16,2176]{1,0:T(8,128)(2,1)S(1)} %slice.68), channel_id=1, source_target_pairs={{0,8},{4,12},{8,0},{12,4},{1,9},{5,13},{9,1},{13,5},{2,10},{6,14},... | collective-permute-start | bytes 208904 | tf_op jit(solution)/shard_map/ppermute | solution.py:28
  19.2 7.6 %collective-permute-start.7 = (bf16[16,2176]{1,0:T(8,128)(2,1)S(1)}, bf16[16,2176]{1,0:T(8,128)(2,1)S(1)}, u32[]{:S(2)}, u32[]{:S(2)}) collective-permute-start(bf16[16,2176]{1,0:T(8,128)(2,1)S(1)} %slice.68), channel_id=1, source_target_pairs={{0,12},{4,0},{8,4},{12,8},{1,13},{5,1},{9,5},{13,9},{2,14},{6,2},{... | collective-permute-start | bytes 208904 | tf_op jit(solution)/shard_map/ppermute | solution.py:28
  21.1 6.8 %collective-permute-start.2 = (bf16[16,2560]{1,0:T(8,128)(2,1)S(1)}, bf16[16,2560]{1,0:T(8,128)(2,1)S(1)}, u32[]{:S(2)}, u32[]{:S(2)}) collective-permute-start(bf16[16,2560]{1,0:T(8,128)(2,1)S(1)} %get-tuple-element.70), channel_id=1, source_target_pairs={{0,16},{16,32},{32,48},{48,0},{1,17},{17,33},{33,49},{49,1},{2,18}... | collective-permute-start | bytes 245768 | tf_op jit(solution)/shard_map/ppermute | solution.py:28
  23.1 6.9 %collective-permute-start.3 = (bf16[16,2560]{1,0:T(8,128)(2,1)S(1)}, bf16[16,2560]{1,0:T(8,128)(2,1)S(1)}, u32[]{:S(2)}, u32[]{:S(2)}) collective-permute-start(bf16[16,2560]{1,0:T(8,128)(2,1)S(1)} %get-tuple-element.71), channel_id=1, source_target_pairs={{0,32},{16,48},{32,0},{48,16},{1,33},{17,49},{33,1},{49,17},{2,34}... | collective-permute-start | bytes 245768 | tf_op jit(solution)/shard_map/ppermute | solution.py:28
  26.7 4.4 %collective-permute-start.4 = (bf16[16,2560]{1,0:T(8,128)(2,1)S(1)}, bf16[16,2560]{1,0:T(8,128)(2,1)S(1)}, u32[]{:S(2)}, u32[]{:S(2)}) collective-permute-start(bf16[16,2560]{1,0:T(8,128)(2,1)S(1)} %get-tuple-element.69), channel_id=1, source_target_pairs={{0,48},{16,0},{32,16},{48,32},{1,49},{17,1},{33,17},{49,33},{2,50}... | collective-permute-start | bytes 245768 | tf_op jit(solution)/shard_map/ppermute | solution.py:28
  27.9 14.8 %collective-permute-start.16 = (bf16[112,4096]{1,0:T(8,128)(2,1)S(1)}, bf16[112,4096]{1,0:T(8,128)(2,1)S(1)}, u32[]{:S(2)}, u32[]{:S(2)}) collective-permute-start(bf16[112,4096]{1,0:T(8,128)(2,1)S(1)} %get-tuple-element.48), channel_id=1, source_target_pairs={{0,1},{1,0},{2,3},{3,2},{4,5},{5,4},{6,7},{7,6},{8,9},{9,8},{10,11... | collective-permute-start | bytes 2752520 | tf_op jit(solution)/shard_map/ppermute | solution.py:28
  30.0 97.9 %collective-permute-start.23 = (bf16[320,7168]{1,0:T(8,128)(2,1)}, bf16[320,7168]{1,0:T(8,128)(2,1)}, u32[]{:S(2)}, u32[]{:S(2)}) collective-permute-start(bf16[320,7168]{1,0:T(8,128)(2,1)} %down.1), channel_id=1, source_target_pairs={{0,1},{1,0},{2,3},{3,2},{4,5},{5,4},{6,7},{7,6},{8,9},{9,8},{10,11... | collective-permute-start | bytes 13762568 | tf_op jit(solution)/shard_map/ppermute | solution.py:28
  35.2 10.8 %collective-permute-start.13 = (bf16[64,2176]{1,0:T(8,128)(2,1)S(1)}, bf16[64,2176]{1,0:T(8,128)(2,1)S(1)}, u32[]{:S(2)}, u32[]{:S(2)}) collective-permute-start(bf16[64,2176]{1,0:T(8,128)(2,1)S(1)} %constant_dynamic-update-slice_fusion.4.b0), channel_id=1, source_target_pairs={{0,16},{16,32},{32,48},{48,0},{1,17},{17,33},{33,49},{49,1},{2,18}... | collective-permute-start | bytes 835592 | tf_op jit(solution)/shard_map/ppermute | solution.py:28
  37.2 15.1 %collective-permute-start.14 = (bf16[64,2176]{1,0:T(8,128)(2,1)S(1)}, bf16[64,2176]{1,0:T(8,128)(2,1)S(1)}, u32[]{:S(2)}, u32[]{:S(2)}) collective-permute-start(bf16[64,2176]{1,0:T(8,128)(2,1)S(1)} %constant_dynamic-update-slice_fusion.4.b0), channel_id=1, source_target_pairs={{0,32},{16,48},{32,0},{48,16},{1,33},{17,49},{33,1},{49,17},{2,34}... | collective-permute-start | bytes 835592 | tf_op jit(solution)/shard_map/ppermute | solution.py:28
  42.3 13.0 %collective-permute-start.17 = (bf16[112,4096]{1,0:T(8,128)(2,1)S(1)}, bf16[112,4096]{1,0:T(8,128)(2,1)S(1)}, u32[]{:S(2)}, u32[]{:S(2)}) collective-permute-start(bf16[112,4096]{1,0:T(8,128)(2,1)S(1)} %get-tuple-element.50), channel_id=1, source_target_pairs={{0,1},{1,0},{2,3},{3,2},{4,5},{5,4},{6,7},{7,6},{8,9},{9,8},{10,11... | collective-permute-start | bytes 2752520 | tf_op jit(solution)/shard_map/ppermute | solution.py:28
  42.7 14.2 %collective-permute-start.15 = (bf16[64,2176]{1,0:T(8,128)(2,1)S(1)}, bf16[64,2176]{1,0:T(8,128)(2,1)S(1)}, u32[]{:S(2)}, u32[]{:S(2)}) collective-permute-start(bf16[64,2176]{1,0:T(8,128)(2,1)S(1)} %constant_dynamic-update-slice_fusion.4.b0), channel_id=1, source_target_pairs={{0,48},{16,0},{32,16},{48,32},{1,49},{17,1},{33,17},{49,33},{2,50}... | collective-permute-start | bytes 835592 | tf_op jit(solution)/shard_map/ppermute | solution.py:28
  46.0 10.9 %collective-permute-start.10 = (bf16[64,2176]{1,0:T(8,128)(2,1)S(1)}, bf16[64,2176]{1,0:T(8,128)(2,1)S(1)}, u32[]{:S(2)}, u32[]{:S(2)}) collective-permute-start(bf16[64,2176]{1,0:T(8,128)(2,1)S(1)} %get-tuple-element.52), channel_id=1, source_target_pairs={{0,4},{4,8},{8,12},{12,0},{1,5},{5,9},{9,13},{13,1},{2,6},{6,10},{... | collective-permute-start | bytes 835592 | tf_op jit(solution)/shard_map/ppermute | solution.py:28
  52.3 8.4 %collective-permute-start.11 = (bf16[64,2176]{1,0:T(8,128)(2,1)S(1)}, bf16[64,2176]{1,0:T(8,128)(2,1)S(1)}, u32[]{:S(2)}, u32[]{:S(2)}) collective-permute-start(bf16[64,2176]{1,0:T(8,128)(2,1)S(1)} %get-tuple-element.53), channel_id=1, source_target_pairs={{0,8},{4,12},{8,0},{12,4},{1,9},{5,13},{9,1},{13,5},{2,10},{6,14},... | collective-permute-start | bytes 835592 | tf_op jit(solution)/shard_map/ppermute | solution.py:28
  55.3 11.2 %collective-permute-start.12 = (bf16[64,2176]{1,0:T(8,128)(2,1)S(1)}, bf16[64,2176]{1,0:T(8,128)(2,1)S(1)}, u32[]{:S(2)}, u32[]{:S(2)}) collective-permute-start(bf16[64,2176]{1,0:T(8,128)(2,1)S(1)} %get-tuple-element.51), channel_id=1, source_target_pairs={{0,12},{4,0},{8,4},{12,8},{1,13},{5,1},{9,5},{13,9},{2,14},{6,2},{... | collective-permute-start | bytes 835592 | tf_op jit(solution)/shard_map/ppermute | solution.py:28
  66.5 7.1 %copy-start.9 = (f32[7168]{0:T(1024)S(1)}, f32[7168]{0:T(1024)}, u32[]{:S(2)}) copy-start(f32[7168]{0:T(1024)} %param.22) | copy-start | bytes 86020
  68.4 5.1 %collective-permute-start.18 = (bf16[224,256]{1,0:T(8,128)(2,1)S(1)}, bf16[224,256]{1,0:T(8,128)(2,1)S(1)}, u32[]{:S(2)}, u32[]{:S(2)}) collective-permute-start(bf16[224,256]{1,0:T(8,128)(2,1)S(1)} %get-tuple-element.38), channel_id=1, source_target_pairs={{0,2},{2,0},{1,3},{3,1},{4,6},{6,4},{5,7},{7,5},{8,10},{10,8},{9,1... | collective-permute-start | bytes 344072 | tf_op jit(solution)/shard_map/ppermute | solution.py:28
  73.5 1.4 collective-permute-start.19
  109.7 6.1 %collective-permute-start.20 = (bf16[64,112,128]{2,1,0:T(8,128)(2,1)S(1)}, bf16[64,112,128]{2,1,0:T(8,128)(2,1)}, u32[]{:S(2)}, u32[]{:S(2)}) collective-permute-start(bf16[64,112,128]{2,1,0:T(8,128)(2,1)S(1)} %all_to_all.10.arrived.own), channel_id=1, source_target_pairs={{0,1},{1,0},{2,3},{3,2},{4,5},{5,4},{6,7},{7,6},{8,9},{9,8},{10,11... | collective-permute-start | bytes 5505032 | tf_op jit(solution)/shard_map/ppermute | solution.py:28
  114.4 1.4 collective-permute-start.21
  127.4 1.4 collective-permute-start.22
  137.2 6.4 %copy-start.10 = (s32[4,3]{1,0:T(4,128)S(1)}, s32[4,3]{1,0:T(4,128)}, u32[]{:S(2)}) copy-start(s32[4,3]{1,0:T(4,128)} %param.27) | copy-start | bytes 148
  137.2 33.1 %all-to-all-start.1 = ((bf16[64,2,7168]{2,1,0:T(2,128)(2,1)}), bf16[64,2,7168]{2,1,0:T(2,128)(2,1)S(1)}, u32[]{:S(2)}, u32[]{:S(2)}) async-start(bf16[64,2,7168]{2,1,0:T(2,128)(2,1)} %reshape.136), calls=%async_computation.1 | async-start | bytes 3670016 | tf_op jit(solution)/shard_map/all_to_all | solution.py:373
  143.6 29.7 %copy-start.1 = (bf16[4,256]{1,0:T(4,128)(2,1)S(1)}, bf16[4,256]{1,0:T(4,128)(2,1)}, u32[]{:S(2)}) copy-start(bf16[4,256]{1,0:T(4,128)(2,1)} %param.16) | copy-start | bytes 6148
  (8 other events, 13.4 us)

commit v2 on v1

v2 whole, which is shorter than its diff:
```python
import math

import jax
import jax.numpy as jnp
from jax import lax
from jax.experimental import pallas as pl
from jax.experimental.pallas import tpu as pltpu
from jax.sharding import Mesh, PartitionSpec as P

D = 7168
HEAD = 256
KALL = 16384
KHALF = KALL // 2
KQ = KHALF // 2
FIRST = 1536
LAST = KQ - FIRST
HID_DEV = 320
COLS = 112
EXPERTS = 8
BF = jnp.bfloat16
F32 = jnp.float32
SIZES = {"g": 2, "z": 4, "x": 4, "y": 2, "c": 2}
ALL = ("g", "z", "x", "y", "c")
SECTION = ("z", "x", "y", "c")


def shift(array, axis, step=1):
    n = SIZES[axis]
    return lax.ppermute(array, axis, [(i, (i + step) % n) for i in range(n)])


def others4(array, axis):
    return [shift(array, axis, 1), shift(array, axis, 2), shift(array, axis, 3)]


def ring_gy(array, step, swap=False):
    pairs = [
        (i * 2 + core, (i + step) % 4 * 2 + (1 - core if swap else core))
        for i in range(4)
        for core in range(2)
    ]
    return lax.ppermute(array, ("g", "y", "c"), pairs)


def crossed(array, stage, step):
    pairs = []
    for z in range(4):
        for x in range(4):
            for c in range(2):
                along_z = c == stage
                to = ((z + step) % 4, x) if along_z else (z, (x + step) % 4)
                pairs.append(((z * 4 + x) * 2 + c, (to[0] * 4 + to[1]) * 2 + c))
    return lax.ppermute(array, ("z", "x", "c"), pairs)


def pair_ordered(own, other, mine):
    return jnp.where(
        mine == 0, jnp.stack([own, other]), jnp.stack([other, own])
    )


VMEM = pl.BlockSpec(memory_space=pltpu.VMEM)
SMEM = pl.BlockSpec(memory_space=pltpu.SMEM)
HBM = pl.BlockSpec(memory_space=pltpu.HBM)


def in_hbm(array):
    return pltpu.with_memory_space_constraint(array, pltpu.HBM)


def row_of(value, row):
    here = lax.broadcasted_iota(jnp.int32, value.shape, 0) == row
    return jnp.sum(jnp.where(here, value, 0.0), axis=0, keepdims=True)


def attend_kernel(
    lengths, q, k, v, new_key, new_value, out, keys, values, fresh_key, fresh_value, sems
):
    rows = q.shape[0]
    fresh = [
        pltpu.make_async_copy(new_key, fresh_key, sems.at[2, 0]),
        pltpu.make_async_copy(new_value, fresh_value, sems.at[2, 1]),
    ]
    copies = [
        [
            pltpu.make_async_copy(source.at[r], kept.at[r], sems.at[i, r])
            for i, (source, kept) in enumerate(((k, keys), (v, values)))
        ]
        for r in range(rows)
    ]
    for copy in fresh + [copies[r][i] for p in range(0, rows, 2) for i in range(2) for r in (p, p + 1)]:
        copy.start()
    scaling = 1.0 / math.sqrt(HEAD)
    for copy in fresh:
        copy.wait()
    own_keys, own_values = fresh_key[...].astype(F32), fresh_value[...].astype(F32)
    for pair in range(0, rows, 2):
        probs, own_probs = [], []
        for r in (pair, pair + 1):
            copies[r][0].wait()
        for r in (pair, pair + 1):
            queried = (q[r].astype(F32) * scaling).astype(BF)
            itself = jnp.sum(
                queried.astype(F32) * row_of(own_keys, r), axis=1, keepdims=True
            )
            cached = lax.dot_general(
                queried, keys[r], (((1,), (1,)), ((), ())), preferred_element_type=F32
            )
            position = lax.broadcasted_iota(jnp.int32, cached.shape, 1)
            cached = jnp.where(position < lengths[r], cached, -jnp.inf)
            highest = jnp.maximum(jnp.max(cached, axis=1, keepdims=True), itself)
            cached_exp = jnp.exp(cached - highest)
            itself_exp = jnp.exp(itself - highest)
            share = 1.0 / (jnp.sum(cached_exp, axis=1, keepdims=True) + itself_exp)
            probs.append((cached_exp * share).astype(BF))
            own_probs.append((itself_exp * share).astype(BF).astype(F32))
        for r in (pair, pair + 1):
            copies[r][1].wait()
        for i, r in enumerate((pair, pair + 1)):
            mixture = jnp.dot(probs[i], values[r], preferred_element_type=F32)
            out[r] = (mixture + own_probs[i] * row_of(own_values, r)).astype(BF)


def attend(queries, new_key, new_value, cache_keys, cache_values, lengths):
    rows, context = cache_keys.shape[0], cache_keys.shape[1]
    heads = queries.shape[1] // HEAD
    return pl.pallas_call(
        attend_kernel,
        out_shape=jax.ShapeDtypeStruct((rows, heads, HEAD), BF),
        in_specs=[SMEM, VMEM, HBM, HBM, HBM, HBM],
        out_specs=VMEM,
        scratch_shapes=[
            pltpu.VMEM((rows, context, HEAD), BF),
            pltpu.VMEM((rows, context, HEAD), BF),
            pltpu.VMEM((rows, HEAD), BF),
            pltpu.VMEM((rows, HEAD), BF),
            pltpu.SemaphoreType.DMA((3, rows)),
        ],
        compiler_params=pltpu.CompilerParams(vmem_limit_bytes=24 << 20),
        cost_estimate=pl.CostEstimate(
            flops=4 * rows * heads * context * HEAD,
            bytes_accessed=4 * rows * context * HEAD,
            transcendentals=rows * heads * context,
        ),
        name="attend",
    )(
        in_hbm(lengths),
        queries.reshape(rows, heads, HEAD),
        in_hbm(cache_keys),
        in_hbm(cache_values),
        in_hbm(new_key),
        in_hbm(new_value),
    )


def at16(index):
    return pl.multiple_of(index, 16)


def cut_kernel(place, turned, near, f0, h0, f1, h1, sems):
    y, c = place[2], place[3]
    lanes = lambda start, size: pl.ds(pl.multiple_of(start, 512), size)
    copies = []
    for n, (of_c, of_y, part, size, out) in enumerate((
        (c, 1 - y, 0, FIRST, f0), (1 - c, 1 - y, 0, FIRST, h0), (1 - c, y, 0, KQ, near),
        (c, 1 - y, FIRST, LAST, f1), (1 - c, 1 - y, FIRST, LAST, h1),
    )):
        source = turned.at[:, lanes(of_c * KHALF + of_y * KQ + part, size)]
        copies.append(pltpu.make_async_copy(source, out, sems.at[n]))
    for copy in copies:
        copy.start()
    for copy in copies:
        copy.wait()


def cut(place, turned):
    return pl.pallas_call(
        cut_kernel,
        out_shape=(jax.ShapeDtypeStruct((COLS, KQ), BF),)
        + (jax.ShapeDtypeStruct((COLS, FIRST), BF),) * 2
        + (jax.ShapeDtypeStruct((COLS, LAST), BF),) * 2,
        in_specs=[SMEM, HBM],
        out_specs=(VMEM,) * 5,
        scratch_shapes=[pltpu.SemaphoreType.DMA((5,))],
        compiler_params=pltpu.CompilerParams(vmem_limit_bytes=16 << 20),
        name="cut",
    )(place, in_hbm(turned))


def spread_kernel(place, b0, b1, b2, b3, o0, o1, o2, o3):
    z, x, c = place[0], place[1], place[3]
    second = jnp.where(c == 0, x, z)
    for i, block in enumerate((b0, b1, b2, b3)):
        rows = slice(16 * i, 16 * i + 16)
        for k, out in enumerate((o0, o1, o2, o3)):
            out[rows, :KQ] = block[:, :KQ]
            lanes = pl.multiple_of(KQ + (second + k) % 4 * 128, 128)
            out[rows, KQ:] = block[:, pl.ds(lanes, 128)]


def spread(place, blocks):
    return pl.pallas_call(
        spread_kernel,
        out_shape=(jax.ShapeDtypeStruct((64, KQ + 128), BF),) * 4,
        in_specs=[SMEM] + [VMEM] * 4,
        out_specs=(VMEM,) * 4,
        compiler_params=pltpu.CompilerParams(vmem_limit_bytes=8 << 20),
        name="spread",
    )(place, *blocks)


def project_kernel(
    place, r0, r1, r2, r3, own, other, f0, f1, h0, h1, sent, kept, tail, w, rows, sems
):
    z, x, y, c = place[0], place[1], place[2], place[3]
    quarter = lambda start: pl.ds(pl.multiple_of(start, KQ), KQ)
    parts = (
        (own.at[:, quarter(c * KHALF + y * KQ)], 0, 0, KQ),
        (other, 1, 0, KQ),
        (f0, 2, 0, FIRST), (f1, 2, FIRST, LAST), (h0, 3, 0, FIRST), (h1, 3, FIRST, LAST),
    )
    copies = [
        pltpu.make_async_copy(
            source, w.at[pl.ds(i * COLS, COLS), pl.ds(start, size)], sems.at[n]
        )
        for n, (source, i, start, size) in enumerate(parts)
    ]
    for copy in copies:
        copy.start()
    for k, block in enumerate((r0, r1, r2, r3)):
        for i in range(4):
            of_z = (z - jnp.where(c == 0, i, k) + 4) % 4
            of_x = (x - jnp.where(c == 0, k, i) + 4) % 4
            row = at16(of_z * 64 + of_x * 16)
            rows[pl.ds(row, 16), :] = block[16 * i : 16 * i + 16, :KQ]
            tail[pl.ds(row, 16), :] = block[16 * i : 16 * i + 16, KQ:]
    for copy in copies:
        copy.wait()
    product = lax.dot_general(
        w[...], rows[...], (((1,), (1,)), ((), ())), preferred_element_type=F32
    )
    kept[...] = product[: 2 * COLS]
    sent[...] = product[2 * COLS :].astype(BF)


def project(place, blocks, own, other, fars):
    return pl.pallas_call(
        project_kernel,
        out_shape=(
            jax.ShapeDtypeStruct((2 * COLS, 256), BF),
            jax.ShapeDtypeStruct((2 * COLS, 256), F32),
            jax.ShapeDtypeStruct((256, 128), BF),
        ),
        in_specs=[SMEM] + [VMEM] * 4 + [HBM] + [pl.BlockSpec(memory_space=pl.ANY)] * 5,
        out_specs=(VMEM,) * 3,
        scratch_shapes=[
            pltpu.VMEM((4 * COLS, KQ), BF),
            pltpu.VMEM((256, KQ), BF),
            pltpu.SemaphoreType.DMA((6,)),
        ],
        compiler_params=pltpu.CompilerParams(vmem_limit_bytes=12 << 20),
        name="project",
    )(place, *blocks, in_hbm(own), other, *fars)


def chunk_kernel(gain, out):
    for i in range(D // COLS):
        out[i : i + 1, :] = gain[:, i * COLS : (i + 1) * COLS]


def chunked(gain):
    return pl.pallas_call(
        chunk_kernel,
        out_shape=jax.ShapeDtypeStruct((D // COLS, COLS), F32),
        in_specs=[VMEM],
        out_specs=VMEM,
        compiler_params=pltpu.CompilerParams(vmem_limit_bytes=2 << 20),
        name="chunked",
    )(gain)


def mix_kernel(place, kept, near, other, gains, tail, dispatched):
    chunk = ((place[0] * 4 + place[1]) * 2 + place[2]) * 2 + place[3]
    projected = kept[...] + near[...].astype(F32) + other[...]
    back = tail[...].astype(F32).T[:COLS]
    widened = (back + projected).astype(BF).astype(F32)
    column = jnp.broadcast_to(row_of(gains[...], chunk), (8, COLS)).T[:, :1]
    carried = (widened * column).astype(BF)
    position = lax.broadcasted_iota(jnp.int32, (256, 128), 0)
    slot = lax.broadcasted_iota(jnp.int32, (256, 128), 1)
    z, x, y, c = position // 64, position // 16 % 4, position // 8 % 2, position // 4 % 2
    here = ((c * 4 + z) * 4 + x) * 2 + y == slot // 2
    rank = (slot % 2 + 1).astype(F32)
    ranks = tail[...].astype(F32)
    for e in range(EXPERTS):
        pick = jnp.where(here & (ranks[:, COLS + e : COLS + e + 1] == rank), 1.0, 0.0).astype(BF)
        block = jnp.dot(carried, pick, preferred_element_type=F32).astype(BF)
        for device in range(8):
            dispatched[8 * e + device] = block


def mix(place, kept, near, other, gains, tail):
    return pl.pallas_call(
        mix_kernel,
        out_shape=jax.ShapeDtypeStruct((64, COLS, 128), BF),
        in_specs=[SMEM] + [VMEM] * 5,
        out_specs=VMEM,
        compiler_params=pltpu.CompilerParams(vmem_limit_bytes=12 << 20),
        name="mix",
    )(place, kept, near, other, gains, tail)


def load_kernel(first, second, out, sems):
    copies = []
    for i, source in enumerate((first, second)):
        for k in range(4):
            lanes = pl.ds(k * (D // 4), D // 4)
            copies.append(pltpu.make_async_copy(
                source.at[:, lanes], out.at[pl.ds(i * HID_DEV, HID_DEV), lanes], sems.at[i, k]
            ))
    for copy in copies:
        copy.start()
    for copy in copies:
        copy.wait()


def load(first, second, name):
    return pl.pallas_call(
        load_kernel,
        out_shape=jax.ShapeDtypeStruct((2 * HID_DEV, D), BF),
        in_specs=[HBM] * 2,
        out_specs=VMEM,
        scratch_shapes=[pltpu.SemaphoreType.DMA((2, 4))],
        compiler_params=pltpu.CompilerParams(vmem_limit_bytes=16 << 20),
        cost_estimate=pl.CostEstimate(
            flops=0, bytes_accessed=8 * HID_DEV * D, transcendentals=0
        ),
        name=name,
    )(in_hbm(first), in_hbm(second))


def squares_of(block, scales, chunk_of_c):
    i, c = chunk_of_c
    scale = jnp.where(c == 0, scales[:, 2 * i : 2 * i + 1], scales[:, 2 * i + 1 : 2 * i + 2])
    value = block.astype(F32) * scale
    return jnp.sum((value * value).reshape(14, 8, 128), axis=0)


def receive_kernel(
    place, arrived, gains, gate, up, columns, squares, kept, sent, weights, sems
):
    x, y, c = place[1], place[2], place[3]
    copies = []
    for i, source in enumerate((gate, up)):
        for k in range(4):
            lanes = pl.ds(k * (D // 4), D // 4)
            copies.append(pltpu.make_async_copy(
                source.at[:, lanes], weights.at[pl.ds(i * HID_DEV, HID_DEV), lanes], sems.at[i, k]
            ))
    for copy in copies:
        copy.start()
    scales = 1.0 / gains[...].T
    for g in range(2):
        total = jnp.zeros((8, 128), F32)
        lanes = slice(128 * g, 128 * g + 128)
        for i in range(32):
            block = arrived[32 * g + i]
            columns[pl.ds(at16((2 * i + c) * COLS), COLS), lanes] = block
            columns[pl.ds(at16((2 * i + 1 - c) * COLS), COLS), lanes] = jnp.zeros_like(block)
            total = total + squares_of(block, scales, (i, c))
        squares[:, lanes] = total
    row = lax.broadcasted_iota(jnp.int32, (32, 256), 0)
    lane = lax.broadcasted_iota(jnp.int32, (32, 256), 1)
    of_c = jnp.where(row < 16, c, 1 - c)
    slot = ((of_c * 4 + row // 2 % 4) * 4 + x) * 2 + y
    mine = lane == row // 8 % 2 * 128 + slot * 2 + row % 2
    residual = lax.dot_general(
        jnp.where(mine, 1.0, 0.0).astype(BF), columns[...],
        (((1,), (1,)), ((), ())), preferred_element_type=F32,
    ).astype(BF)
    kept[...] = residual[:16]
    sent[...] = residual[16:]
    for copy in copies:
        copy.wait()


def receive(place, arrived, gains, gate, up):
    return pl.pallas_call(
        receive_kernel,
        out_shape=(
            jax.ShapeDtypeStruct((D, 256), BF),
            jax.ShapeDtypeStruct((8, 256), F32),
            jax.ShapeDtypeStruct((16, D), BF),
            jax.ShapeDtypeStruct((16, D), BF),
            jax.ShapeDtypeStruct((2 * HID_DEV, D), BF),
        ),
        in_specs=[SMEM] + [VMEM] * 2 + [HBM] * 2,
        out_specs=(VMEM,) * 5,
        scratch_shapes=[pltpu.SemaphoreType.DMA((2, 4))],
        compiler_params=pltpu.CompilerParams(vmem_limit_bytes=16 << 20),
        name="receive",
    )(place, arrived, gains, in_hbm(gate), in_hbm(up))


def expert_kernel(place, seen, other, own_squares, gains, weights, sent, kept, columns, act):
    c = place[3]
    scales = 1.0 / gains[...].T
    other_squares = [jnp.zeros((8, 128), F32)] * 2
    for i in range(32):
        own_rows = pl.ds(at16((2 * i + c) * COLS), COLS)
        other_rows = pl.ds(at16((2 * i + 1 - c) * COLS), COLS)
        columns[own_rows, :] = seen[own_rows, :]
        for g in range(2):
            block = other[32 * g + i]
            columns[other_rows, 128 * g : 128 * g + 128] = block
            other_squares[g] = other_squares[g] + squares_of(block, scales, (i, 1 - c))
    product = jnp.dot(weights[...], columns[...], preferred_element_type=F32)
    squares = own_squares[...] + jnp.concatenate(other_squares, axis=1)
    scale = lax.rsqrt(jnp.sum(squares, axis=0, keepdims=True) / D + 1e-05)
    gated = product[:HID_DEV] * scale
    upward = product[HID_DEV:] * scale
    activated = gated / (1.0 + jnp.exp(-gated)) * upward
    act[...] = activated.T.astype(BF)
    for g in range(2):
        sent[g * 64 : g * 64 + 64, :] = act[pl.ds(at16(g * 128 + (1 - c) * 64), 64), :]
        kept[g * 64 : g * 64 + 64, :] = act[pl.ds(at16(g * 128 + c * 64), 64), :]


def expert(place, seen, other, own_squares, gains, weights):
    return pl.pallas_call(
        expert_kernel,
        out_shape=(jax.ShapeDtypeStruct((128, HID_DEV), BF),) * 2,
        in_specs=[SMEM] + [VMEM] * 5,
        out_specs=(VMEM,) * 2,
        scratch_shapes=[pltpu.VMEM((D, 256), BF), pltpu.VMEM((256, HID_DEV), BF)],
        compiler_params=pltpu.CompilerParams(vmem_limit_bytes=16 << 20),
        name="expert",
    )(place, seen, other, own_squares, gains, weights)


def lower_kernel(place, own, other, weights, kept, taken, gain, out, act):
    x, y = place[1], place[2]
    act[:, :HID_DEV] = own[...]
    act[:, HID_DEV:] = other[...]
    row = lax.broadcasted_iota(jnp.int32, (128, 16), 0)
    column = lax.broadcasted_iota(jnp.int32, (128, 16), 1)
    here = (row // 2 % 8 == x * 2 + y) & (row // 16 * 2 + row % 2 == column)
    place_in = jnp.where(here, 1.0, 0.0).astype(BF)
    width = D // 4
    for k in range(4):
        lanes = slice(k * width, (k + 1) * width)
        part = jnp.dot(act[...], weights[:, lanes], preferred_element_type=F32)
        residual = (kept[:, lanes] + taken[:, lanes]).astype(F32) / gain[:, lanes]
        high = residual.astype(BF)
        low = (residual - high.astype(F32)).astype(BF)
        part = part + jnp.dot(place_in, high, preferred_element_type=F32)
        part = part + jnp.dot(place_in, low, preferred_element_type=F32)
        out[:, :, lanes] = part.astype(BF).reshape(64, 2, width)


def lower(place, own, other, weights, kept, taken, gain):
    return pl.pallas_call(
        lower_kernel,
        out_shape=jax.ShapeDtypeStruct((64, 2, D), BF),
        in_specs=[SMEM] + [VMEM] * 6,
        out_specs=VMEM,
        scratch_shapes=[pltpu.VMEM((128, 2 * HID_DEV), BF)],
        compiler_params=pltpu.CompilerParams(vmem_limit_bytes=16 << 20),
        name="lower",
    )(place, own, other, weights, kept, taken, gain)


def combine_kernel(returned, parts, out):
    width = D // 4
    weights = parts[...]
    high = weights.astype(BF)
    low = (weights - high.astype(F32)).astype(BF)
    both = jnp.concatenate([high.astype(F32), low.astype(F32)], axis=0).astype(BF)
    for k in range(4):
        lanes = slice(k * width, (k + 1) * width)
        rows = returned[:, :, lanes].reshape(128, width)
        total = jnp.dot(both, rows, preferred_element_type=F32)
        out[:, lanes] = (total[:4] + total[8:12]).astype(BF)


def combine(returned, parts):
    return pl.pallas_call(
        combine_kernel,
        out_shape=jax.ShapeDtypeStruct((4, D), BF),
        in_specs=[VMEM] * 2,
        out_specs=VMEM,
        compiler_params=pltpu.CompilerParams(vmem_limit_bytes=8 << 20),
        name="combine",
    )(returned, parts)


def per_device(
    hidden,
    queries,
    new_key,
    new_value,
    cache_keys,
    cache_values,
    lengths,
    out_weight,
    ffn_gain,
    gate_weight,
    up_weight,
    down_weight,
    routes,
    route_gates,
):
    z, x, y, c = (lax.axis_index(a) for a in SECTION)
    chunk = ((z * 4 + x) * 2 + y) * 2 + c
    place = jnp.stack([z, x, y, c]).astype(jnp.int32)

    turned = out_weight.T

    expert_ids = lax.broadcasted_iota(jnp.int32, (1, 1, EXPERTS), 2)
    named = routes[:, :, None] == expert_ids
    names = jnp.any(named, axis=1).astype(jnp.int32)
    before = jnp.concatenate(
        [jnp.zeros((1, EXPERTS), jnp.int32), jnp.cumsum(names, axis=0)[:-1]], axis=0
    )
    slot_table = names * (before + 1)
    gate_table = jnp.sum(jnp.where(named, route_gates[:, :, None], 0), axis=1).astype(F32)
    shares = gate_table / jnp.sum(route_gates, axis=1, keepdims=True).astype(F32)
    ranks = lax.broadcasted_iota(jnp.int32, (1, 1, 8, 2), 3) + 1
    parts = jnp.where(
        slot_table[:, :, None, None] == ranks, shares[:, :, None, None], 0.0
    ).reshape(4, 128)
    parts = jnp.pad(parts, ((0, 4), (0, 0)))
    slot_lanes = jnp.pad(slot_table.astype(BF), ((0, 0), (0, 8)))

    def pick(array, index, dim):
        return lax.dynamic_index_in_dim(array, index, dim, keepdims=False)

    tails = jnp.concatenate(
        [
            hidden.reshape(4, 32, 2, COLS).transpose(2, 0, 1, 3),
            jnp.broadcast_to(slot_lanes[None, :, None, :], (2, 4, 32, 16)),
        ],
        axis=3,
    ).reshape(2, 4, 4, 4, 2, 128)
    tails = jnp.stack(
        [tails[0].transpose(3, 0, 1, 2, 4), tails[1].transpose(3, 0, 2, 1, 4)]
    ).reshape(2, 2, 4, 16 * 128)

    other_down = shift(down_weight, "c")
    attended = attend(queries, new_key, new_value, cache_keys, cache_values, lengths)
    halves = attended.reshape(4, 2, KHALF)

    def for_core(of_c):
        of_tails = pick(tails, of_c, 0)
        return jnp.concatenate([pick(halves, of_c, 1), of_tails[0], of_tails[1]], axis=1)

    block = pair_ordered(for_core(c), shift(for_core(1 - c), "c"), c).reshape(8, KHALF + 4096)
    block, cuttable = lax.optimization_barrier((block, turned))
    near, f0, h0, f1, h1 = cut(place, cuttable)
    near = shift(near, "c")

    def for_y(of_y):
        return jnp.concatenate(
            [
                lax.dynamic_slice_in_dim(block, of_y * KQ, KQ, 1),
                lax.dynamic_slice_in_dim(block, KHALF + of_y * 2048, 2048, 1),
            ],
            axis=1,
        )

    block = pair_ordered(for_y(y), shift(for_y(1 - y), "y"), y).reshape(16, KQ + 2048)
    block, f0, h0 = lax.optimization_barrier((block, f0, h0))
    f0, h0 = ring_gy(f0, 1), ring_gy(h0, -1, True)
    block, near, other_down = lax.optimization_barrier((block, near, other_down))
    along = jnp.where(c == 0, z, x)

    def with_tail(k):
        own = lax.dynamic_slice_in_dim(block, KQ + (along + k) % 4 * 512, 512, 1)
        return jnp.concatenate([block[:, :KQ], own], axis=1)

    blocks = [with_tail(0)] + [crossed(with_tail(k), 0, k) for k in (1, 2, 3)]
    blocks, f0, h0, f1, h1 = lax.optimization_barrier((blocks, f0, h0, f1, h1))
    f1, h1 = ring_gy(f1, 1), ring_gy(h1, -1, True)
    blocks, ffn_gain = lax.optimization_barrier((spread(place, blocks), ffn_gain))
    ffn_gain = ffn_gain.reshape(1, D)
    gains = chunked(ffn_gain)
    blocks = [blocks[0]] + [crossed(blocks[k], 1, k) for k in (1, 2, 3)]
    blocks, gains = lax.optimization_barrier((blocks, gains))
    sent, kept, tail = project(
        place, blocks, turned, near, (f0, f1, h0, h1)
    )
    near_sum = shift(sent, "y")
    crossing = kept[COLS:] + near_sum[COLS:].astype(F32)
    dispatched = mix(
        place, kept[:COLS], near_sum[:COLS], shift(crossing, "c"), gains, tail
    )
    dispatched, ready = lax.optimization_barrier((dispatched, (down_weight, other_down)))
    lower_weights = load(*ready, "load_lower")
    arrived = lax.all_to_all(dispatched, ("g", "z", "x", "y"), 0, 0, tiled=True)
    arrived, lower_weights = lax.optimization_barrier((arrived, lower_weights))
    other = shift(arrived, "c")
    seen, squares, kept, sent, upper_weights = receive(
        place, arrived, gains, gate_weight.T, up_weight.T
    )
    taken = shift(sent, "c")
    sent, own = expert(place, seen, other, squares, gains, upper_weights)
    summed = lower(place, own, shift(sent, "c"), lower_weights, kept, taken, ffn_gain)
    returned = lax.all_to_all(summed, ("g", "z", "x", "y"), 0, 0, tiled=True)
    return combine(returned, parts)


def solution(mesh):
    fine = Mesh(mesh.devices.reshape(*SIZES.values()), ALL)
    rows = P(ALL, None)
    return jax.shard_map(
        per_device,
        mesh=fine,
        in_specs=(
            rows,
            rows,
            rows,
            rows,
            P(ALL, None, None),
            P(ALL, None, None),
            P(ALL),
            P(None, SECTION),
            P(),
            P(None, ALL),
            P(None, ALL),
            rows,
            rows,
            rows,
        ),
        out_specs=rows,
        check_vma=False,
    )
```

time: 174 us -> 148 us (0.85)
  blocking collectives: 34.4 us -> 0 us
  Pallas kernels: 14.8 us -> 32.6 us
  waiting for transfers between devices: 57.8 us -> 70.4 us
  local copies, waits for them, and re-layouts: 18 us -> 7.63 us
  other arithmetic: 6.26 us -> 1.17 us
  starting transfers between devices: 39.1 us -> 35.3 us
  matrix products: 2.47 us -> 0 us
    all_to_all x1 -> x0, blocking collectives: 34.4 us -> none  [per_device(): arrived = lax.all_to_all(dispatched, ('g', 'z', 'x', 'y'), 0, 0, tiled=True)]
    ppermute x22 -> x9, starting transfers between devices: 29.5 us -> 4.85 us  [shift(): return lax.ppermute(array, axis, [(i, (i + step) % n) for i in range(n)])]
    ppermute x22 -> x9, waiting for transfers between devices: 27.9 us -> 7.8 us  [shift(): return lax.ppermute(array, axis, [(i, (i + step) % n) for i in range(n)])]
    all_to_all x1 -> x2, waiting for transfers between devices: 25.9 us -> 45 us  [the longest x1 25.7 us: per_device(): returned = lax.all_to_all(summed, ('g', 'z', 'x', 'y'), 0, 0, tiled=True)]
    pallas_call x2 -> x8, Pallas kernels: 5.5 us -> 23.4 us  [the longest x1 5.64 us: receive(): pl.pallas_call(receive_kernel, out_shape=(jax.ShapeDtypeStruct((D, 256),...]
    ppermute x2 -> x10, waiting for transfers between devices: 3.98 us -> 17.6 us  [the longest x6 14.4 us: crossed(): return lax.ppermute(array, ('z', 'x', 'c'), pairs)]
    ppermute x2 -> x10, starting transfers between devices: 3.24 us -> 15.7 us  [the longest x6 11.8 us: crossed(): return lax.ppermute(array, ('z', 'x', 'c'), pairs)]
    all_to_all x1 -> x2, starting transfers between devices: 6.41 us -> 14.7 us  [the longest x1 8.67 us: per_device(): arrived = lax.all_to_all(dispatched, ('g', 'z', 'x', 'y'), 0, 0, tiled=True)]
  transfers between devices with their start and end apart: 25 -> 21, of which waited for: 15 -> 13; matrix products, arithmetic and copies ran while one was open for 3% -> 1% of each run, Pallas kernels for 6% -> 11%
where the time goes in v2:
time: 148 us
  waiting for transfers between devices  70.4 us (48%)
  starting transfers between devices  35.3 us (24%)
  Pallas kernels  32.6 us (22%)
  local copies, waits for them, and re-layouts  7.63 us (5%)
    all_to_all x1, waiting for transfers between devices, per_device(): returned = lax.all_to_all(summed, ('g', 'z', 'x', 'y'), 0, 0, tiled=True)  25.7 us
    all_to_all x1, waiting for transfers between devices, per_device(): arrived = lax.all_to_all(dispatched, ('g', 'z', 'x', 'y'), 0, 0, tiled=True)  19.3 us
    ppermute x6, waiting for transfers between devices, crossed(): return lax.ppermute(array, ('z', 'x', 'c'), pairs)  14.4 us
    ppermute x6, starting transfers between devices, crossed(): return lax.ppermute(array, ('z', 'x', 'c'), pairs)  11.8 us
    all_to_all x1, starting transfers between devices, per_device(): arrived = lax.all_to_all(dispatched, ('g', 'z', 'x', 'y'), 0, 0, tiled=True)  8.67 us
    ppermute x9, waiting for transfers between devices, shift(): return lax.ppermute(array, axis, [(i, (i + step) % n) for i in range(n)])  7.8 us
    all_to_all x1, starting transfers between devices, per_device(): returned = lax.all_to_all(summed, ('g', 'z', 'x', 'y'), 0, 0, tiled=True)  6.07 us
    pallas_call x1, Pallas kernels, receive(): pl.pallas_call(receive_kernel, out_shape=(jax.ShapeDtypeStruct((D, 256),...  5.64 us
  transfers between devices with their start and end apart: 21, of which 13 were waited for; matrix products, arithmetic and copies ran while one was open for 1% of the time, Pallas kernels for 11%

profile of v2, /device:TPU:0, one launch (start us, length us, event | category | flops | bytes accessed | tf_op | source)
XLA Modules:
  0.0 147.6 jit_solution(15496889039663308490)
XLA Ops:
  0.9 0.9 reshape.72
  3.3 5.4 %attend.1 = bf16[4,64,256]{2,1,0:T(8,128)(2,1)S(1)} custom-call(s32[4]{0:T(128)} %lengths.1, bf16[4,64,256]{2,1,0:T(8,128)(2,1)S(1)} %bitcast.46, bf16[4,2048,256]{2,1,0:T(8,128)(2,1)} %k.1, bf16[4,2048,256]{2,1,0:T(8,128)(2,1)} %v.1, bf16[4,256]{1,0:T(4,128)(2,1)} %new_key.1, bf16[4,256]{1,0:T(4,128)(2,1)} %new_value.1), custom_call_target="tpu_custom_call" | custom-call | flops 536870912 | bytes 8388608 | tf_op jit(solution)/shard_map/attend/pallas_call | solution.py:127
  10.9 1.7 %collective-permute-start.1 = (bf16[8,6144]{1,0:T(8,128)(2,1)S(1)}, bf16[8,6144]{1,0:T(8,128)(2,1)S(1)}, u32[]{:S(2)}, u32[]{:S(2)}) collective-permute-start(bf16[8,6144]{1,0:T(8,128)(2,1)S(1)} %pad_maximum_fusion.5), channel_id=1, source_target_pairs={{0,2},{2,0},{1,3},{3,1},{4,6},{6,4},{5,7},{7,5},{8,10},{10,8},{9,1... | collective-permute-start | bytes 294920 | tf_op jit(solution)/shard_map/ppermute | solution.py:29
  12.7 2.3 %cut.1 = (bf16[112,4096]{1,0:T(8,128)(2,1)S(1)}, bf16[112,1536]{1,0:T(8,128)(2,1)S(1)}, bf16[112,1536]{1,0:T(8,128)(2,1)S(1)}, bf16[112,2560]{1,0:T(8,128)(2,1)S(1)}, bf16[112,2560]{1,0:T(8,128)(2,1)S(1)}) custom-call(s32[4]{0:T(128)S(1)} %pad_add_fusion.place, bf16[112,16384]{1,0:T(8,128)(2,1)} %bitcast.49), custom_call_target="tpu_custom_call" | custom-call | tf_op jit(solution)/shard_map/cut/pallas_call | solution.py:177
  15.9 1.7 %collective-permute-start.7 = (bf16[112,1536]{1,0:T(8,128)(2,1)S(1)}, bf16[112,1536]{1,0:T(8,128)(2,1)S(1)}, u32[]{:S(2)}, u32[]{:S(2)}) collective-permute-start(bf16[112,1536]{1,0:T(8,128)(2,1)S(1)} %get-tuple-element.62), channel_id=1, source_target_pairs={{0,2},{1,3},{2,64},{3,65},{64,66},{65,67},{66,0},{67,1},{4,6},{5,7... | collective-permute-start | bytes 1032200 | tf_op jit(solution)/shard_map/ppermute | solution.py:42
  18.6 4.2 %collective-permute-start.6 = (bf16[16,4608]{1,0:T(8,128)(2,1)S(1)}, bf16[16,4608]{1,0:T(8,128)(2,1)S(1)}, u32[]{:S(2)}, u32[]{:S(2)}) collective-permute-start(bf16[16,4608]{1,0:T(8,128)(2,1)S(1)} %get-tuple-element.117), channel_id=1, source_target_pairs={{0,48},{1,13},{4,52},{5,1},{8,56},{9,5},{12,60},{13,9},{16,0},{17,... | collective-permute-start | bytes 442376 | tf_op jit(solution)/shard_map/ppermute | solution.py:53
  22.8 1.9 %collective-permute-start.5 = (bf16[16,4608]{1,0:T(8,128)(2,1)S(1)}, bf16[16,4608]{1,0:T(8,128)(2,1)S(1)}, u32[]{:S(2)}, u32[]{:S(2)}) collective-permute-start(bf16[16,4608]{1,0:T(8,128)(2,1)S(1)} %get-tuple-element.119), channel_id=1, source_target_pairs={{0,32},{1,9},{4,36},{5,13},{8,40},{9,1},{12,44},{13,5},{16,48},{17... | collective-permute-start | bytes 442376 | tf_op jit(solution)/shard_map/ppermute | solution.py:53
  24.7 2.2 %collective-permute-done.7.f0 = bf16[112,1536]{1,0:T(8,128)(2,1)S(1)} collective-permute-done((bf16[112,1536]{1,0:T(8,128)(2,1)S(1)}, bf16[112,1536]{1,0:T(8,128)(2,1)S(1)}, u32[]{:S(2)}, u32[]{:S(2)}) %collective-permute-start.7) | collective-permute-done | bytes 344096 | tf_op jit(solution)/shard_map/ppermute | solution.py:42
  26.9 1.0 collective-permute-done.8.h0
  27.8 2.9 %collective-permute-done.4.b1 = bf16[16,4608]{1,0:T(8,128)(2,1)S(1)} collective-permute-done((bf16[16,4608]{1,0:T(8,128)(2,1)S(1)}, bf16[16,4608]{1,0:T(8,128)(2,1)S(1)}, u32[]{:S(2)}, u32[]{:S(2)}) %collective-permute-start.4) | collective-permute-done | bytes 147488 | tf_op jit(solution)/shard_map/ppermute | solution.py:53
  30.7 1.6 %collective-permute-start.12 = (bf16[112,2560]{1,0:T(8,128)(2,1)S(1)}, bf16[112,2560]{1,0:T(8,128)(2,1)S(1)}, u32[]{:S(2)}, u32[]{:S(2)}) collective-permute-start(bf16[112,2560]{1,0:T(8,128)(2,1)S(1)} %get-tuple-element.85), channel_id=1, source_target_pairs={{0,2},{1,3},{2,64},{3,65},{64,66},{65,67},{66,0},{67,1},{4,6},{5,7... | collective-permute-start | bytes 1720328 | tf_op jit(solution)/shard_map/ppermute | solution.py:42
  33.0 1.6 %collective-permute-start.9 = (bf16[64,4224]{1,0:T(8,128)(2,1)S(1)}, bf16[64,4224]{1,0:T(8,128)(2,1)S(1)}, u32[]{:S(2)}, u32[]{:S(2)}) collective-permute-start(bf16[64,4224]{1,0:T(8,128)(2,1)S(1)} %get-tuple-element.75), channel_id=1, source_target_pairs={{0,4},{1,17},{4,8},{5,21},{8,12},{9,25},{12,0},{13,29},{16,20},{17... | collective-permute-start | bytes 1622024 | tf_op jit(solution)/shard_map/ppermute | solution.py:53
  34.6 2.7 %collective-permute-start.10 = (bf16[64,4224]{1,0:T(8,128)(2,1)S(1)}, bf16[64,4224]{1,0:T(8,128)(2,1)S(1)}, u32[]{:S(2)}, u32[]{:S(2)}) collective-permute-start(bf16[64,4224]{1,0:T(8,128)(2,1)S(1)} %get-tuple-element.76), channel_id=1, source_target_pairs={{0,8},{1,33},{4,12},{5,37},{8,0},{9,41},{12,4},{13,45},{16,24},{17... | collective-permute-start | bytes 1622024 | tf_op jit(solution)/shard_map/ppermute | solution.py:53
  37.3 1.4 collective-permute-start.11
  38.9 4.7 %collective-permute-done.9.r1 = bf16[64,4224]{1,0:T(8,128)(2,1)S(1)} collective-permute-done((bf16[64,4224]{1,0:T(8,128)(2,1)S(1)}, bf16[64,4224]{1,0:T(8,128)(2,1)S(1)}, u32[]{:S(2)}, u32[]{:S(2)}) %collective-permute-start.9) | collective-permute-done | bytes 540704 | tf_op jit(solution)/shard_map/ppermute | solution.py:53
  43.6 6.8 %collective-permute-done.10.r2 = bf16[64,4224]{1,0:T(8,128)(2,1)S(1)} collective-permute-done((bf16[64,4224]{1,0:T(8,128)(2,1)S(1)}, bf16[64,4224]{1,0:T(8,128)(2,1)S(1)}, u32[]{:S(2)}, u32[]{:S(2)}) %collective-permute-start.10) | collective-permute-done | bytes 540704 | tf_op jit(solution)/shard_map/ppermute | solution.py:53
  50.4 2.9 %project.1 = (bf16[224,256]{1,0:T(8,128)(2,1)S(1)}, f32[224,256]{1,0:T(8,128)S(1)}, bf16[256,128]{1,0:T(8,128)(2,1)S(1)}) custom-call(s32[4]{0:T(128)S(1)} %pad_add_fusion.place, bf16[64,4224]{1,0:T(8,128)(2,1)S(1)} %get-tuple-element.79.r0, bf16[64,4224]{1,0:T(8,128)(2,1)S(1)} %collective-permute-done.9.r1, ...), custom_call_target="tpu_custom_call" | custom-call | tf_op jit(solution)/shard_map/project/pallas_call | solution.py:247
  53.4 1.7 %collective-permute-start.14 = (bf16[224,256]{1,0:T(8,128)(2,1)S(1)}, bf16[224,256]{1,0:T(8,128)(2,1)S(1)}, u32[]{:S(2)}, u32[]{:S(2)}) collective-permute-start(bf16[224,256]{1,0:T(8,128)(2,1)S(1)} %get-tuple-element.89), channel_id=1, source_target_pairs={{0,2},{2,0},{1,3},{3,1},{4,6},{6,4},{5,7},{7,5},{8,10},{10,8},{9,1... | collective-permute-start | bytes 344072 | tf_op jit(solution)/shard_map/ppermute | solution.py:29
  55.0 3.7 %collective-permute-done.14 = bf16[224,256]{1,0:T(8,128)(2,1)S(1)} collective-permute-done((bf16[224,256]{1,0:T(8,128)(2,1)S(1)}, bf16[224,256]{1,0:T(8,128)(2,1)S(1)}, u32[]{:S(2)}, u32[]{:S(2)}) %collective-permute-start.14) | collective-permute-done | bytes 114720 | tf_op jit(solution)/shard_map/ppermute | solution.py:29
  58.9 1.3 collective-permute-done.15.other
  60.2 2.3 %mix.1 = bf16[64,112,128]{2,1,0:T(8,128)(2,1)} custom-call(s32[4]{0:T(128)S(1)} %pad_add_fusion.place, f32[112,256]{1,0:T(8,128)S(1)} %get-tuple-element.108.kept, bf16[112,256]{1,0:T(8,128)(2,1)S(1)} %slice.59.near, f32[112,256]{1,0:T(8,128)S(1)} %collective-permute-done.15.other, f32[64,112]{1,0:T(8,128)S(1)} %chunked.1.gains, ...), custom_call_target="tpu_custom_call" | custom-call | tf_op jit(solution)/shard_map/mix/pallas_call | solution.py:303
  62.5 8.7 %all-to-all-start = ((bf16[64,112,128]{2,1,0:T(8,128)(2,1)}), bf16[64,112,128]{2,1,0:T(8,128)(2,1)S(1)}, u32[]{:S(2)}, u32[]{:S(2)}) async-start(bf16[64,112,128]{2,1,0:T(8,128)(2,1)} %mix.1), calls=%async_computation | async-start | bytes 3670016 | tf_op jit(solution)/shard_map/all_to_all | solution.py:599
  71.2 3.7 %load_lower.1.weights = bf16[640,7168]{1,0:T(8,128)(2,1)S(1)} custom-call(bf16[320,7168]{1,0:T(8,128)(2,1)} %first, bf16[320,7168]{1,0:T(8,128)(2,1)} %collective-permute-done.3.second), custom_call_target="tpu_custom_call" | custom-call | bytes 18350080 | tf_op jit(solution)/shard_map/load_lower/pallas_call | solution.py:328
  74.9 3.6 %copy-done = bf16[640,7168]{1,0:T(8,128)(2,1)} copy-done((bf16[640,7168]{1,0:T(8,128)(2,1)}, bf16[640,7168]{1,0:T(8,128)(2,1)S(1)}, u32[]{:S(2)}) %copy-start) | copy-done | bytes 9175064
  78.5 19.3 %all-to-all-done.arrived = bf16[64,112,128]{2,1,0:T(8,128)(2,1)S(1)} async-done(((bf16[64,112,128]{2,1,0:T(8,128)(2,1)}), bf16[64,112,128]{2,1,0:T(8,128)(2,1)S(1)}, u32[]{:S(2)}, u32[]{:S(2)}) %all-to-all-start) | async-done | bytes 1835040 | tf_op jit(solution)/shard_map/all_to_all | solution.py:599
  97.8 5.6 %receive.1 = (bf16[7168,256]{1,0:T(8,128)(2,1)S(1)}, f32[8,256]{1,0:T(8,128)S(1)}, bf16[16,7168]{1,0:T(8,128)(2,1)S(1)}, bf16[16,7168]{1,0:T(8,128)(2,1)S(1)}, bf16[640,7168]{1,0:T(8,128)(2,1)S(1)}) custom-call(s32[4]{0:T(128)S(1)} %pad_add_fusion.place, bf16[64,112,128]{2,1,0:T(8,128)(2,1)S(1)} %all-to-all-done.arrived, f32[64,112]{1,0:T(8,128)S(1)} %chunked.1.gains, ...), custom_call_target="tpu_custom_call" | custom-call | tf_op jit(solution)/shard_map/receive/pallas_call | solution.py:388
  104.0 3.9 %expert.1 = (bf16[128,320]{1,0:T(8,128)(2,1)S(1)}, bf16[128,320]{1,0:T(8,128)(2,1)S(1)}) custom-call(s32[4]{0:T(128)S(1)} %pad_add_fusion.place, bf16[7168,256]{1,0:T(8,128)(2,1)S(1)} %get-tuple-element.97.seen, bf16[64,112,128]{2,1,0:T(8,128)(2,1)S(1)} %collective-permute-done.16.other, f32[8,256]{1,0:T(8,128)S(1)} %get-tuple-element.98.own_squares, ...), custom_call_target="tpu_custom_call" | custom-call | tf_op jit(solution)/shard_map/expert/pallas_call | solution.py:430
  108.1 1.3 collective-permute-done.17.other
  109.4 4.5 %lower.1 = bf16[64,2,7168]{2,1,0:T(2,128)(2,1)} custom-call(s32[4]{0:T(128)S(1)} %pad_add_fusion.place, bf16[128,320]{1,0:T(8,128)(2,1)S(1)} %get-tuple-element.100.own, bf16[128,320]{1,0:T(8,128)(2,1)S(1)} %collective-permute-done.17.other, bf16[640,7168]{1,0:T(8,128)(2,1)S(1)} %bitcast.45, bf16[16,7168]{1,0:T(8,128)(2,1)S(1)} %get-tuple-element.103.kept, ...), custom_call_target="tpu_custom_call" | custom-call | tf_op jit(solution)/shard_map/lower/pallas_call | solution.py:462
  113.8 6.1 %all-to-all-start.1 = ((bf16[64,2,7168]{2,1,0:T(2,128)(2,1)}), bf16[64,2,7168]{2,1,0:T(2,128)(2,1)S(1)}, u32[]{:S(2)}, u32[]{:S(2)}) async-start(bf16[64,2,7168]{2,1,0:T(2,128)(2,1)} %lower.1), calls=%async_computation.1 | async-start | bytes 3670016 | tf_op jit(solution)/shard_map/all_to_all | solution.py:608
  120.8 25.7 %all-to-all-done.1.returned = bf16[64,2,7168]{2,1,0:T(2,128)(2,1)S(1)} async-done(((bf16[64,2,7168]{2,1,0:T(2,128)(2,1)}), bf16[64,2,7168]{2,1,0:T(2,128)(2,1)S(1)}, u32[]{:S(2)}, u32[]{:S(2)}) %all-to-all-start.1) | async-done | bytes 1835040 | tf_op jit(solution)/shard_map/all_to_all | solution.py:608
  146.5 1.0 combine.1
  (88 shorter events, 8.8 us)
Async XLA Ops:
  9.2 29.6 %copy-start.1 = (f32[7168]{0:T(1024)S(1)}, f32[7168]{0:T(1024)}, u32[]{:S(2)}) copy-start(f32[7168]{0:T(1024)} %param.22) | copy-start | bytes 86020
  9.3 1.4 collective-permute-start
  9.4 9.2 %collective-permute-start.3 = (bf16[320,7168]{1,0:T(8,128)(2,1)}, bf16[320,7168]{1,0:T(8,128)(2,1)}, u32[]{:S(2)}, u32[]{:S(2)}) collective-permute-start(bf16[320,7168]{1,0:T(8,128)(2,1)} %first), channel_id=1, source_target_pairs={{0,1},{1,0},{2,3},{3,2},{4,5},{5,4},{6,7},{7,6},{8,9},{9,8},{10,11... | collective-permute-start | bytes 13762568 | tf_op jit(solution)/shard_map/ppermute | solution.py:29
  10.9 4.9 %collective-permute-start.1 = (bf16[8,6144]{1,0:T(8,128)(2,1)S(1)}, bf16[8,6144]{1,0:T(8,128)(2,1)S(1)}, u32[]{:S(2)}, u32[]{:S(2)}) collective-permute-start(bf16[8,6144]{1,0:T(8,128)(2,1)S(1)} %pad_maximum_fusion.5), channel_id=1, source_target_pairs={{0,2},{2,0},{1,3},{3,1},{4,6},{6,4},{5,7},{7,5},{8,10},{10,8},{9,1... | collective-permute-start | bytes 294920 | tf_op jit(solution)/shard_map/ppermute | solution.py:29
  15.0 3.5 %collective-permute-start.2 = (bf16[112,4096]{1,0:T(8,128)(2,1)S(1)}, bf16[112,4096]{1,0:T(8,128)(2,1)S(1)}, u32[]{:S(2)}, u32[]{:S(2)}) collective-permute-start(bf16[112,4096]{1,0:T(8,128)(2,1)S(1)} %get-tuple-element.60), channel_id=1, source_target_pairs={{0,1},{1,0},{2,3},{3,2},{4,5},{5,4},{6,7},{7,6},{8,9},{9,8},{10,11... | collective-permute-start | bytes 2752520 | tf_op jit(solution)/shard_map/ppermute | solution.py:29
  15.9 11.0 %collective-permute-start.7 = (bf16[112,1536]{1,0:T(8,128)(2,1)S(1)}, bf16[112,1536]{1,0:T(8,128)(2,1)S(1)}, u32[]{:S(2)}, u32[]{:S(2)}) collective-permute-start(bf16[112,1536]{1,0:T(8,128)(2,1)S(1)} %get-tuple-element.62), channel_id=1, source_target_pairs={{0,2},{1,3},{2,64},{3,65},{64,66},{65,67},{66,0},{67,1},{4,6},{5,7... | collective-permute-start | bytes 1032200 | tf_op jit(solution)/shard_map/ppermute | solution.py:42
  17.6 10.2 %collective-permute-start.8 = (bf16[112,1536]{1,0:T(8,128)(2,1)S(1)}, bf16[112,1536]{1,0:T(8,128)(2,1)S(1)}, u32[]{:S(2)}, u32[]{:S(2)}) collective-permute-start(bf16[112,1536]{1,0:T(8,128)(2,1)S(1)} %get-tuple-element.63), channel_id=1, source_target_pairs={{0,67},{1,66},{2,1},{3,0},{64,3},{65,2},{66,65},{67,64},{4,71},{5,... | collective-permute-start | bytes 1032200 | tf_op jit(solution)/shard_map/ppermute | solution.py:42
  18.6 9.2 %collective-permute-start.6 = (bf16[16,4608]{1,0:T(8,128)(2,1)S(1)}, bf16[16,4608]{1,0:T(8,128)(2,1)S(1)}, u32[]{:S(2)}, u32[]{:S(2)}) collective-permute-start(bf16[16,4608]{1,0:T(8,128)(2,1)S(1)} %get-tuple-element.117), channel_id=1, source_target_pairs={{0,48},{1,13},{4,52},{5,1},{8,56},{9,5},{12,60},{13,9},{16,0},{17,... | collective-permute-start | bytes 442376 | tf_op jit(solution)/shard_map/ppermute | solution.py:53
  22.8 7.9 %collective-permute-start.4 = (bf16[16,4608]{1,0:T(8,128)(2,1)S(1)}, bf16[16,4608]{1,0:T(8,128)(2,1)S(1)}, u32[]{:S(2)}, u32[]{:S(2)}) collective-permute-start(bf16[16,4608]{1,0:T(8,128)(2,1)S(1)} %get-tuple-element.118), channel_id=1, source_target_pairs={{0,16},{1,5},{4,20},{5,9},{8,24},{9,13},{12,28},{13,1},{16,32},{17... | collective-permute-start | bytes 442376 | tf_op jit(solution)/shard_map/ppermute | solution.py:53
  22.8 7.9 %collective-permute-start.5 = (bf16[16,4608]{1,0:T(8,128)(2,1)S(1)}, bf16[16,4608]{1,0:T(8,128)(2,1)S(1)}, u32[]{:S(2)}, u32[]{:S(2)}) collective-permute-start(bf16[16,4608]{1,0:T(8,128)(2,1)S(1)} %get-tuple-element.119), channel_id=1, source_target_pairs={{0,32},{1,9},{4,36},{5,13},{8,40},{9,1},{12,44},{13,5},{16,48},{17... | collective-permute-start | bytes 442376 | tf_op jit(solution)/shard_map/ppermute | solution.py:53
  30.7 19.7 %collective-permute-start.12 = (bf16[112,2560]{1,0:T(8,128)(2,1)S(1)}, bf16[112,2560]{1,0:T(8,128)(2,1)S(1)}, u32[]{:S(2)}, u32[]{:S(2)}) collective-permute-start(bf16[112,2560]{1,0:T(8,128)(2,1)S(1)} %get-tuple-element.85), channel_id=1, source_target_pairs={{0,2},{1,3},{2,64},{3,65},{64,66},{65,67},{66,0},{67,1},{4,6},{5,7... | collective-permute-start | bytes 1720328 | tf_op jit(solution)/shard_map/ppermute | solution.py:42
  32.3 18.1 %collective-permute-start.13 = (bf16[112,2560]{1,0:T(8,128)(2,1)S(1)}, bf16[112,2560]{1,0:T(8,128)(2,1)S(1)}, u32[]{:S(2)}, u32[]{:S(2)}) collective-permute-start(bf16[112,2560]{1,0:T(8,128)(2,1)S(1)} %get-tuple-element.87), channel_id=1, source_target_pairs={{0,67},{1,66},{2,1},{3,0},{64,3},{65,2},{66,65},{67,64},{4,71},{5,... | collective-permute-start | bytes 1720328 | tf_op jit(solution)/shard_map/ppermute | solution.py:42
  33.0 10.6 %collective-permute-start.9 = (bf16[64,4224]{1,0:T(8,128)(2,1)S(1)}, bf16[64,4224]{1,0:T(8,128)(2,1)S(1)}, u32[]{:S(2)}, u32[]{:S(2)}) collective-permute-start(bf16[64,4224]{1,0:T(8,128)(2,1)S(1)} %get-tuple-element.75), channel_id=1, source_target_pairs={{0,4},{1,17},{4,8},{5,21},{8,12},{9,25},{12,0},{13,29},{16,20},{17... | collective-permute-start | bytes 1622024 | tf_op jit(solution)/shard_map/ppermute | solution.py:53
  34.6 15.9 %collective-permute-start.10 = (bf16[64,4224]{1,0:T(8,128)(2,1)S(1)}, bf16[64,4224]{1,0:T(8,128)(2,1)S(1)}, u32[]{:S(2)}, u32[]{:S(2)}) collective-permute-start(bf16[64,4224]{1,0:T(8,128)(2,1)S(1)} %get-tuple-element.76), channel_id=1, source_target_pairs={{0,8},{1,33},{4,12},{5,37},{8,0},{9,41},{12,4},{13,45},{16,24},{17... | collective-permute-start | bytes 1622024 | tf_op jit(solution)/shard_map/ppermute | solution.py:53
  37.3 13.1 %collective-permute-start.11 = (bf16[64,4224]{1,0:T(8,128)(2,1)S(1)}, bf16[64,4224]{1,0:T(8,128)(2,1)S(1)}, u32[]{:S(2)}, u32[]{:S(2)}) collective-permute-start(bf16[64,4224]{1,0:T(8,128)(2,1)S(1)} %get-tuple-element.77), channel_id=1, source_target_pairs={{0,12},{1,49},{4,0},{5,53},{8,4},{9,57},{12,8},{13,61},{16,28},{17... | collective-permute-start | bytes 1622024 | tf_op jit(solution)/shard_map/ppermute | solution.py:53
  53.4 5.4 %collective-permute-start.14 = (bf16[224,256]{1,0:T(8,128)(2,1)S(1)}, bf16[224,256]{1,0:T(8,128)(2,1)S(1)}, u32[]{:S(2)}, u32[]{:S(2)}) collective-permute-start(bf16[224,256]{1,0:T(8,128)(2,1)S(1)} %get-tuple-element.89), channel_id=1, source_target_pairs={{0,2},{2,0},{1,3},{3,1},{4,6},{6,4},{5,7},{7,5},{8,10},{10,8},{9,1... | collective-permute-start | bytes 344072 | tf_op jit(solution)/shard_map/ppermute | solution.py:29
  58.8 1.4 collective-permute-start.15
  62.5 35.3 %all-to-all-start = ((bf16[64,112,128]{2,1,0:T(8,128)(2,1)}), bf16[64,112,128]{2,1,0:T(8,128)(2,1)S(1)}, u32[]{:S(2)}, u32[]{:S(2)}) async-start(bf16[64,112,128]{2,1,0:T(8,128)(2,1)} %mix.1), calls=%async_computation | async-start | bytes 3670016 | tf_op jit(solution)/shard_map/all_to_all | solution.py:599
  74.9 3.6 %copy-start = (bf16[640,7168]{1,0:T(8,128)(2,1)}, bf16[640,7168]{1,0:T(8,128)(2,1)S(1)}, u32[]{:S(2)}) copy-start(bf16[640,7168]{1,0:T(8,128)(2,1)S(1)} %load_lower.1.weights) | copy-start | bytes 27525124
  97.8 6.2 %collective-permute-start.16 = (bf16[64,112,128]{2,1,0:T(8,128)(2,1)S(1)}, bf16[64,112,128]{2,1,0:T(8,128)(2,1)S(1)}, u32[]{:S(2)}, u32[]{:S(2)}) collective-permute-start(bf16[64,112,128]{2,1,0:T(8,128)(2,1)S(1)} %all-to-all-done.arrived), channel_id=1, source_target_pairs={{0,1},{1,0},{2,3},{3,2},{4,5},{5,4},{6,7},{7,6},{8,9},{9,8},{10,11... | collective-permute-start | bytes 5505032 | tf_op jit(solution)/shard_map/ppermute | solution.py:29
  97.8 11.6 %slice-start = ((s8[9175040]{0:T(1024)(128)(4,1)}), s8[4194304]{0:T(1024)(128)(4,1)S(1)}, s32[]{:S(2)}) async-start(s8[9175040]{0:T(1024)(128)(4,1)} %bitcast.44), calls=%async_computation.2 | async-start | bytes 8388608
  97.8 11.6 %slice-start.1 = ((s8[9175040]{0:T(1024)(128)(4,1)}), s8[786432]{0:T(1024)(128)(4,1)S(1)}, s32[]{:S(2)}) async-start(s8[9175040]{0:T(1024)(128)(4,1)} %bitcast.44), calls=%async_computation.3 | async-start | bytes 1572864
  103.4 4.6 %collective-permute-start.18 = (bf16[16,7168]{1,0:T(8,128)(2,1)S(1)}, bf16[16,7168]{1,0:T(8,128)(2,1)S(1)}, u32[]{:S(2)}, u32[]{:S(2)}) collective-permute-start(bf16[16,7168]{1,0:T(8,128)(2,1)S(1)} %get-tuple-element.104), channel_id=1, source_target_pairs={{0,1},{1,0},{2,3},{3,2},{4,5},{5,4},{6,7},{7,6},{8,9},{9,8},{10,11... | collective-permute-start | bytes 688136 | tf_op jit(solution)/shard_map/ppermute | solution.py:29
  104.0 5.3 %slice-start.2 = ((s8[9175040]{0:T(1024)(128)(4,1)}), s8[4194304]{0:T(1024)(128)(4,1)S(1)}, s32[]{:S(2)}) async-start(s8[9175040]{0:T(1024)(128)(4,1)} %bitcast.44), calls=%async_computation.4 | async-start | bytes 8388608
  108.0 1.4 collective-permute-start.17
  109.4 10.6 %copy-start.2 = (s32[4,3]{1,0:T(4,128)S(1)}, s32[4,3]{1,0:T(4,128)}, u32[]{:S(2)}) copy-start(s32[4,3]{1,0:T(4,128)} %param.27) | copy-start | bytes 148
  113.8 32.7 %all-to-all-start.1 = ((bf16[64,2,7168]{2,1,0:T(2,128)(2,1)}), bf16[64,2,7168]{2,1,0:T(2,128)(2,1)S(1)}, u32[]{:S(2)}, u32[]{:S(2)}) async-start(bf16[64,2,7168]{2,1,0:T(2,128)(2,1)} %lower.1), calls=%async_computation.1 | async-start | bytes 3670016 | tf_op jit(solution)/shard_map/all_to_all | solution.py:608

commit v3 on v2

--- a/solution.py
+++ b/solution.py
@@ -12,8 +12,6 @@
 KALL = 16384
 KHALF = KALL // 2
 KQ = KHALF // 2
-FIRST = 1536
-LAST = KQ - FIRST
 HID_DEV = 320
 COLS = 112
 EXPERTS = 8
@@ -40,6 +38,10 @@
         for core in range(2)
     ]
     return lax.ppermute(array, ("g", "y", "c"), pairs)
+
+
+def around(array, k):
+    return lax.ppermute(array, ("y", "c"), [(i, i ^ k) for i in range(4)])
 
 
 def crossed(array, stage, step):
@@ -74,13 +76,24 @@
 
 
 def attend_kernel(
-    lengths, q, k, v, new_key, new_value, out, keys, values, fresh_key, fresh_value, sems
+    lengths, routes, route_gates, place, q_in, hidden_in, k, v, new_key, new_value, turned,
+    p0, p1, p2, p3, f0, h0, near, parts,
+    q, hidden, keys, values, fresh_key, fresh_value, heads_of, flat, tails, sems,
 ):
     rows = q.shape[0]
+    y, c = place[2], place[3]
     fresh = [
-        pltpu.make_async_copy(new_key, fresh_key, sems.at[2, 0]),
-        pltpu.make_async_copy(new_value, fresh_value, sems.at[2, 1]),
+        pltpu.make_async_copy(q_in, q, sems.at[2, 0]),
+        pltpu.make_async_copy(hidden_in, hidden, sems.at[2, 1]),
+        pltpu.make_async_copy(new_key, fresh_key, sems.at[2, 2]),
+        pltpu.make_async_copy(new_value, fresh_value, sems.at[2, 3]),
     ]
+    cuts = []
+    for n, (of_c, of_y, part) in enumerate(((c, 1 - y, f0), (1 - c, 1 - y, h0), (1 - c, y, near))):
+        at = pl.multiple_of(of_c * KHALF + of_y * KQ, KQ)
+        cuts.append(pltpu.make_async_copy(
+            turned.at[:, pl.ds(at, KQ)], part, sems.at[3, n]
+        ))
     copies = [
         [
             pltpu.make_async_copy(source.at[r], kept.at[r], sems.at[i, r])
@@ -90,8 +103,55 @@
     ]
     for copy in fresh + [copies[r][i] for p in range(0, rows, 2) for i in range(2) for r in (p, p + 1)]:
         copy.start()
+    for copy in cuts:
+        copy.start()
+    fresh[0].wait()
     scaling = 1.0 / math.sqrt(HEAD)
-    for copy in fresh:
+    scaled = q[...].astype(F32) * scaling
+    for h in range(heads_of.shape[1]):
+        heads_of[:, h, :] = scaled[:, h * HEAD : (h + 1) * HEAD]
+
+    lane = lax.broadcasted_iota(jnp.int32, (1, 128), 1) - COLS
+    line = lax.broadcasted_iota(jnp.int32, (rows, 128), 0)
+    count = jnp.zeros((1, 128), F32)
+    slots = jnp.zeros((rows, 128), F32)
+    for r in range(rows):
+        named = (lane == routes[r, 0]) | (lane == routes[r, 1]) | (lane == routes[r, 2])
+        count = count + jnp.where(named, 1.0, 0.0)
+        slots = slots + jnp.where((line == r) & named, count, 0.0)
+    spot = lax.broadcasted_iota(jnp.int32, (1, 128), 1)
+    half = lax.broadcasted_iota(jnp.int32, (2 * rows, 128), 0)
+    of_expert, of_slot = spot // 16, spot % 2
+    used = jnp.zeros((1, 128), jnp.int32)
+    combined = jnp.zeros((2 * rows, 128), F32)
+    for r in range(rows):
+        gates = [jnp.full((1, 128), route_gates[r, k], jnp.int32).astype(F32) for k in range(3)]
+        named = [of_expert == routes[r, k] for k in range(3)]
+        chosen = jnp.zeros((1, 128), F32)
+        for k in range(3):
+            chosen = chosen + jnp.where(named[k], gates[k], 0.0)
+        share = chosen / (gates[0] + gates[1] + gates[2])
+        here = named[0] | named[1] | named[2]
+        share = jnp.where(here & (used == of_slot), share, 0.0)
+        used = used + jnp.where(here, 1, 0)
+        high = share.astype(BF).astype(F32)
+        combined = combined + jnp.where(half == r, high, 0.0)
+        combined = combined + jnp.where(half == rows + r, share - high, 0.0)
+    parts[...] = combined.astype(BF)
+    fresh[1].wait()
+    stream = hidden[...].astype(F32)
+    blank = jnp.zeros((rows, 128 - COLS), F32)
+    for z in range(4):
+        for x in range(4):
+            for iy in range(2):
+                for ic in range(2):
+                    chunk = ((z * 4 + x) * 2 + iy) * 2 + ic
+                    at = (x * 4 + z if ic else z * 4 + x) * 128
+                    part = stream[:, chunk * COLS : (chunk + 1) * COLS]
+                    part = jnp.concatenate([part, blank], axis=1) + slots
+                    tails[ic * 2 + iy, :, at : at + 128] = part.astype(BF)
+
+    for copy in fresh[2:]:
         copy.wait()
     own_keys, own_values = fresh_key[...].astype(F32), fresh_value[...].astype(F32)
     for pair in range(0, rows, 2):
@@ -99,12 +159,11 @@
         for r in (pair, pair + 1):
             copies[r][0].wait()
         for r in (pair, pair + 1):
-            queried = (q[r].astype(F32) * scaling).astype(BF)
-            itself = jnp.sum(
-                queried.astype(F32) * row_of(own_keys, r), axis=1, keepdims=True
-            )
+            queried = heads_of[r]
+            itself = jnp.sum(queried * row_of(own_keys, r), axis=1, keepdims=True)
             cached = lax.dot_general(
-                queried, keys[r], (((1,), (1,)), ((), ())), preferred_element_type=F32
+                queried.astype(BF), keys[r], (((1,), (1,)), ((), ())),
+                preferred_element_type=F32,
             )
             position = lax.broadcasted_iota(jnp.int32, cached.shape, 1)
             cached = jnp.where(position < lengths[r], cached, -jnp.inf)
@@ -118,23 +177,47 @@
             copies[r][1].wait()
         for i, r in enumerate((pair, pair + 1)):
             mixture = jnp.dot(probs[i], values[r], preferred_element_type=F32)
-            out[r] = (mixture + own_probs[i] * row_of(own_values, r)).astype(BF)
-
-
-def attend(queries, new_key, new_value, cache_keys, cache_values, lengths):
+            mixture = mixture + own_probs[i] * row_of(own_values, r)
+            for h in range(mixture.shape[0]):
+                at = h % 16 * HEAD
+                flat[h // 16, r : r + 1, at : at + HEAD] = mixture[h : h + 1, :]
+    for k, out in enumerate((p0, p1, p2, p3)):
+        of_c = 1 - c if k % 2 else c
+        of_y = 1 - y if k // 2 else y
+        out[:, :KQ] = flat[of_c * 2 + of_y].astype(BF)
+        out[:, KQ:] = tails[of_c * 2 + of_y]
+    for copy in cuts:
+        copy.wait()
+
+
+def attend(
+    queries, new_key, new_value, cache_keys, cache_values, lengths, routes, route_gates, hidden,
+    place, turned,
+):
     rows, context = cache_keys.shape[0], cache_keys.shape[1]
     heads = queries.shape[1] // HEAD
     return pl.pallas_call(
         attend_kernel,
-        out_shape=jax.ShapeDtypeStruct((rows, heads, HEAD), BF),
-        in_specs=[SMEM, VMEM, HBM, HBM, HBM, HBM],
-        out_specs=VMEM,
+        out_shape=(
+            *(jax.ShapeDtypeStruct((rows, KQ + 16 * 128), BF),) * 4,
+            jax.ShapeDtypeStruct((COLS, KQ), BF),
+            jax.ShapeDtypeStruct((COLS, KQ), BF),
+            jax.ShapeDtypeStruct((COLS, KQ), BF),
+            jax.ShapeDtypeStruct((2 * rows, 128), BF),
+        ),
+        in_specs=[SMEM] * 4 + [HBM] * 7,
+        out_specs=(VMEM,) * 8,
         scratch_shapes=[
+            pltpu.VMEM(queries.shape, BF),
+            pltpu.VMEM(hidden.shape, BF),
             pltpu.VMEM((rows, context, HEAD), BF),
             pltpu.VMEM((rows, context, HEAD), BF),
             pltpu.VMEM((rows, HEAD), BF),
             pltpu.VMEM((rows, HEAD), BF),
-            pltpu.SemaphoreType.DMA((3, rows)),
+            pltpu.VMEM((rows, heads, HEAD), F32),
+            pltpu.VMEM((4, rows, KQ), F32),
+            pltpu.VMEM((4, rows, 16 * 128), BF),
+            pltpu.SemaphoreType.DMA((4, rows)),
         ],
         compiler_params=pltpu.CompilerParams(vmem_limit_bytes=24 << 20),
         cost_estimate=pl.CostEstimate(
@@ -145,46 +228,21 @@
         name="attend",
     )(
         in_hbm(lengths),
-        queries.reshape(rows, heads, HEAD),
+        in_hbm(routes),
+        in_hbm(route_gates),
+        place,
+        in_hbm(queries),
+        in_hbm(hidden),
         in_hbm(cache_keys),
         in_hbm(cache_values),
         in_hbm(new_key),
         in_hbm(new_value),
+        in_hbm(turned),
     )
 
 
 def at16(index):
     return pl.multiple_of(index, 16)
-
-
-def cut_kernel(place, turned, near, f0, h0, f1, h1, sems):
-    y, c = place[2], place[3]
-    lanes = lambda start, size: pl.ds(pl.multiple_of(start, 512), size)
-    copies = []
-    for n, (of_c, of_y, part, size, out) in enumerate((
-        (c, 1 - y, 0, FIRST, f0), (1 - c, 1 - y, 0, FIRST, h0), (1 - c, y, 0, KQ, near),
-        (c, 1 - y, FIRST, LAST, f1), (1 - c, 1 - y, FIRST, LAST, h1),
-    )):
-        source = turned.at[:, lanes(of_c * KHALF + of_y * KQ + part, size)]
-        copies.append(pltpu.make_async_copy(source, out, sems.at[n]))
-    for copy in copies:
-        copy.start()
-    for copy in copies:
-        copy.wait()
-
-
-def cut(place, turned):
-    return pl.pallas_call(
-        cut_kernel,
-        out_shape=(jax.ShapeDtypeStruct((COLS, KQ), BF),)
-        + (jax.ShapeDtypeStruct((COLS, FIRST), BF),) * 2
-        + (jax.ShapeDtypeStruct((COLS, LAST), BF),) * 2,
-        in_specs=[SMEM, HBM],
-        out_specs=(VMEM,) * 5,
-        scratch_shapes=[pltpu.SemaphoreType.DMA((5,))],
-        compiler_params=pltpu.CompilerParams(vmem_limit_bytes=16 << 20),
-        name="cut",
-    )(place, in_hbm(turned))
 
 
 def spread_kernel(place, b0, b1, b2, b3, o0, o1, o2, o3):
@@ -210,20 +268,14 @@
 
 
 def project_kernel(
-    place, r0, r1, r2, r3, own, other, f0, f1, h0, h1, sent, kept, tail, w, rows, sems
+    place, r0, r1, r2, r3, own, other, far, far_other, kept, s1, s2, s3, tail, w, rows, sems
 ):
     z, x, y, c = place[0], place[1], place[2], place[3]
     quarter = lambda start: pl.ds(pl.multiple_of(start, KQ), KQ)
-    parts = (
-        (own.at[:, quarter(c * KHALF + y * KQ)], 0, 0, KQ),
-        (other, 1, 0, KQ),
-        (f0, 2, 0, FIRST), (f1, 2, FIRST, LAST), (h0, 3, 0, FIRST), (h1, 3, FIRST, LAST),
-    )
+    sources = (own.at[:, quarter(c * KHALF + y * KQ)], other, far, far_other)
     copies = [
-        pltpu.make_async_copy(
-            source, w.at[pl.ds(i * COLS, COLS), pl.ds(start, size)], sems.at[n]
-        )
-        for n, (source, i, start, size) in enumerate(parts)
+        pltpu.make_async_copy(source, w.at[pl.ds(n * COLS, COLS), :], sems.at[n])
+        for n, source in enumerate(sources)
     ]
     for copy in copies:
         copy.start()
@@ -239,24 +291,25 @@
     product = lax.dot_general(
         w[...], rows[...], (((1,), (1,)), ((), ())), preferred_element_type=F32
     )
-    kept[...] = product[: 2 * COLS]
-    sent[...] = product[2 * COLS :].astype(BF)
+    kept[...] = product[:COLS]
+    for i, sent in enumerate((s1, s2, s3)):
+        sent[...] = product[(i + 1) * COLS : (i + 2) * COLS].astype(BF)
 
 
 def project(place, blocks, own, other, fars):
     return pl.pallas_call(
         project_kernel,
         out_shape=(
-            jax.ShapeDtypeStruct((2 * COLS, 256), BF),
-            jax.ShapeDtypeStruct((2 * COLS, 256), F32),
+            jax.ShapeDtypeStruct((COLS, 256), F32),
+            *(jax.ShapeDtypeStruct((COLS, 256), BF),) * 3,
             jax.ShapeDtypeStruct((256, 128), BF),
         ),
-        in_specs=[SMEM] + [VMEM] * 4 + [HBM] + [pl.BlockSpec(memory_space=pl.ANY)] * 5,
-        out_specs=(VMEM,) * 3,
+        in_specs=[SMEM] + [VMEM] * 4 + [HBM] + [pl.BlockSpec(memory_space=pl.ANY)] * 3,
+        out_specs=(VMEM,) * 5,
         scratch_shapes=[
             pltpu.VMEM((4 * COLS, KQ), BF),
             pltpu.VMEM((256, KQ), BF),
-            pltpu.SemaphoreType.DMA((6,)),
+            pltpu.SemaphoreType.DMA((4,)),
         ],
         compiler_params=pltpu.CompilerParams(vmem_limit_bytes=12 << 20),
         name="project",
@@ -279,9 +332,9 @@
     )(gain)
 
 
-def mix_kernel(place, kept, near, other, gains, tail, dispatched):
+def mix_kernel(place, kept, r1, r2, r3, gains, tail, dispatched):
     chunk = ((place[0] * 4 + place[1]) * 2 + place[2]) * 2 + place[3]
-    projected = kept[...] + near[...].astype(F32) + other[...]
+    projected = kept[...] + r1[...].astype(F32) + (r2[...].astype(F32) + r3[...].astype(F32))
     back = tail[...].astype(F32).T[:COLS]
     widened = (back + projected).astype(BF).astype(F32)
     column = jnp.broadcast_to(row_of(gains[...], chunk), (8, COLS)).T[:, :1]
@@ -299,15 +352,15 @@
             dispatched[8 * e + device] = block
 
 
-def mix(place, kept, near, other, gains, tail):
+def mix(place, kept, taken, gains, tail):
     return pl.pallas_call(
         mix_kernel,
         out_shape=jax.ShapeDtypeStruct((64, COLS, 128), BF),
-        in_specs=[SMEM] + [VMEM] * 5,
+        in_specs=[SMEM] + [VMEM] * 6,
         out_specs=VMEM,
         compiler_params=pltpu.CompilerParams(vmem_limit_bytes=12 << 20),
         name="mix",
-    )(place, kept, near, other, gains, tail)
+    )(place, kept, *taken, gains, tail)
 
 
 def load_kernel(first, second, out, sems):
@@ -470,28 +523,25 @@
     )(place, own, other, weights, kept, taken, gain)
 
 
-def combine_kernel(returned, parts, out):
+def combine_kernel(returned, weights, out):
+    rows = out.shape[0]
     width = D // 4
-    weights = parts[...]
-    high = weights.astype(BF)
-    low = (weights - high.astype(F32)).astype(BF)
-    both = jnp.concatenate([high.astype(F32), low.astype(F32)], axis=0).astype(BF)
     for k in range(4):
         lanes = slice(k * width, (k + 1) * width)
-        rows = returned[:, :, lanes].reshape(128, width)
-        total = jnp.dot(both, rows, preferred_element_type=F32)
-        out[:, lanes] = (total[:4] + total[8:12]).astype(BF)
-
-
-def combine(returned, parts):
+        sums = returned[:, :, lanes].reshape(128, width)
+        total = jnp.dot(weights[...], sums, preferred_element_type=F32)
+        out[:, lanes] = (total[:rows] + total[rows:]).astype(BF)
+
+
+def combine(returned, weights):
     return pl.pallas_call(
         combine_kernel,
-        out_shape=jax.ShapeDtypeStruct((4, D), BF),
+        out_shape=jax.ShapeDtypeStruct((weights.shape[0] // 2, D), BF),
         in_specs=[VMEM] * 2,
         out_specs=VMEM,
         compiler_params=pltpu.CompilerParams(vmem_limit_bytes=8 << 20),
         name="combine",
-    )(returned, parts)
+    )(returned, weights)
 
 
 def per_device(
@@ -516,62 +566,17 @@
 
     turned = out_weight.T
 
-    expert_ids = lax.broadcasted_iota(jnp.int32, (1, 1, EXPERTS), 2)
-    named = routes[:, :, None] == expert_ids
-    names = jnp.any(named, axis=1).astype(jnp.int32)
-    before = jnp.concatenate(
-        [jnp.zeros((1, EXPERTS), jnp.int32), jnp.cumsum(names, axis=0)[:-1]], axis=0
-    )
-    slot_table = names * (before + 1)
-    gate_table = jnp.sum(jnp.where(named, route_gates[:, :, None], 0), axis=1).astype(F32)
-    shares = gate_table / jnp.sum(route_gates, axis=1, keepdims=True).astype(F32)
-    ranks = lax.broadcasted_iota(jnp.int32, (1, 1, 8, 2), 3) + 1
-    parts = jnp.where(
-        slot_table[:, :, None, None] == ranks, shares[:, :, None, None], 0.0
-    ).reshape(4, 128)
-    parts = jnp.pad(parts, ((0, 4), (0, 0)))
-    slot_lanes = jnp.pad(slot_table.astype(BF), ((0, 0), (0, 8)))
-
-    def pick(array, index, dim):
-        return lax.dynamic_index_in_dim(array, index, dim, keepdims=False)
-
-    tails = jnp.concatenate(
-        [
-            hidden.reshape(4, 32, 2, COLS).transpose(2, 0, 1, 3),
-            jnp.broadcast_to(slot_lanes[None, :, None, :], (2, 4, 32, 16)),
-        ],
-        axis=3,
-    ).reshape(2, 4, 4, 4, 2, 128)
-    tails = jnp.stack(
-        [tails[0].transpose(3, 0, 1, 2, 4), tails[1].transpose(3, 0, 2, 1, 4)]
-    ).reshape(2, 2, 4, 16 * 128)
-
     other_down = shift(down_weight, "c")
-    attended = attend(queries, new_key, new_value, cache_keys, cache_values, lengths)
-    halves = attended.reshape(4, 2, KHALF)
-
-    def for_core(of_c):
-        of_tails = pick(tails, of_c, 0)
-        return jnp.concatenate([pick(halves, of_c, 1), of_tails[0], of_tails[1]], axis=1)
-
-    block = pair_ordered(for_core(c), shift(for_core(1 - c), "c"), c).reshape(8, KHALF + 4096)
-    block, cuttable = lax.optimization_barrier((block, turned))
-    near, f0, h0, f1, h1 = cut(place, cuttable)
+    *payloads, f0, h0, near, parts = attend(
+        queries, new_key, new_value, cache_keys, cache_values, lengths, routes, route_gates,
+        hidden, place, turned,
+    )
     near = shift(near, "c")
-
-    def for_y(of_y):
-        return jnp.concatenate(
-            [
-                lax.dynamic_slice_in_dim(block, of_y * KQ, KQ, 1),
-                lax.dynamic_slice_in_dim(block, KHALF + of_y * 2048, 2048, 1),
-            ],
-            axis=1,
-        )
-
-    block = pair_ordered(for_y(y), shift(for_y(1 - y), "y"), y).reshape(16, KQ + 2048)
-    block, f0, h0 = lax.optimization_barrier((block, f0, h0))
-    f0, h0 = ring_gy(f0, 1), ring_gy(h0, -1, True)
-    block, near, other_down = lax.optimization_barrier((block, near, other_down))
+    far, far_other, near, other_down = lax.optimization_barrier((f0, h0, near, other_down))
+    far, far_other = ring_gy(far, 1), ring_gy(far_other, -1, True)
+    got = [payloads[0]] + [around(payloads[k], k) for k in (1, 2, 3)]
+    block = pair_ordered(pair_ordered(got[0], got[1], c), pair_ordered(got[2], got[3], c), y)
+    block = block.reshape(16, KQ + 2048)
     along = jnp.where(c == 0, z, x)
 
     def with_tail(k):
@@ -579,25 +584,20 @@
         return jnp.concatenate([block[:, :KQ], own], axis=1)
 
     blocks = [with_tail(0)] + [crossed(with_tail(k), 0, k) for k in (1, 2, 3)]
-    blocks, f0, h0, f1, h1 = lax.optimization_barrier((blocks, f0, h0, f1, h1))
-    f1, h1 = ring_gy(f1, 1), ring_gy(h1, -1, True)
-    blocks, ffn_gain = lax.optimization_barrier((spread(place, blocks), ffn_gain))
+    blocks, ffn_gain, ready = lax.optimization_barrier(
+        (spread(place, blocks), ffn_gain, (down_weight, other_down))
+    )
+    lower_weights = load(*ready, "load_lower")
     ffn_gain = ffn_gain.reshape(1, D)
     gains = chunked(ffn_gain)
     blocks = [blocks[0]] + [crossed(blocks[k], 1, k) for k in (1, 2, 3)]
-    blocks, gains = lax.optimization_barrier((blocks, gains))
-    sent, kept, tail = project(
-        place, blocks, turned, near, (f0, f1, h0, h1)
-    )
-    near_sum = shift(sent, "y")
-    crossing = kept[COLS:] + near_sum[COLS:].astype(F32)
-    dispatched = mix(
-        place, kept[:COLS], near_sum[:COLS], shift(crossing, "c"), gains, tail
-    )
-    dispatched, ready = lax.optimization_barrier((dispatched, (down_weight, other_down)))
-    lower_weights = load(*ready, "load_lower")
+    blocks, gains, lower_weights = lax.optimization_barrier((blocks, gains, lower_weights))
+    kept, *sent, tail = project(
+        place, blocks, turned, near, (far, far_other)
+    )
+    taken = [around(sent[k - 1], k) for k in (1, 2, 3)]
+    dispatched = mix(place, kept, taken, gains, tail)
     arrived = lax.all_to_all(dispatched, ("g", "z", "x", "y"), 0, 0, tiled=True)
-    arrived, lower_weights = lax.optimization_barrier((arrived, lower_weights))
     other = shift(arrived, "c")
     seen, squares, kept, sent, upper_weights = receive(
         place, arrived, gains, gate_weight.T, up_weight.T

time: 148 us -> 138 us (0.932)
  blocking collectives: 0 us -> 66.8 us
  waiting for transfers between devices: 70.4 us -> 21.8 us
  starting transfers between devices: 35.3 us -> 19.8 us
  local copies, waits for them, and re-layouts: 7.63 us -> 0.09 us
  Pallas kernels: 32.6 us -> 29.1 us
    all_to_all x0 -> x2, blocking collectives: none -> 66.8 us  [the longest x1 34.4 us: per_device(): arrived = lax.all_to_all(dispatched, ('g', 'z', 'x', 'y'), 0, 0, tiled=True)]
    all_to_all x2 -> x0, waiting for transfers between devices: 45 us -> none  [the longest x1 25.7 us: per_device(): returned = lax.all_to_all(summed, ('g', 'z', 'x', 'y'), 0, 0, tiled=True)]
    all_to_all x2 -> x0, starting transfers between devices: 14.7 us -> none  [the longest x1 8.67 us: per_device(): arrived = lax.all_to_all(dispatched, ('g', 'z', 'x', 'y'), 0, 0, tiled=True)]
    ppermute x0 -> x6, waiting for transfers between devices: none -> 6.69 us  [around(): return lax.ppermute(array, ('y', 'c'), [(i, i ^ k) for i in range(4)])]
    ppermute x9 -> x5, waiting for transfers between devices: 7.8 us -> 1.29 us  [shift(): return lax.ppermute(array, axis, [(i, (i + step) % n) for i in range(n)])]
    unnamed x20 -> x2, local copies, waits for them, and re-layouts: 5.58 us -> 0.01 us
    ppermute x0 -> x6, starting transfers between devices: none -> 4.2 us  [around(): return lax.ppermute(array, ('y', 'c'), [(i, i ^ k) for i in range(4)])]
    ppermute x9 -> x5, starting transfers between devices: 4.85 us -> 1.16 us  [shift(): return lax.ppermute(array, axis, [(i, (i + step) % n) for i in range(n)])]
  transfers between devices with their start and end apart: 21 -> 19, of which waited for: 13 -> 9; matrix products, arithmetic and copies ran while one was open for 1% -> 0% of each run, Pallas kernels for 11% -> 15%
where the time goes in v3:
time: 138 us
  blocking collectives  66.8 us (48%)
  Pallas kernels  29.1 us (21%)
  waiting for transfers between devices  21.8 us (16%)
  starting transfers between devices  19.8 us (14%)
    all_to_all x1, blocking collectives, per_device(): arrived = lax.all_to_all(dispatched, ('g', 'z', 'x', 'y'), 0, 0, tiled=True)  34.4 us
    all_to_all x1, blocking collectives, per_device(): returned = lax.all_to_all(summed, ('g', 'z', 'x', 'y'), 0, 0, tiled=True)  32.4 us
    ppermute x6, waiting for transfers between devices, crossed(): return lax.ppermute(array, ('z', 'x', 'c'), pairs)  13.9 us
    ppermute x6, starting transfers between devices, crossed(): return lax.ppermute(array, ('z', 'x', 'c'), pairs)  11.7 us
    pallas_call x1, Pallas kernels, attend(): pl.pallas_call(attend_kernel, out_shape=(*(jax.ShapeDtypeStruct((rows, KQ...  6.78 us
    ppermute x6, waiting for transfers between devices, around(): return lax.ppermute(array, ('y', 'c'), [(i, i ^ k) for i in range(4)])  6.69 us
    pallas_call x1, Pallas kernels, receive(): pl.pallas_call(receive_kernel, out_shape=(jax.ShapeDtypeStruct((D, 256),...  5.57 us
    ppermute x6, starting transfers between devices, around(): return lax.ppermute(array, ('y', 'c'), [(i, i ^ k) for i in range(4)])  4.2 us
  transfers between devices with their start and end apart: 19, of which 9 were waited for; matrix products, arithmetic and copies ran while one was open for 0% of the time, Pallas kernels for 15%

profile of v3, /device:TPU:0, one launch (start us, length us, event | category | flops | bytes accessed | tf_op | source)
XLA Modules:
  0.0 138.2 jit_solution(7325439586242360592)
XLA Ops:
  0.1 6.8 %attend.1 = (bf16[4,6144]{1,0:T(4,128)(2,1)S(1)}, bf16[4,6144]{1,0:T(4,128)(2,1)S(1)}, bf16[4,6144]{1,0:T(4,128)(2,1)S(1)}, bf16[4,6144]{1,0:T(4,128)(2,1)S(1)},...) custom-call(s32[4]{0:T(128)} %lengths.1, ...), custom_call_target="tpu_custom_call" | custom-call | flops 536870912 | bytes 8388608 | tf_op jit(solution)/shard_map/attend/pallas_call | solution.py:199
  6.9 0.6 collective-permute-start
  7.5 1.7 %collective-permute-start.1 = (bf16[4,6144]{1,0:T(4,128)(2,1)S(1)}, bf16[4,6144]{1,0:T(4,128)(2,1)S(1)}, u32[]{:S(2)}, u32[]{:S(2)}) collective-permute-start(bf16[4,6144]{1,0:T(4,128)(2,1)S(1)} %get-tuple-element.48), channel_id=1, source_target_pairs={{0,2},{1,3},{2,0},{3,1},{4,6},{5,7},{6,4},{7,5},{8,10},{9,11},{10,... | collective-permute-start | bytes 147464 | tf_op jit(solution)/shard_map/ppermute | solution.py:44
  9.1 0.5 collective-permute-start.6
  9.7 1.9 %collective-permute-done.1 = bf16[4,6144]{1,0:T(4,128)(2,1)S(1)} collective-permute-done((bf16[4,6144]{1,0:T(4,128)(2,1)S(1)}, bf16[4,6144]{1,0:T(4,128)(2,1)S(1)}, u32[]{:S(2)}, u32[]{:S(2)}) %collective-permute-start.1) | collective-permute-done | bytes 49184 | tf_op jit(solution)/shard_map/ppermute | solution.py:44
  11.6 1.6 %collective-permute-done.2 = bf16[4,6144]{1,0:T(4,128)(2,1)S(1)} collective-permute-done((bf16[4,6144]{1,0:T(4,128)(2,1)S(1)}, bf16[4,6144]{1,0:T(4,128)(2,1)S(1)}, u32[]{:S(2)}, u32[]{:S(2)}) %collective-permute-start.2) | collective-permute-done | bytes 49184 | tf_op jit(solution)/shard_map/ppermute | solution.py:44
  13.5 0.4 collective-permute-start.11
  14.0 2.3 %collective-permute-start.12 = (bf16[112,4096]{1,0:T(8,128)(2,1)S(1)}, bf16[112,4096]{1,0:T(8,128)(2,1)S(1)}, u32[]{:S(2)}, u32[]{:S(2)}) collective-permute-start(bf16[112,4096]{1,0:T(8,128)(2,1)S(1)} %get-tuple-element.71), channel_id=1, source_target_pairs={{0,67},{1,66},{2,1},{3,0},{64,3},{65,2},{66,65},{67,64},{4,71},{5,... | collective-permute-start | bytes 2752520 | tf_op jit(solution)/shard_map/ppermute | solution.py:40
  16.3 4.1 %collective-permute-start.5 = (bf16[16,4608]{1,0:T(8,128)(2,1)S(1)}, bf16[16,4608]{1,0:T(8,128)(2,1)S(1)}, u32[]{:S(2)}, u32[]{:S(2)}) collective-permute-start(bf16[16,4608]{1,0:T(8,128)(2,1)S(1)} %get-tuple-element.91), channel_id=1, source_target_pairs={{0,48},{1,13},{4,52},{5,1},{8,56},{9,5},{12,60},{13,9},{16,0},{17,... | collective-permute-start | bytes 442376 | tf_op jit(solution)/shard_map/ppermute | solution.py:55
  20.4 1.9 %collective-permute-start.4 = (bf16[16,4608]{1,0:T(8,128)(2,1)S(1)}, bf16[16,4608]{1,0:T(8,128)(2,1)S(1)}, u32[]{:S(2)}, u32[]{:S(2)}) collective-permute-start(bf16[16,4608]{1,0:T(8,128)(2,1)S(1)} %get-tuple-element.93), channel_id=1, source_target_pairs={{0,32},{1,9},{4,36},{5,13},{8,40},{9,1},{12,44},{13,5},{16,48},{17... | collective-permute-start | bytes 442376 | tf_op jit(solution)/shard_map/ppermute | solution.py:55
  22.3 0.8 collective-permute-done.5.b3
  23.1 5.3 %collective-permute-done.3.b1 = bf16[16,4608]{1,0:T(8,128)(2,1)S(1)} collective-permute-done((bf16[16,4608]{1,0:T(8,128)(2,1)S(1)}, bf16[16,4608]{1,0:T(8,128)(2,1)S(1)}, u32[]{:S(2)}, u32[]{:S(2)}) %collective-permute-start.3) | collective-permute-done | bytes 147488 | tf_op jit(solution)/shard_map/ppermute | solution.py:55
  28.3 0.7 spread.1
  29.0 1.6 %collective-permute-start.8 = (bf16[64,4224]{1,0:T(8,128)(2,1)S(1)}, bf16[64,4224]{1,0:T(8,128)(2,1)S(1)}, u32[]{:S(2)}, u32[]{:S(2)}) collective-permute-start(bf16[64,4224]{1,0:T(8,128)(2,1)S(1)} %get-tuple-element.59), channel_id=1, source_target_pairs={{0,4},{1,17},{4,8},{5,21},{8,12},{9,25},{12,0},{13,29},{16,20},{17... | collective-permute-start | bytes 1622024 | tf_op jit(solution)/shard_map/ppermute | solution.py:55
  30.6 2.7 %collective-permute-start.9 = (bf16[64,4224]{1,0:T(8,128)(2,1)S(1)}, bf16[64,4224]{1,0:T(8,128)(2,1)S(1)}, u32[]{:S(2)}, u32[]{:S(2)}) collective-permute-start(bf16[64,4224]{1,0:T(8,128)(2,1)S(1)} %get-tuple-element.60), channel_id=1, source_target_pairs={{0,8},{1,33},{4,12},{5,37},{8,0},{9,41},{12,4},{13,45},{16,24},{17... | collective-permute-start | bytes 1622024 | tf_op jit(solution)/shard_map/ppermute | solution.py:55
  33.3 1.4 %collective-permute-start.10 = (bf16[64,4224]{1,0:T(8,128)(2,1)S(1)}, bf16[64,4224]{1,0:T(8,128)(2,1)S(1)}, u32[]{:S(2)}, u32[]{:S(2)}) collective-permute-start(bf16[64,4224]{1,0:T(8,128)(2,1)S(1)} %get-tuple-element.61), channel_id=1, source_target_pairs={{0,12},{1,49},{4,0},{5,53},{8,4},{9,57},{12,8},{13,61},{16,28},{17... | collective-permute-start | bytes 1622024 | tf_op jit(solution)/shard_map/ppermute | solution.py:55
  34.9 3.7 %load_lower.1.weights = bf16[640,7168]{1,0:T(8,128)(2,1)S(1)} custom-call(bf16[320,7168]{1,0:T(8,128)(2,1)} %first, bf16[320,7168]{1,0:T(8,128)(2,1)} %collective-permute-done.7.second), custom_call_target="tpu_custom_call" | custom-call | bytes 18350080 | tf_op jit(solution)/shard_map/load_lower/pallas_call | solution.py:381
  38.7 1.0 collective-permute-done.8.r1
  39.7 6.8 %collective-permute-done.9.r2 = bf16[64,4224]{1,0:T(8,128)(2,1)S(1)} collective-permute-done((bf16[64,4224]{1,0:T(8,128)(2,1)S(1)}, bf16[64,4224]{1,0:T(8,128)(2,1)S(1)}, u32[]{:S(2)}, u32[]{:S(2)}) %collective-permute-start.9) | collective-permute-done | bytes 540704 | tf_op jit(solution)/shard_map/ppermute | solution.py:55
  46.5 2.9 %project.1 = (f32[112,256]{1,0:T(8,128)S(1)}, bf16[112,256]{1,0:T(8,128)(2,1)S(1)}, bf16[112,256]{1,0:T(8,128)(2,1)S(1)}, bf16[112,256]{1,0:T(8,128)(2,1)S(1)}, bf16[256,128]{1,0:T(8,128)(2,1)S(1)}) custom-call(s32[4]{0:T(128)S(1)} %pad_add_fusion.place, bf16[64,4224]{1,0:T(8,128)(2,1)S(1)} %get-tuple-element.65.r0, ...), custom_call_target="tpu_custom_call" | custom-call | tf_op jit(solution)/shard_map/project/pallas_call | solution.py:300
  49.7 1.6 %collective-permute-start.15 = (bf16[112,256]{1,0:T(8,128)(2,1)S(1)}, bf16[112,256]{1,0:T(8,128)(2,1)S(1)}, u32[]{:S(2)}, u32[]{:S(2)}) collective-permute-start(bf16[112,256]{1,0:T(8,128)(2,1)S(1)} %get-tuple-element.75), channel_id=1, source_target_pairs={{0,3},{1,2},{2,1},{3,0},{4,7},{5,6},{6,5},{7,4},{8,11},{9,10},{10,... | collective-permute-start | bytes 172040 | tf_op jit(solution)/shard_map/ppermute | solution.py:44
  51.3 2.9 %collective-permute-done.14.r2 = bf16[112,256]{1,0:T(8,128)(2,1)S(1)} collective-permute-done((bf16[112,256]{1,0:T(8,128)(2,1)S(1)}, bf16[112,256]{1,0:T(8,128)(2,1)S(1)}, u32[]{:S(2)}, u32[]{:S(2)}) %collective-permute-start.14) | collective-permute-done | bytes 57376 | tf_op jit(solution)/shard_map/ppermute | solution.py:44
  54.3 0.3 collective-permute-done.15.r3
  54.6 1.1 mix.1
  55.6 34.4 %all_to_all.10.arrived = bf16[64,112,128]{2,1,0:T(8,128)(2,1)S(1)} all-to-all(bf16[64,112,128]{2,1,0:T(8,128)(2,1)S(1)} %mix.1), channel_id=1, replica_groups=mesh['g'=2,'z'=4,'x'=4,'y'=2,'c'=2] {'g','z','x','y'}, dimensions={0} | all-to-all | bytes 3670016 | tf_op jit(solution)/shard_map/all_to_all | solution.py:600
  90.0 5.6 %receive.1 = (bf16[7168,256]{1,0:T(8,128)(2,1)S(1)}, f32[8,256]{1,0:T(8,128)S(1)}, bf16[16,7168]{1,0:T(8,128)(2,1)S(1)}, bf16[16,7168]{1,0:T(8,128)(2,1)S(1)}, bf16[640,7168]{1,0:T(8,128)(2,1)S(1)}) custom-call(s32[4]{0:T(128)S(1)} %pad_add_fusion.place, bf16[64,112,128]{2,1,0:T(8,128)(2,1)S(1)} %all_to_all.10.arrived, f32[64,112]{1,0:T(8,128)S(1)} %chunked.1.gains, ...), custom_call_target="tpu_custom_call" | custom-call | tf_op jit(solution)/shard_map/receive/pallas_call | solution.py:441
  95.6 0.6 collective-permute-start.18
  96.2 3.9 %expert.1 = (bf16[128,320]{1,0:T(8,128)(2,1)S(1)}, bf16[128,320]{1,0:T(8,128)(2,1)S(1)}) custom-call(s32[4]{0:T(128)S(1)} %pad_add_fusion.place, bf16[7168,256]{1,0:T(8,128)(2,1)S(1)} %get-tuple-element.78.seen, bf16[64,112,128]{2,1,0:T(8,128)(2,1)S(1)} %collective-permute-done.16.other, f32[8,256]{1,0:T(8,128)S(1)} %get-tuple-element.79.own_squares, ...), custom_call_target="tpu_custom_call" | custom-call | tf_op jit(solution)/shard_map/expert/pallas_call | solution.py:483
  100.2 1.3 collective-permute-done.17.other
  101.5 3.2 %lower.1 = bf16[64,2,7168]{2,1,0:T(2,128)(2,1)S(1)} custom-call(s32[4]{0:T(128)S(1)} %pad_add_fusion.place, bf16[128,320]{1,0:T(8,128)(2,1)S(1)} %get-tuple-element.81.own, bf16[128,320]{1,0:T(8,128)(2,1)S(1)} %collective-permute-done.17.other, bf16[640,7168]{1,0:T(8,128)(2,1)S(1)} %load_lower.1.weights, bf16[16,7168]{1,0:T(8,128)(2,1)S(1)} %get-tuple-element.84.kept, ...), custom_call_target="tpu_custom_call" | custom-call | tf_op jit(solution)/shard_map/lower/pallas_call | solution.py:515
  104.7 32.4 %all_to_all.11.returned = bf16[64,2,7168]{2,1,0:T(2,128)(2,1)S(1)} all-to-all(bf16[64,2,7168]{2,1,0:T(2,128)(2,1)S(1)} %lower.1), channel_id=1, replica_groups=mesh['g'=2,'z'=4,'x'=4,'y'=2,'c'=2] {'g','z','x','y'}, dimensions={0} | all-to-all | bytes 3670016 | tf_op jit(solution)/shard_map/all_to_all | solution.py:608
  137.1 1.0 combine.1
  (28 shorter events, 1.2 us)
Async XLA Ops:
  0.0 13.5 %collective-permute-start.7 = (bf16[320,7168]{1,0:T(8,128)(2,1)}, bf16[320,7168]{1,0:T(8,128)(2,1)}, u32[]{:S(2)}, u32[]{:S(2)}) collective-permute-start(bf16[320,7168]{1,0:T(8,128)(2,1)} %first), channel_id=1, source_target_pairs={{0,1},{1,0},{2,3},{3,2},{4,5},{5,4},{6,7},{7,6},{8,9},{9,8},{10,11... | collective-permute-start | bytes 13762568 | tf_op jit(solution)/shard_map/ppermute | solution.py:27
  0.1 34.7 %copy-start = (f32[7168]{0:T(1024)S(1)}, f32[7168]{0:T(1024)}, u32[]{:S(2)}) copy-start(f32[7168]{0:T(1024)} %param.22) | copy-start | bytes 86020
  6.9 2.7 %collective-permute-start = (bf16[4,6144]{1,0:T(4,128)(2,1)S(1)}, bf16[4,6144]{1,0:T(4,128)(2,1)S(1)}, u32[]{:S(2)}, u32[]{:S(2)}) collective-permute-start(bf16[4,6144]{1,0:T(4,128)(2,1)S(1)} %get-tuple-element.47), channel_id=1, source_target_pairs={{0,1},{1,0},{2,3},{3,2},{4,5},{5,4},{6,7},{7,6},{8,9},{9,8},{10,11... | collective-permute-start | bytes 147464 | tf_op jit(solution)/shard_map/ppermute | solution.py:44
  7.5 4.1 %collective-permute-start.1 = (bf16[4,6144]{1,0:T(4,128)(2,1)S(1)}, bf16[4,6144]{1,0:T(4,128)(2,1)S(1)}, u32[]{:S(2)}, u32[]{:S(2)}) collective-permute-start(bf16[4,6144]{1,0:T(4,128)(2,1)S(1)} %get-tuple-element.48), channel_id=1, source_target_pairs={{0,2},{1,3},{2,0},{3,1},{4,6},{5,7},{6,4},{7,5},{8,10},{9,11},{10,... | collective-permute-start | bytes 147464 | tf_op jit(solution)/shard_map/ppermute | solution.py:44
  9.1 4.0 %collective-permute-start.2 = (bf16[4,6144]{1,0:T(4,128)(2,1)S(1)}, bf16[4,6144]{1,0:T(4,128)(2,1)S(1)}, u32[]{:S(2)}, u32[]{:S(2)}) collective-permute-start(bf16[4,6144]{1,0:T(4,128)(2,1)S(1)} %get-tuple-element.49), channel_id=1, source_target_pairs={{0,3},{1,2},{2,1},{3,0},{4,7},{5,6},{6,5},{7,4},{8,11},{9,10},{10,... | collective-permute-start | bytes 147464 | tf_op jit(solution)/shard_map/ppermute | solution.py:44
  9.1 4.4 %collective-permute-start.6 = (bf16[112,4096]{1,0:T(8,128)(2,1)}, bf16[112,4096]{1,0:T(8,128)(2,1)S(1)}, u32[]{:S(2)}, u32[]{:S(2)}) collective-permute-start(bf16[112,4096]{1,0:T(8,128)(2,1)} %get-tuple-element.56), channel_id=1, source_target_pairs={{0,1},{1,0},{2,3},{3,2},{4,5},{5,4},{6,7},{7,6},{8,9},{9,8},{10,11... | collective-permute-start | bytes 2752520 | tf_op jit(solution)/shard_map/ppermute | solution.py:27
  13.5 32.9 %collective-permute-start.11 = (bf16[112,4096]{1,0:T(8,128)(2,1)S(1)}, bf16[112,4096]{1,0:T(8,128)(2,1)S(1)}, u32[]{:S(2)}, u32[]{:S(2)}) collective-permute-start(bf16[112,4096]{1,0:T(8,128)(2,1)S(1)} %get-tuple-element.70), channel_id=1, source_target_pairs={{0,2},{1,3},{2,64},{3,65},{64,66},{65,67},{66,0},{67,1},{4,6},{5,7... | collective-permute-start | bytes 2752520 | tf_op jit(solution)/shard_map/ppermute | solution.py:40
  14.0 32.5 %collective-permute-start.12 = (bf16[112,4096]{1,0:T(8,128)(2,1)S(1)}, bf16[112,4096]{1,0:T(8,128)(2,1)S(1)}, u32[]{:S(2)}, u32[]{:S(2)}) collective-permute-start(bf16[112,4096]{1,0:T(8,128)(2,1)S(1)} %get-tuple-element.71), channel_id=1, source_target_pairs={{0,67},{1,66},{2,1},{3,0},{64,3},{65,2},{66,65},{67,64},{4,71},{5,... | collective-permute-start | bytes 2752520 | tf_op jit(solution)/shard_map/ppermute | solution.py:40
  16.3 6.8 %collective-permute-start.5 = (bf16[16,4608]{1,0:T(8,128)(2,1)S(1)}, bf16[16,4608]{1,0:T(8,128)(2,1)S(1)}, u32[]{:S(2)}, u32[]{:S(2)}) collective-permute-start(bf16[16,4608]{1,0:T(8,128)(2,1)S(1)} %get-tuple-element.91), channel_id=1, source_target_pairs={{0,48},{1,13},{4,52},{5,1},{8,56},{9,5},{12,60},{13,9},{16,0},{17,... | collective-permute-start | bytes 442376 | tf_op jit(solution)/shard_map/ppermute | solution.py:55
  20.4 7.9 %collective-permute-start.3 = (bf16[16,4608]{1,0:T(8,128)(2,1)S(1)}, bf16[16,4608]{1,0:T(8,128)(2,1)S(1)}, u32[]{:S(2)}, u32[]{:S(2)}) collective-permute-start(bf16[16,4608]{1,0:T(8,128)(2,1)S(1)} %get-tuple-element.92), channel_id=1, source_target_pairs={{0,16},{1,5},{4,20},{5,9},{8,24},{9,13},{12,28},{13,1},{16,32},{17... | collective-permute-start | bytes 442376 | tf_op jit(solution)/shard_map/ppermute | solution.py:55
  20.4 7.9 %collective-permute-start.4 = (bf16[16,4608]{1,0:T(8,128)(2,1)S(1)}, bf16[16,4608]{1,0:T(8,128)(2,1)S(1)}, u32[]{:S(2)}, u32[]{:S(2)}) collective-permute-start(bf16[16,4608]{1,0:T(8,128)(2,1)S(1)} %get-tuple-element.93), channel_id=1, source_target_pairs={{0,32},{1,9},{4,36},{5,13},{8,40},{9,1},{12,44},{13,5},{16,48},{17... | collective-permute-start | bytes 442376 | tf_op jit(solution)/shard_map/ppermute | solution.py:55
  29.0 10.6 %collective-permute-start.8 = (bf16[64,4224]{1,0:T(8,128)(2,1)S(1)}, bf16[64,4224]{1,0:T(8,128)(2,1)S(1)}, u32[]{:S(2)}, u32[]{:S(2)}) collective-permute-start(bf16[64,4224]{1,0:T(8,128)(2,1)S(1)} %get-tuple-element.59), channel_id=1, source_target_pairs={{0,4},{1,17},{4,8},{5,21},{8,12},{9,25},{12,0},{13,29},{16,20},{17... | collective-permute-start | bytes 1622024 | tf_op jit(solution)/shard_map/ppermute | solution.py:55
  30.6 15.9 %collective-permute-start.9 = (bf16[64,4224]{1,0:T(8,128)(2,1)S(1)}, bf16[64,4224]{1,0:T(8,128)(2,1)S(1)}, u32[]{:S(2)}, u32[]{:S(2)}) collective-permute-start(bf16[64,4224]{1,0:T(8,128)(2,1)S(1)} %get-tuple-element.60), channel_id=1, source_target_pairs={{0,8},{1,33},{4,12},{5,37},{8,0},{9,41},{12,4},{13,45},{16,24},{17... | collective-permute-start | bytes 1622024 | tf_op jit(solution)/shard_map/ppermute | solution.py:55
  33.3 13.1 %collective-permute-start.10 = (bf16[64,4224]{1,0:T(8,128)(2,1)S(1)}, bf16[64,4224]{1,0:T(8,128)(2,1)S(1)}, u32[]{:S(2)}, u32[]{:S(2)}) collective-permute-start(bf16[64,4224]{1,0:T(8,128)(2,1)S(1)} %get-tuple-element.61), channel_id=1, source_target_pairs={{0,12},{1,49},{4,0},{5,53},{8,4},{9,57},{12,8},{13,61},{16,28},{17... | collective-permute-start | bytes 1622024 | tf_op jit(solution)/shard_map/ppermute | solution.py:55
  49.4 2.0 %collective-permute-start.13 = (bf16[112,256]{1,0:T(8,128)(2,1)S(1)}, bf16[112,256]{1,0:T(8,128)(2,1)S(1)}, u32[]{:S(2)}, u32[]{:S(2)}) collective-permute-start(bf16[112,256]{1,0:T(8,128)(2,1)S(1)} %get-tuple-element.73), channel_id=1, source_target_pairs={{0,1},{1,0},{2,3},{3,2},{4,5},{5,4},{6,7},{7,6},{8,9},{9,8},{10,11... | collective-permute-start | bytes 172040 | tf_op jit(solution)/shard_map/ppermute | solution.py:44
  49.5 4.8 %collective-permute-start.14 = (bf16[112,256]{1,0:T(8,128)(2,1)S(1)}, bf16[112,256]{1,0:T(8,128)(2,1)S(1)}, u32[]{:S(2)}, u32[]{:S(2)}) collective-permute-start(bf16[112,256]{1,0:T(8,128)(2,1)S(1)} %get-tuple-element.74), channel_id=1, source_target_pairs={{0,2},{1,3},{2,0},{3,1},{4,6},{5,7},{6,4},{7,5},{8,10},{9,11},{10,... | collective-permute-start | bytes 172040 | tf_op jit(solution)/shard_map/ppermute | solution.py:44
  49.7 4.8 %collective-permute-start.15 = (bf16[112,256]{1,0:T(8,128)(2,1)S(1)}, bf16[112,256]{1,0:T(8,128)(2,1)S(1)}, u32[]{:S(2)}, u32[]{:S(2)}) collective-permute-start(bf16[112,256]{1,0:T(8,128)(2,1)S(1)} %get-tuple-element.75), channel_id=1, source_target_pairs={{0,3},{1,2},{2,1},{3,0},{4,7},{5,6},{6,5},{7,4},{8,11},{9,10},{10,... | collective-permute-start | bytes 172040 | tf_op jit(solution)/shard_map/ppermute | solution.py:44
  90.0 6.2 %collective-permute-start.16 = (bf16[64,112,128]{2,1,0:T(8,128)(2,1)S(1)}, bf16[64,112,128]{2,1,0:T(8,128)(2,1)S(1)}, u32[]{:S(2)}, u32[]{:S(2)}) collective-permute-start(bf16[64,112,128]{2,1,0:T(8,128)(2,1)S(1)} %all_to_all.10.arrived), channel_id=1, source_target_pairs={{0,1},{1,0},{2,3},{3,2},{4,5},{5,4},{6,7},{7,6},{8,9},{9,8},{10,11... | collective-permute-start | bytes 5505032 | tf_op jit(solution)/shard_map/ppermute | solution.py:27
  95.6 4.6 %collective-permute-start.18 = (bf16[16,7168]{1,0:T(8,128)(2,1)S(1)}, bf16[16,7168]{1,0:T(8,128)(2,1)S(1)}, u32[]{:S(2)}, u32[]{:S(2)}) collective-permute-start(bf16[16,7168]{1,0:T(8,128)(2,1)S(1)} %get-tuple-element.85), channel_id=1, source_target_pairs={{0,1},{1,0},{2,3},{3,2},{4,5},{5,4},{6,7},{7,6},{8,9},{9,8},{10,11... | collective-permute-start | bytes 688136 | tf_op jit(solution)/shard_map/ppermute | solution.py:27
  100.1 1.4 collective-permute-start.17

commit v4 on v3

--- a/solution.py
+++ b/solution.py
@@ -76,18 +76,12 @@
 
 
 def attend_kernel(
-    lengths, routes, route_gates, place, q_in, hidden_in, k, v, new_key, new_value, turned,
+    lengths, routes, route_gates, place, q, hidden, k, v, new_key, new_value, turned,
     p0, p1, p2, p3, f0, h0, near, parts,
-    q, hidden, keys, values, fresh_key, fresh_value, heads_of, flat, tails, sems,
+    keys, values, heads_of, flat, tails, sems,
 ):
     rows = q.shape[0]
     y, c = place[2], place[3]
-    fresh = [
-        pltpu.make_async_copy(q_in, q, sems.at[2, 0]),
-        pltpu.make_async_copy(hidden_in, hidden, sems.at[2, 1]),
-        pltpu.make_async_copy(new_key, fresh_key, sems.at[2, 2]),
-        pltpu.make_async_copy(new_value, fresh_value, sems.at[2, 3]),
-    ]
     cuts = []
     for n, (of_c, of_y, part) in enumerate(((c, 1 - y, f0), (1 - c, 1 - y, h0), (1 - c, y, near))):
         at = pl.multiple_of(of_c * KHALF + of_y * KQ, KQ)
@@ -101,11 +95,10 @@
         ]
         for r in range(rows)
     ]
-    for copy in fresh + [copies[r][i] for p in range(0, rows, 2) for i in range(2) for r in (p, p + 1)]:
+    for copy in [copies[r][i] for p in range(0, rows, 2) for i in range(2) for r in (p, p + 1)]:
         copy.start()
     for copy in cuts:
         copy.start()
-    fresh[0].wait()
     scaling = 1.0 / math.sqrt(HEAD)
     scaled = q[...].astype(F32) * scaling
     for h in range(heads_of.shape[1]):
@@ -138,7 +131,6 @@
         combined = combined + jnp.where(half == r, high, 0.0)
         combined = combined + jnp.where(half == rows + r, share - high, 0.0)
     parts[...] = combined.astype(BF)
-    fresh[1].wait()
     stream = hidden[...].astype(F32)
     blank = jnp.zeros((rows, 128 - COLS), F32)
     for z in range(4):
@@ -151,9 +143,7 @@
                     part = jnp.concatenate([part, blank], axis=1) + slots
                     tails[ic * 2 + iy, :, at : at + 128] = part.astype(BF)
 
-    for copy in fresh[2:]:
-        copy.wait()
-    own_keys, own_values = fresh_key[...].astype(F32), fresh_value[...].astype(F32)
+    own_keys, own_values = new_key[...].astype(F32), new_value[...].astype(F32)
     for pair in range(0, rows, 2):
         probs, own_probs = [], []
         for r in (pair, pair + 1):
@@ -205,15 +195,11 @@
             jax.ShapeDtypeStruct((COLS, KQ), BF),
             jax.ShapeDtypeStruct((2 * rows, 128), BF),
         ),
-        in_specs=[SMEM] * 4 + [HBM] * 7,
+        in_specs=[SMEM] * 4 + [VMEM] * 2 + [HBM] * 2 + [VMEM] * 2 + [HBM],
         out_specs=(VMEM,) * 8,
         scratch_shapes=[
-            pltpu.VMEM(queries.shape, BF),
-            pltpu.VMEM(hidden.shape, BF),
             pltpu.VMEM((rows, context, HEAD), BF),
             pltpu.VMEM((rows, context, HEAD), BF),
-            pltpu.VMEM((rows, HEAD), BF),
-            pltpu.VMEM((rows, HEAD), BF),
             pltpu.VMEM((rows, heads, HEAD), F32),
             pltpu.VMEM((4, rows, KQ), F32),
             pltpu.VMEM((4, rows, 16 * 128), BF),

time: 138 us -> 138 us (level)
  no operation moved by 1% of the time
where the time goes in v4:
time: 138 us
  blocking collectives  66.8 us (48%)
  Pallas kernels  29.1 us (21%)
  waiting for transfers between devices  21.8 us (16%)
  starting transfers between devices  19.8 us (14%)
    all_to_all x1, blocking collectives, per_device(): arrived = lax.all_to_all(dispatched, ('g', 'z', 'x', 'y'), 0, 0, tiled=True)  34.4 us
    all_to_all x1, blocking collectives, per_device(): returned = lax.all_to_all(summed, ('g', 'z', 'x', 'y'), 0, 0, tiled=True)  32.4 us
    ppermute x6, waiting for transfers between devices, crossed(): return lax.ppermute(array, ('z', 'x', 'c'), pairs)  13.8 us
    ppermute x6, starting transfers between devices, crossed(): return lax.ppermute(array, ('z', 'x', 'c'), pairs)  11.7 us
    pallas_call x1, Pallas kernels, attend(): pl.pallas_call(attend_kernel, out_shape=(*(jax.ShapeDtypeStruct((rows, KQ...  6.78 us
    ppermute x6, waiting for transfers between devices, around(): return lax.ppermute(array, ('y', 'c'), [(i, i ^ k) for i in range(4)])  6.7 us
    pallas_call x1, Pallas kernels, receive(): pl.pallas_call(receive_kernel, out_shape=(jax.ShapeDtypeStruct((D, 256),...  5.57 us
    ppermute x6, starting transfers between devices, around(): return lax.ppermute(array, ('y', 'c'), [(i, i ^ k) for i in range(4)])  4.19 us
  transfers between devices with their start and end apart: 19, of which 9 were waited for; matrix products, arithmetic and copies ran while one was open for 0% of the time, Pallas kernels for 15%

profile of v4, /device:TPU:0, one launch (start us, length us, event | category | flops | bytes accessed | tf_op | source)
XLA Modules:
  0.0 138.2 jit_solution(4773880266593657587)
XLA Ops:
  0.1 6.8 %attend.1 = (bf16[4,6144]{1,0:T(4,128)(2,1)S(1)}, bf16[4,6144]{1,0:T(4,128)(2,1)S(1)}, bf16[4,6144]{1,0:T(4,128)(2,1)S(1)}, bf16[4,6144]{1,0:T(4,128)(2,1)S(1)},...) custom-call(s32[4]{0:T(128)} %lengths.1, ...), custom_call_target="tpu_custom_call" | custom-call | flops 536870912 | bytes 8388608 | tf_op jit(solution)/shard_map/attend/pallas_call | solution.py:189
  6.9 0.6 collective-permute-start
  7.5 1.7 %collective-permute-start.1 = (bf16[4,6144]{1,0:T(4,128)(2,1)S(1)}, bf16[4,6144]{1,0:T(4,128)(2,1)S(1)}, u32[]{:S(2)}, u32[]{:S(2)}) collective-permute-start(bf16[4,6144]{1,0:T(4,128)(2,1)S(1)} %get-tuple-element.48), channel_id=1, source_target_pairs={{0,2},{1,3},{2,0},{3,1},{4,6},{5,7},{6,4},{7,5},{8,10},{9,11},{10,... | collective-permute-start | bytes 147464 | tf_op jit(solution)/shard_map/ppermute | solution.py:44
  9.1 0.5 collective-permute-start.6
  9.7 1.9 %collective-permute-done.1 = bf16[4,6144]{1,0:T(4,128)(2,1)S(1)} collective-permute-done((bf16[4,6144]{1,0:T(4,128)(2,1)S(1)}, bf16[4,6144]{1,0:T(4,128)(2,1)S(1)}, u32[]{:S(2)}, u32[]{:S(2)}) %collective-permute-start.1) | collective-permute-done | bytes 49184 | tf_op jit(solution)/shard_map/ppermute | solution.py:44
  11.5 1.6 %collective-permute-done.2 = bf16[4,6144]{1,0:T(4,128)(2,1)S(1)} collective-permute-done((bf16[4,6144]{1,0:T(4,128)(2,1)S(1)}, bf16[4,6144]{1,0:T(4,128)(2,1)S(1)}, u32[]{:S(2)}, u32[]{:S(2)}) %collective-permute-start.2) | collective-permute-done | bytes 49184 | tf_op jit(solution)/shard_map/ppermute | solution.py:44
  13.5 0.4 collective-permute-start.11
  14.0 2.3 %collective-permute-start.12 = (bf16[112,4096]{1,0:T(8,128)(2,1)S(1)}, bf16[112,4096]{1,0:T(8,128)(2,1)S(1)}, u32[]{:S(2)}, u32[]{:S(2)}) collective-permute-start(bf16[112,4096]{1,0:T(8,128)(2,1)S(1)} %get-tuple-element.71), channel_id=1, source_target_pairs={{0,67},{1,66},{2,1},{3,0},{64,3},{65,2},{66,65},{67,64},{4,71},{5,... | collective-permute-start | bytes 2752520 | tf_op jit(solution)/shard_map/ppermute | solution.py:40
  16.3 4.1 %collective-permute-start.5 = (bf16[16,4608]{1,0:T(8,128)(2,1)S(1)}, bf16[16,4608]{1,0:T(8,128)(2,1)S(1)}, u32[]{:S(2)}, u32[]{:S(2)}) collective-permute-start(bf16[16,4608]{1,0:T(8,128)(2,1)S(1)} %get-tuple-element.91), channel_id=1, source_target_pairs={{0,48},{1,13},{4,52},{5,1},{8,56},{9,5},{12,60},{13,9},{16,0},{17,... | collective-permute-start | bytes 442376 | tf_op jit(solution)/shard_map/ppermute | solution.py:55
  20.4 1.9 %collective-permute-start.4 = (bf16[16,4608]{1,0:T(8,128)(2,1)S(1)}, bf16[16,4608]{1,0:T(8,128)(2,1)S(1)}, u32[]{:S(2)}, u32[]{:S(2)}) collective-permute-start(bf16[16,4608]{1,0:T(8,128)(2,1)S(1)} %get-tuple-element.93), channel_id=1, source_target_pairs={{0,32},{1,9},{4,36},{5,13},{8,40},{9,1},{12,44},{13,5},{16,48},{17... | collective-permute-start | bytes 442376 | tf_op jit(solution)/shard_map/ppermute | solution.py:55
  22.3 0.8 collective-permute-done.5.b3
  23.1 5.3 %collective-permute-done.3.b1 = bf16[16,4608]{1,0:T(8,128)(2,1)S(1)} collective-permute-done((bf16[16,4608]{1,0:T(8,128)(2,1)S(1)}, bf16[16,4608]{1,0:T(8,128)(2,1)S(1)}, u32[]{:S(2)}, u32[]{:S(2)}) %collective-permute-start.3) | collective-permute-done | bytes 147488 | tf_op jit(solution)/shard_map/ppermute | solution.py:55
  28.3 0.7 spread.1
  29.0 1.6 %collective-permute-start.8 = (bf16[64,4224]{1,0:T(8,128)(2,1)S(1)}, bf16[64,4224]{1,0:T(8,128)(2,1)S(1)}, u32[]{:S(2)}, u32[]{:S(2)}) collective-permute-start(bf16[64,4224]{1,0:T(8,128)(2,1)S(1)} %get-tuple-element.59), channel_id=1, source_target_pairs={{0,4},{1,17},{4,8},{5,21},{8,12},{9,25},{12,0},{13,29},{16,20},{17... | collective-permute-start | bytes 1622024 | tf_op jit(solution)/shard_map/ppermute | solution.py:55
  30.6 2.7 %collective-permute-start.9 = (bf16[64,4224]{1,0:T(8,128)(2,1)S(1)}, bf16[64,4224]{1,0:T(8,128)(2,1)S(1)}, u32[]{:S(2)}, u32[]{:S(2)}) collective-permute-start(bf16[64,4224]{1,0:T(8,128)(2,1)S(1)} %get-tuple-element.60), channel_id=1, source_target_pairs={{0,8},{1,33},{4,12},{5,37},{8,0},{9,41},{12,4},{13,45},{16,24},{17... | collective-permute-start | bytes 1622024 | tf_op jit(solution)/shard_map/ppermute | solution.py:55
  33.3 1.4 %collective-permute-start.10 = (bf16[64,4224]{1,0:T(8,128)(2,1)S(1)}, bf16[64,4224]{1,0:T(8,128)(2,1)S(1)}, u32[]{:S(2)}, u32[]{:S(2)}) collective-permute-start(bf16[64,4224]{1,0:T(8,128)(2,1)S(1)} %get-tuple-element.61), channel_id=1, source_target_pairs={{0,12},{1,49},{4,0},{5,53},{8,4},{9,57},{12,8},{13,61},{16,28},{17... | collective-permute-start | bytes 1622024 | tf_op jit(solution)/shard_map/ppermute | solution.py:55
  34.9 3.7 %load_lower.1.weights = bf16[640,7168]{1,0:T(8,128)(2,1)S(1)} custom-call(bf16[320,7168]{1,0:T(8,128)(2,1)} %first, bf16[320,7168]{1,0:T(8,128)(2,1)} %collective-permute-done.7.second), custom_call_target="tpu_custom_call" | custom-call | bytes 18350080 | tf_op jit(solution)/shard_map/load_lower/pallas_call | solution.py:367
  38.7 1.0 collective-permute-done.8.r1
  39.7 6.8 %collective-permute-done.9.r2 = bf16[64,4224]{1,0:T(8,128)(2,1)S(1)} collective-permute-done((bf16[64,4224]{1,0:T(8,128)(2,1)S(1)}, bf16[64,4224]{1,0:T(8,128)(2,1)S(1)}, u32[]{:S(2)}, u32[]{:S(2)}) %collective-permute-start.9) | collective-permute-done | bytes 540704 | tf_op jit(solution)/shard_map/ppermute | solution.py:55
  46.4 2.9 %project.1 = (f32[112,256]{1,0:T(8,128)S(1)}, bf16[112,256]{1,0:T(8,128)(2,1)S(1)}, bf16[112,256]{1,0:T(8,128)(2,1)S(1)}, bf16[112,256]{1,0:T(8,128)(2,1)S(1)}, bf16[256,128]{1,0:T(8,128)(2,1)S(1)}) custom-call(s32[4]{0:T(128)S(1)} %pad_add_fusion.place, bf16[64,4224]{1,0:T(8,128)(2,1)S(1)} %get-tuple-element.65.r0, ...), custom_call_target="tpu_custom_call" | custom-call | tf_op jit(solution)/shard_map/project/pallas_call | solution.py:286
  49.7 1.6 %collective-permute-start.15 = (bf16[112,256]{1,0:T(8,128)(2,1)S(1)}, bf16[112,256]{1,0:T(8,128)(2,1)S(1)}, u32[]{:S(2)}, u32[]{:S(2)}) collective-permute-start(bf16[112,256]{1,0:T(8,128)(2,1)S(1)} %get-tuple-element.75), channel_id=1, source_target_pairs={{0,3},{1,2},{2,1},{3,0},{4,7},{5,6},{6,5},{7,4},{8,11},{9,10},{10,... | collective-permute-start | bytes 172040 | tf_op jit(solution)/shard_map/ppermute | solution.py:44
  51.3 2.9 %collective-permute-done.14.r2 = bf16[112,256]{1,0:T(8,128)(2,1)S(1)} collective-permute-done((bf16[112,256]{1,0:T(8,128)(2,1)S(1)}, bf16[112,256]{1,0:T(8,128)(2,1)S(1)}, u32[]{:S(2)}, u32[]{:S(2)}) %collective-permute-start.14) | collective-permute-done | bytes 57376 | tf_op jit(solution)/shard_map/ppermute | solution.py:44
  54.3 0.3 collective-permute-done.15.r3
  54.6 1.1 mix.1
  55.6 34.4 %all_to_all.10.arrived = bf16[64,112,128]{2,1,0:T(8,128)(2,1)S(1)} all-to-all(bf16[64,112,128]{2,1,0:T(8,128)(2,1)S(1)} %mix.1), channel_id=1, replica_groups=mesh['g'=2,'z'=4,'x'=4,'y'=2,'c'=2] {'g','z','x','y'}, dimensions={0} | all-to-all | bytes 3670016 | tf_op jit(solution)/shard_map/all_to_all | solution.py:586
  90.0 5.6 %receive.1 = (bf16[7168,256]{1,0:T(8,128)(2,1)S(1)}, f32[8,256]{1,0:T(8,128)S(1)}, bf16[16,7168]{1,0:T(8,128)(2,1)S(1)}, bf16[16,7168]{1,0:T(8,128)(2,1)S(1)}, bf16[640,7168]{1,0:T(8,128)(2,1)S(1)}) custom-call(s32[4]{0:T(128)S(1)} %pad_add_fusion.place, bf16[64,112,128]{2,1,0:T(8,128)(2,1)S(1)} %all_to_all.10.arrived, f32[64,112]{1,0:T(8,128)S(1)} %chunked.1.gains, ...), custom_call_target="tpu_custom_call" | custom-call | tf_op jit(solution)/shard_map/receive/pallas_call | solution.py:427
  95.6 0.6 collective-permute-start.18
  96.2 3.9 %expert.1 = (bf16[128,320]{1,0:T(8,128)(2,1)S(1)}, bf16[128,320]{1,0:T(8,128)(2,1)S(1)}) custom-call(s32[4]{0:T(128)S(1)} %pad_add_fusion.place, bf16[7168,256]{1,0:T(8,128)(2,1)S(1)} %get-tuple-element.78.seen, bf16[64,112,128]{2,1,0:T(8,128)(2,1)S(1)} %collective-permute-done.16.other, f32[8,256]{1,0:T(8,128)S(1)} %get-tuple-element.79.own_squares, ...), custom_call_target="tpu_custom_call" | custom-call | tf_op jit(solution)/shard_map/expert/pallas_call | solution.py:469
  100.2 1.3 collective-permute-done.17.other
  101.5 3.2 %lower.1 = bf16[64,2,7168]{2,1,0:T(2,128)(2,1)S(1)} custom-call(s32[4]{0:T(128)S(1)} %pad_add_fusion.place, bf16[128,320]{1,0:T(8,128)(2,1)S(1)} %get-tuple-element.81.own, bf16[128,320]{1,0:T(8,128)(2,1)S(1)} %collective-permute-done.17.other, bf16[640,7168]{1,0:T(8,128)(2,1)S(1)} %load_lower.1.weights, bf16[16,7168]{1,0:T(8,128)(2,1)S(1)} %get-tuple-element.84.kept, ...), custom_call_target="tpu_custom_call" | custom-call | tf_op jit(solution)/shard_map/lower/pallas_call | solution.py:501
  104.7 32.4 %all_to_all.11.returned = bf16[64,2,7168]{2,1,0:T(2,128)(2,1)S(1)} all-to-all(bf16[64,2,7168]{2,1,0:T(2,128)(2,1)S(1)} %lower.1), channel_id=1, replica_groups=mesh['g'=2,'z'=4,'x'=4,'y'=2,'c'=2] {'g','z','x','y'}, dimensions={0} | all-to-all | bytes 3670016 | tf_op jit(solution)/shard_map/all_to_all | solution.py:594
  137.1 1.0 combine.1
  (28 shorter events, 1.2 us)
Async XLA Ops:
  0.0 13.5 %collective-permute-start.7 = (bf16[320,7168]{1,0:T(8,128)(2,1)}, bf16[320,7168]{1,0:T(8,128)(2,1)}, u32[]{:S(2)}, u32[]{:S(2)}) collective-permute-start(bf16[320,7168]{1,0:T(8,128)(2,1)} %first), channel_id=1, source_target_pairs={{0,1},{1,0},{2,3},{3,2},{4,5},{5,4},{6,7},{7,6},{8,9},{9,8},{10,11... | collective-permute-start | bytes 13762568 | tf_op jit(solution)/shard_map/ppermute | solution.py:27
  0.1 34.7 %copy-start = (f32[7168]{0:T(1024)S(1)}, f32[7168]{0:T(1024)}, u32[]{:S(2)}) copy-start(f32[7168]{0:T(1024)} %param.22) | copy-start | bytes 86020
  6.9 2.7 %collective-permute-start = (bf16[4,6144]{1,0:T(4,128)(2,1)S(1)}, bf16[4,6144]{1,0:T(4,128)(2,1)S(1)}, u32[]{:S(2)}, u32[]{:S(2)}) collective-permute-start(bf16[4,6144]{1,0:T(4,128)(2,1)S(1)} %get-tuple-element.47), channel_id=1, source_target_pairs={{0,1},{1,0},{2,3},{3,2},{4,5},{5,4},{6,7},{7,6},{8,9},{9,8},{10,11... | collective-permute-start | bytes 147464 | tf_op jit(solution)/shard_map/ppermute | solution.py:44
  7.5 4.1 %collective-permute-start.1 = (bf16[4,6144]{1,0:T(4,128)(2,1)S(1)}, bf16[4,6144]{1,0:T(4,128)(2,1)S(1)}, u32[]{:S(2)}, u32[]{:S(2)}) collective-permute-start(bf16[4,6144]{1,0:T(4,128)(2,1)S(1)} %get-tuple-element.48), channel_id=1, source_target_pairs={{0,2},{1,3},{2,0},{3,1},{4,6},{5,7},{6,4},{7,5},{8,10},{9,11},{10,... | collective-permute-start | bytes 147464 | tf_op jit(solution)/shard_map/ppermute | solution.py:44
  9.1 4.0 %collective-permute-start.2 = (bf16[4,6144]{1,0:T(4,128)(2,1)S(1)}, bf16[4,6144]{1,0:T(4,128)(2,1)S(1)}, u32[]{:S(2)}, u32[]{:S(2)}) collective-permute-start(bf16[4,6144]{1,0:T(4,128)(2,1)S(1)} %get-tuple-element.49), channel_id=1, source_target_pairs={{0,3},{1,2},{2,1},{3,0},{4,7},{5,6},{6,5},{7,4},{8,11},{9,10},{10,... | collective-permute-start | bytes 147464 | tf_op jit(solution)/shard_map/ppermute | solution.py:44
  9.1 4.4 %collective-permute-start.6 = (bf16[112,4096]{1,0:T(8,128)(2,1)}, bf16[112,4096]{1,0:T(8,128)(2,1)S(1)}, u32[]{:S(2)}, u32[]{:S(2)}) collective-permute-start(bf16[112,4096]{1,0:T(8,128)(2,1)} %get-tuple-element.56), channel_id=1, source_target_pairs={{0,1},{1,0},{2,3},{3,2},{4,5},{5,4},{6,7},{7,6},{8,9},{9,8},{10,11... | collective-permute-start | bytes 2752520 | tf_op jit(solution)/shard_map/ppermute | solution.py:27
  13.5 32.9 %collective-permute-start.11 = (bf16[112,4096]{1,0:T(8,128)(2,1)S(1)}, bf16[112,4096]{1,0:T(8,128)(2,1)S(1)}, u32[]{:S(2)}, u32[]{:S(2)}) collective-permute-start(bf16[112,4096]{1,0:T(8,128)(2,1)S(1)} %get-tuple-element.70), channel_id=1, source_target_pairs={{0,2},{1,3},{2,64},{3,65},{64,66},{65,67},{66,0},{67,1},{4,6},{5,7... | collective-permute-start | bytes 2752520 | tf_op jit(solution)/shard_map/ppermute | solution.py:40
  14.0 32.5 %collective-permute-start.12 = (bf16[112,4096]{1,0:T(8,128)(2,1)S(1)}, bf16[112,4096]{1,0:T(8,128)(2,1)S(1)}, u32[]{:S(2)}, u32[]{:S(2)}) collective-permute-start(bf16[112,4096]{1,0:T(8,128)(2,1)S(1)} %get-tuple-element.71), channel_id=1, source_target_pairs={{0,67},{1,66},{2,1},{3,0},{64,3},{65,2},{66,65},{67,64},{4,71},{5,... | collective-permute-start | bytes 2752520 | tf_op jit(solution)/shard_map/ppermute | solution.py:40
  16.3 6.8 %collective-permute-start.5 = (bf16[16,4608]{1,0:T(8,128)(2,1)S(1)}, bf16[16,4608]{1,0:T(8,128)(2,1)S(1)}, u32[]{:S(2)}, u32[]{:S(2)}) collective-permute-start(bf16[16,4608]{1,0:T(8,128)(2,1)S(1)} %get-tuple-element.91), channel_id=1, source_target_pairs={{0,48},{1,13},{4,52},{5,1},{8,56},{9,5},{12,60},{13,9},{16,0},{17,... | collective-permute-start | bytes 442376 | tf_op jit(solution)/shard_map/ppermute | solution.py:55
  20.4 7.9 %collective-permute-start.3 = (bf16[16,4608]{1,0:T(8,128)(2,1)S(1)}, bf16[16,4608]{1,0:T(8,128)(2,1)S(1)}, u32[]{:S(2)}, u32[]{:S(2)}) collective-permute-start(bf16[16,4608]{1,0:T(8,128)(2,1)S(1)} %get-tuple-element.92), channel_id=1, source_target_pairs={{0,16},{1,5},{4,20},{5,9},{8,24},{9,13},{12,28},{13,1},{16,32},{17... | collective-permute-start | bytes 442376 | tf_op jit(solution)/shard_map/ppermute | solution.py:55
  20.4 7.9 %collective-permute-start.4 = (bf16[16,4608]{1,0:T(8,128)(2,1)S(1)}, bf16[16,4608]{1,0:T(8,128)(2,1)S(1)}, u32[]{:S(2)}, u32[]{:S(2)}) collective-permute-start(bf16[16,4608]{1,0:T(8,128)(2,1)S(1)} %get-tuple-element.93), channel_id=1, source_target_pairs={{0,32},{1,9},{4,36},{5,13},{8,40},{9,1},{12,44},{13,5},{16,48},{17... | collective-permute-start | bytes 442376 | tf_op jit(solution)/shard_map/ppermute | solution.py:55
  29.0 10.6 %collective-permute-start.8 = (bf16[64,4224]{1,0:T(8,128)(2,1)S(1)}, bf16[64,4224]{1,0:T(8,128)(2,1)S(1)}, u32[]{:S(2)}, u32[]{:S(2)}) collective-permute-start(bf16[64,4224]{1,0:T(8,128)(2,1)S(1)} %get-tuple-element.59), channel_id=1, source_target_pairs={{0,4},{1,17},{4,8},{5,21},{8,12},{9,25},{12,0},{13,29},{16,20},{17... | collective-permute-start | bytes 1622024 | tf_op jit(solution)/shard_map/ppermute | solution.py:55
  30.6 15.9 %collective-permute-start.9 = (bf16[64,4224]{1,0:T(8,128)(2,1)S(1)}, bf16[64,4224]{1,0:T(8,128)(2,1)S(1)}, u32[]{:S(2)}, u32[]{:S(2)}) collective-permute-start(bf16[64,4224]{1,0:T(8,128)(2,1)S(1)} %get-tuple-element.60), channel_id=1, source_target_pairs={{0,8},{1,33},{4,12},{5,37},{8,0},{9,41},{12,4},{13,45},{16,24},{17... | collective-permute-start | bytes 1622024 | tf_op jit(solution)/shard_map/ppermute | solution.py:55
  33.3 13.1 %collective-permute-start.10 = (bf16[64,4224]{1,0:T(8,128)(2,1)S(1)}, bf16[64,4224]{1,0:T(8,128)(2,1)S(1)}, u32[]{:S(2)}, u32[]{:S(2)}) collective-permute-start(bf16[64,4224]{1,0:T(8,128)(2,1)S(1)} %get-tuple-element.61), channel_id=1, source_target_pairs={{0,12},{1,49},{4,0},{5,53},{8,4},{9,57},{12,8},{13,61},{16,28},{17... | collective-permute-start | bytes 1622024 | tf_op jit(solution)/shard_map/ppermute | solution.py:55
  49.4 2.0 %collective-permute-start.13 = (bf16[112,256]{1,0:T(8,128)(2,1)S(1)}, bf16[112,256]{1,0:T(8,128)(2,1)S(1)}, u32[]{:S(2)}, u32[]{:S(2)}) collective-permute-start(bf16[112,256]{1,0:T(8,128)(2,1)S(1)} %get-tuple-element.73), channel_id=1, source_target_pairs={{0,1},{1,0},{2,3},{3,2},{4,5},{5,4},{6,7},{7,6},{8,9},{9,8},{10,11... | collective-permute-start | bytes 172040 | tf_op jit(solution)/shard_map/ppermute | solution.py:44
  49.5 4.8 %collective-permute-start.14 = (bf16[112,256]{1,0:T(8,128)(2,1)S(1)}, bf16[112,256]{1,0:T(8,128)(2,1)S(1)}, u32[]{:S(2)}, u32[]{:S(2)}) collective-permute-start(bf16[112,256]{1,0:T(8,128)(2,1)S(1)} %get-tuple-element.74), channel_id=1, source_target_pairs={{0,2},{1,3},{2,0},{3,1},{4,6},{5,7},{6,4},{7,5},{8,10},{9,11},{10,... | collective-permute-start | bytes 172040 | tf_op jit(solution)/shard_map/ppermute | solution.py:44
  49.7 4.8 %collective-permute-start.15 = (bf16[112,256]{1,0:T(8,128)(2,1)S(1)}, bf16[112,256]{1,0:T(8,128)(2,1)S(1)}, u32[]{:S(2)}, u32[]{:S(2)}) collective-permute-start(bf16[112,256]{1,0:T(8,128)(2,1)S(1)} %get-tuple-element.75), channel_id=1, source_target_pairs={{0,3},{1,2},{2,1},{3,0},{4,7},{5,6},{6,5},{7,4},{8,11},{9,10},{10,... | collective-permute-start | bytes 172040 | tf_op jit(solution)/shard_map/ppermute | solution.py:44
  90.0 6.2 %collective-permute-start.16 = (bf16[64,112,128]{2,1,0:T(8,128)(2,1)S(1)}, bf16[64,112,128]{2,1,0:T(8,128)(2,1)S(1)}, u32[]{:S(2)}, u32[]{:S(2)}) collective-permute-start(bf16[64,112,128]{2,1,0:T(8,128)(2,1)S(1)} %all_to_all.10.arrived), channel_id=1, source_target_pairs={{0,1},{1,0},{2,3},{3,2},{4,5},{5,4},{6,7},{7,6},{8,9},{9,8},{10,11... | collective-permute-start | bytes 5505032 | tf_op jit(solution)/shard_map/ppermute | solution.py:27
  95.6 4.6 %collective-permute-start.18 = (bf16[16,7168]{1,0:T(8,128)(2,1)S(1)}, bf16[16,7168]{1,0:T(8,128)(2,1)S(1)}, u32[]{:S(2)}, u32[]{:S(2)}) collective-permute-start(bf16[16,7168]{1,0:T(8,128)(2,1)S(1)} %get-tuple-element.85), channel_id=1, source_target_pairs={{0,1},{1,0},{2,3},{3,2},{4,5},{5,4},{6,7},{7,6},{8,9},{9,8},{10,11... | collective-permute-start | bytes 688136 | tf_op jit(solution)/shard_map/ppermute | solution.py:27
  100.1 1.4 collective-permute-start.17

commit v5 on v4

--- a/solution.py
+++ b/solution.py
@@ -253,18 +253,30 @@
     )(place, *blocks)
 
 
+def own_kernel(place, turned, out, sem):
+    y, c = place[2], place[3]
+    quarter = pl.ds(pl.multiple_of(c * KHALF + y * KQ, KQ), KQ)
+    copy = pltpu.make_async_copy(turned.at[:, quarter], out, sem.at[0])
+    copy.start()
+    copy.wait()
+
+
+def own_quarter(place, turned):
+    return pl.pallas_call(
+        own_kernel,
+        out_shape=jax.ShapeDtypeStruct((COLS, KQ), BF),
+        in_specs=[SMEM, HBM],
+        out_specs=VMEM,
+        scratch_shapes=[pltpu.SemaphoreType.DMA((1,))],
+        compiler_params=pltpu.CompilerParams(vmem_limit_bytes=4 << 20),
+        name="own_quarter",
+    )(place, in_hbm(turned))
+
+
 def project_kernel(
-    place, r0, r1, r2, r3, own, other, far, far_other, kept, s1, s2, s3, tail, w, rows, sems
+    place, r0, r1, r2, r3, own, other, far, far_other, kept, s1, s2, s3, tail, rows
 ):
-    z, x, y, c = place[0], place[1], place[2], place[3]
-    quarter = lambda start: pl.ds(pl.multiple_of(start, KQ), KQ)
-    sources = (own.at[:, quarter(c * KHALF + y * KQ)], other, far, far_other)
-    copies = [
-        pltpu.make_async_copy(source, w.at[pl.ds(n * COLS, COLS), :], sems.at[n])
-        for n, source in enumerate(sources)
-    ]
-    for copy in copies:
-        copy.start()
+    z, x, c = place[0], place[1], place[3]
     for k, block in enumerate((r0, r1, r2, r3)):
         for i in range(4):
             of_z = (z - jnp.where(c == 0, i, k) + 4) % 4
@@ -272,10 +284,9 @@
             row = at16(of_z * 64 + of_x * 16)
             rows[pl.ds(row, 16), :] = block[16 * i : 16 * i + 16, :KQ]
             tail[pl.ds(row, 16), :] = block[16 * i : 16 * i + 16, KQ:]
-    for copy in copies:
-        copy.wait()
+    weights = jnp.concatenate([own[...], other[...], far[...], far_other[...]], axis=0)
     product = lax.dot_general(
-        w[...], rows[...], (((1,), (1,)), ((), ())), preferred_element_type=F32
+        weights, rows[...], (((1,), (1,)), ((), ())), preferred_element_type=F32
     )
     kept[...] = product[:COLS]
     for i, sent in enumerate((s1, s2, s3)):
@@ -290,16 +301,14 @@
             *(jax.ShapeDtypeStruct((COLS, 256), BF),) * 3,
             jax.ShapeDtypeStruct((256, 128), BF),
         ),
-        in_specs=[SMEM] + [VMEM] * 4 + [HBM] + [pl.BlockSpec(memory_space=pl.ANY)] * 3,
+        in_specs=[SMEM] + [VMEM] * 8,
         out_specs=(VMEM,) * 5,
         scratch_shapes=[
-            pltpu.VMEM((4 * COLS, KQ), BF),
             pltpu.VMEM((256, KQ), BF),
-            pltpu.SemaphoreType.DMA((4,)),
         ],
         compiler_params=pltpu.CompilerParams(vmem_limit_bytes=12 << 20),
         name="project",
-    )(place, *blocks, in_hbm(own), other, *fars)
+    )(place, *blocks, own, other, *fars)
 
 
 def chunk_kernel(gain, out):
@@ -571,15 +580,18 @@
 
     blocks = [with_tail(0)] + [crossed(with_tail(k), 0, k) for k in (1, 2, 3)]
     blocks, ffn_gain, ready = lax.optimization_barrier(
-        (spread(place, blocks), ffn_gain, (down_weight, other_down))
-    )
-    lower_weights = load(*ready, "load_lower")
+        (spread(place, blocks), ffn_gain, (down_weight, other_down, turned))
+    )
+    lower_weights = load(*ready[:2], "load_lower")
+    own = own_quarter(place, ready[2])
     ffn_gain = ffn_gain.reshape(1, D)
     gains = chunked(ffn_gain)
     blocks = [blocks[0]] + [crossed(blocks[k], 1, k) for k in (1, 2, 3)]
-    blocks, gains, lower_weights = lax.optimization_barrier((blocks, gains, lower_weights))
+    blocks, gains, lower_weights, own = lax.optimization_barrier(
+        (blocks, gains, lower_weights, own)
+    )
     kept, *sent, tail = project(
-        place, blocks, turned, near, (far, far_other)
+        place, blocks, own, near, (far, far_other)
     )
     taken = [around(sent[k - 1], k) for k in (1, 2, 3)]
     dispatched = mix(place, kept, taken, gains, tail)

time: 138 us -> 137 us (level)
  waiting for transfers between devices: 21.8 us -> 20.1 us
    ppermute x6, waiting for transfers between devices: 13.8 us -> 12.1 us  [crossed(): return lax.ppermute(array, ('z', 'x', 'c'), pairs)]
    pallas_call x0 -> x1, Pallas kernels: none -> 1.73 us  [own_quarter(): pl.pallas_call(own_kernel, out_shape=jax.ShapeDtypeStruct((COLS, KQ), BF)...]
  transfers between devices with their start and end apart: 19 -> 19, of which waited for: 9 -> 8; matrix products, arithmetic and copies ran while one was open for 0% -> 0% of each run, Pallas kernels for 15% -> 16%
where the time goes in v5:
time: 137 us
  blocking collectives  66.8 us (49%)
  Pallas kernels  29.8 us (22%)
  waiting for transfers between devices  20.1 us (15%)
  starting transfers between devices  19.8 us (14%)
    all_to_all x1, blocking collectives, per_device(): arrived = lax.all_to_all(dispatched, ('g', 'z', 'x', 'y'), 0, 0, tiled=True)  34.4 us
    all_to_all x1, blocking collectives, per_device(): returned = lax.all_to_all(summed, ('g', 'z', 'x', 'y'), 0, 0, tiled=True)  32.4 us
    ppermute x6, waiting for transfers between devices, crossed(): return lax.ppermute(array, ('z', 'x', 'c'), pairs)  12.1 us
    ppermute x6, starting transfers between devices, crossed(): return lax.ppermute(array, ('z', 'x', 'c'), pairs)  11.7 us
    pallas_call x1, Pallas kernels, attend(): pl.pallas_call(attend_kernel, out_shape=(*(jax.ShapeDtypeStruct((rows, KQ...  6.78 us
    ppermute x6, waiting for transfers between devices, around(): return lax.ppermute(array, ('y', 'c'), [(i, i ^ k) for i in range(4)])  6.7 us
    pallas_call x1, Pallas kernels, receive(): pl.pallas_call(receive_kernel, out_shape=(jax.ShapeDtypeStruct((D, 256),...  5.57 us
    ppermute x6, starting transfers between devices, around(): return lax.ppermute(array, ('y', 'c'), [(i, i ^ k) for i in range(4)])  4.19 us
  transfers between devices with their start and end apart: 19, of which 8 were waited for; matrix products, arithmetic and copies ran while one was open for 0% of the time, Pallas kernels for 16%

profile of v5, /device:TPU:0, one launch (start us, length us, event | category | flops | bytes accessed | tf_op | source)
XLA Modules:
  0.0 137.1 jit_solution(2404349105699218542)
XLA Ops:
  0.1 6.8 %attend.1 = (bf16[4,6144]{1,0:T(4,128)(2,1)S(1)}, bf16[4,6144]{1,0:T(4,128)(2,1)S(1)}, bf16[4,6144]{1,0:T(4,128)(2,1)S(1)}, bf16[4,6144]{1,0:T(4,128)(2,1)S(1)},...) custom-call(s32[4]{0:T(128)} %lengths.1, ...), custom_call_target="tpu_custom_call" | custom-call | flops 536870912 | bytes 8388608 | tf_op jit(solution)/shard_map/attend/pallas_call | solution.py:189
  6.9 0.6 collective-permute-start
  7.5 1.7 %collective-permute-start.1 = (bf16[4,6144]{1,0:T(4,128)(2,1)S(1)}, bf16[4,6144]{1,0:T(4,128)(2,1)S(1)}, u32[]{:S(2)}, u32[]{:S(2)}) collective-permute-start(bf16[4,6144]{1,0:T(4,128)(2,1)S(1)} %get-tuple-element.50), channel_id=1, source_target_pairs={{0,2},{1,3},{2,0},{3,1},{4,6},{5,7},{6,4},{7,5},{8,10},{9,11},{10,... | collective-permute-start | bytes 147464 | tf_op jit(solution)/shard_map/ppermute | solution.py:44
  9.1 0.5 collective-permute-start.6
  9.7 1.9 %collective-permute-done.1 = bf16[4,6144]{1,0:T(4,128)(2,1)S(1)} collective-permute-done((bf16[4,6144]{1,0:T(4,128)(2,1)S(1)}, bf16[4,6144]{1,0:T(4,128)(2,1)S(1)}, u32[]{:S(2)}, u32[]{:S(2)}) %collective-permute-start.1) | collective-permute-done | bytes 49184 | tf_op jit(solution)/shard_map/ppermute | solution.py:44
  11.5 1.6 %collective-permute-done.2 = bf16[4,6144]{1,0:T(4,128)(2,1)S(1)} collective-permute-done((bf16[4,6144]{1,0:T(4,128)(2,1)S(1)}, bf16[4,6144]{1,0:T(4,128)(2,1)S(1)}, u32[]{:S(2)}, u32[]{:S(2)}) %collective-permute-start.2) | collective-permute-done | bytes 49184 | tf_op jit(solution)/shard_map/ppermute | solution.py:44
  13.5 0.4 collective-permute-start.11
  14.0 2.3 %collective-permute-start.12 = (bf16[112,4096]{1,0:T(8,128)(2,1)S(1)}, bf16[112,4096]{1,0:T(8,128)(2,1)S(1)}, u32[]{:S(2)}, u32[]{:S(2)}) collective-permute-start(bf16[112,4096]{1,0:T(8,128)(2,1)S(1)} %get-tuple-element.75), channel_id=1, source_target_pairs={{0,67},{1,66},{2,1},{3,0},{64,3},{65,2},{66,65},{67,64},{4,71},{5,... | collective-permute-start | bytes 2752520 | tf_op jit(solution)/shard_map/ppermute | solution.py:40
  16.3 4.1 %collective-permute-start.5 = (bf16[16,4608]{1,0:T(8,128)(2,1)S(1)}, bf16[16,4608]{1,0:T(8,128)(2,1)S(1)}, u32[]{:S(2)}, u32[]{:S(2)}) collective-permute-start(bf16[16,4608]{1,0:T(8,128)(2,1)S(1)} %get-tuple-element.95), channel_id=1, source_target_pairs={{0,48},{1,13},{4,52},{5,1},{8,56},{9,5},{12,60},{13,9},{16,0},{17,... | collective-permute-start | bytes 442376 | tf_op jit(solution)/shard_map/ppermute | solution.py:55
  20.4 1.9 %collective-permute-start.4 = (bf16[16,4608]{1,0:T(8,128)(2,1)S(1)}, bf16[16,4608]{1,0:T(8,128)(2,1)S(1)}, u32[]{:S(2)}, u32[]{:S(2)}) collective-permute-start(bf16[16,4608]{1,0:T(8,128)(2,1)S(1)} %get-tuple-element.97), channel_id=1, source_target_pairs={{0,32},{1,9},{4,36},{5,13},{8,40},{9,1},{12,44},{13,5},{16,48},{17... | collective-permute-start | bytes 442376 | tf_op jit(solution)/shard_map/ppermute | solution.py:55
  22.3 0.8 collective-permute-done.5.b3
  23.1 5.3 %collective-permute-done.3.b1 = bf16[16,4608]{1,0:T(8,128)(2,1)S(1)} collective-permute-done((bf16[16,4608]{1,0:T(8,128)(2,1)S(1)}, bf16[16,4608]{1,0:T(8,128)(2,1)S(1)}, u32[]{:S(2)}, u32[]{:S(2)}) %collective-permute-start.3) | collective-permute-done | bytes 147488 | tf_op jit(solution)/shard_map/ppermute | solution.py:55
  28.3 0.7 spread.1
  29.0 1.6 %collective-permute-start.8 = (bf16[64,4224]{1,0:T(8,128)(2,1)S(1)}, bf16[64,4224]{1,0:T(8,128)(2,1)S(1)}, u32[]{:S(2)}, u32[]{:S(2)}) collective-permute-start(bf16[64,4224]{1,0:T(8,128)(2,1)S(1)} %get-tuple-element.61), channel_id=1, source_target_pairs={{0,4},{1,17},{4,8},{5,21},{8,12},{9,25},{12,0},{13,29},{16,20},{17... | collective-permute-start | bytes 1622024 | tf_op jit(solution)/shard_map/ppermute | solution.py:55
  30.6 2.7 %collective-permute-start.9 = (bf16[64,4224]{1,0:T(8,128)(2,1)S(1)}, bf16[64,4224]{1,0:T(8,128)(2,1)S(1)}, u32[]{:S(2)}, u32[]{:S(2)}) collective-permute-start(bf16[64,4224]{1,0:T(8,128)(2,1)S(1)} %get-tuple-element.62), channel_id=1, source_target_pairs={{0,8},{1,33},{4,12},{5,37},{8,0},{9,41},{12,4},{13,45},{16,24},{17... | collective-permute-start | bytes 1622024 | tf_op jit(solution)/shard_map/ppermute | solution.py:55
  33.3 1.4 %collective-permute-start.10 = (bf16[64,4224]{1,0:T(8,128)(2,1)S(1)}, bf16[64,4224]{1,0:T(8,128)(2,1)S(1)}, u32[]{:S(2)}, u32[]{:S(2)}) collective-permute-start(bf16[64,4224]{1,0:T(8,128)(2,1)S(1)} %get-tuple-element.63), channel_id=1, source_target_pairs={{0,12},{1,49},{4,0},{5,53},{8,4},{9,57},{12,8},{13,61},{16,28},{17... | collective-permute-start | bytes 1622024 | tf_op jit(solution)/shard_map/ppermute | solution.py:55
  34.9 1.7 %own_quarter.1.own = bf16[112,4096]{1,0:T(8,128)(2,1)S(1)} custom-call(s32[4]{0:T(128)S(1)} %pad_add_fusion.place, bf16[112,16384]{1,0:T(8,128)(2,1)} %bitcast.16), custom_call_target="tpu_custom_call" | custom-call | tf_op jit(solution)/shard_map/own_quarter/pallas_call | solution.py:265
  36.7 3.7 %load_lower.1.weights = bf16[640,7168]{1,0:T(8,128)(2,1)S(1)} custom-call(bf16[320,7168]{1,0:T(8,128)(2,1)} %first, bf16[320,7168]{1,0:T(8,128)(2,1)} %collective-permute-done.7.second), custom_call_target="tpu_custom_call" | custom-call | bytes 18350080 | tf_op jit(solution)/shard_map/load_lower/pallas_call | solution.py:376
  40.4 6.0 %collective-permute-done.9.r2 = bf16[64,4224]{1,0:T(8,128)(2,1)S(1)} collective-permute-done((bf16[64,4224]{1,0:T(8,128)(2,1)S(1)}, bf16[64,4224]{1,0:T(8,128)(2,1)S(1)}, u32[]{:S(2)}, u32[]{:S(2)}) %collective-permute-start.9) | collective-permute-done | bytes 540704 | tf_op jit(solution)/shard_map/ppermute | solution.py:55
  46.4 1.9 %project.1 = (f32[112,256]{1,0:T(8,128)S(1)}, bf16[112,256]{1,0:T(8,128)(2,1)S(1)}, bf16[112,256]{1,0:T(8,128)(2,1)S(1)}, bf16[112,256]{1,0:T(8,128)(2,1)S(1)}, bf16[256,128]{1,0:T(8,128)(2,1)S(1)}) custom-call(s32[4]{0:T(128)S(1)} %pad_add_fusion.place, bf16[64,4224]{1,0:T(8,128)(2,1)S(1)} %get-tuple-element.68.r0, ...), custom_call_target="tpu_custom_call" | custom-call | tf_op jit(solution)/shard_map/project/pallas_call | solution.py:297
  48.7 1.6 %collective-permute-start.15 = (bf16[112,256]{1,0:T(8,128)(2,1)S(1)}, bf16[112,256]{1,0:T(8,128)(2,1)S(1)}, u32[]{:S(2)}, u32[]{:S(2)}) collective-permute-start(bf16[112,256]{1,0:T(8,128)(2,1)S(1)} %get-tuple-element.79), channel_id=1, source_target_pairs={{0,3},{1,2},{2,1},{3,0},{4,7},{5,6},{6,5},{7,4},{8,11},{9,10},{10,... | collective-permute-start | bytes 172040 | tf_op jit(solution)/shard_map/ppermute | solution.py:44
  50.3 2.9 %collective-permute-done.14.r2 = bf16[112,256]{1,0:T(8,128)(2,1)S(1)} collective-permute-done((bf16[112,256]{1,0:T(8,128)(2,1)S(1)}, bf16[112,256]{1,0:T(8,128)(2,1)S(1)}, u32[]{:S(2)}, u32[]{:S(2)}) %collective-permute-start.14) | collective-permute-done | bytes 57376 | tf_op jit(solution)/shard_map/ppermute | solution.py:44
  53.2 0.3 collective-permute-done.15.r3
  53.5 1.1 mix.1
  54.6 34.4 %all_to_all.10.arrived = bf16[64,112,128]{2,1,0:T(8,128)(2,1)S(1)} all-to-all(bf16[64,112,128]{2,1,0:T(8,128)(2,1)S(1)} %mix.1), channel_id=1, replica_groups=mesh['g'=2,'z'=4,'x'=4,'y'=2,'c'=2] {'g','z','x','y'}, dimensions={0} | all-to-all | bytes 3670016 | tf_op jit(solution)/shard_map/all_to_all | solution.py:598
  89.0 5.6 %receive.1 = (bf16[7168,256]{1,0:T(8,128)(2,1)S(1)}, f32[8,256]{1,0:T(8,128)S(1)}, bf16[16,7168]{1,0:T(8,128)(2,1)S(1)}, bf16[16,7168]{1,0:T(8,128)(2,1)S(1)}, bf16[640,7168]{1,0:T(8,128)(2,1)S(1)}) custom-call(s32[4]{0:T(128)S(1)} %pad_add_fusion.place, bf16[64,112,128]{2,1,0:T(8,128)(2,1)S(1)} %all_to_all.10.arrived, f32[64,112]{1,0:T(8,128)S(1)} %chunked.1.gains, ...), custom_call_target="tpu_custom_call" | custom-call | tf_op jit(solution)/shard_map/receive/pallas_call | solution.py:436
  94.5 0.6 collective-permute-start.18
  95.1 3.9 %expert.1 = (bf16[128,320]{1,0:T(8,128)(2,1)S(1)}, bf16[128,320]{1,0:T(8,128)(2,1)S(1)}) custom-call(s32[4]{0:T(128)S(1)} %pad_add_fusion.place, bf16[7168,256]{1,0:T(8,128)(2,1)S(1)} %get-tuple-element.82.seen, bf16[64,112,128]{2,1,0:T(8,128)(2,1)S(1)} %collective-permute-done.16.other, f32[8,256]{1,0:T(8,128)S(1)} %get-tuple-element.83.own_squares, ...), custom_call_target="tpu_custom_call" | custom-call | tf_op jit(solution)/shard_map/expert/pallas_call | solution.py:478
  99.2 1.3 collective-permute-done.17.other
  100.5 3.2 %lower.1 = bf16[64,2,7168]{2,1,0:T(2,128)(2,1)S(1)} custom-call(s32[4]{0:T(128)S(1)} %pad_add_fusion.place, bf16[128,320]{1,0:T(8,128)(2,1)S(1)} %get-tuple-element.85.own, bf16[128,320]{1,0:T(8,128)(2,1)S(1)} %collective-permute-done.17.other, bf16[640,7168]{1,0:T(8,128)(2,1)S(1)} %load_lower.1.weights, bf16[16,7168]{1,0:T(8,128)(2,1)S(1)} %get-tuple-element.88.kept, ...), custom_call_target="tpu_custom_call" | custom-call | tf_op jit(solution)/shard_map/lower/pallas_call | solution.py:510
  103.7 32.4 %all_to_all.11.returned = bf16[64,2,7168]{2,1,0:T(2,128)(2,1)S(1)} all-to-all(bf16[64,2,7168]{2,1,0:T(2,128)(2,1)S(1)} %lower.1), channel_id=1, replica_groups=mesh['g'=2,'z'=4,'x'=4,'y'=2,'c'=2] {'g','z','x','y'}, dimensions={0} | all-to-all | bytes 3670016 | tf_op jit(solution)/shard_map/all_to_all | solution.py:606
  136.1 1.0 combine.1
  (29 shorter events, 1.2 us)
Async XLA Ops:
  0.0 13.5 %collective-permute-start.7 = (bf16[320,7168]{1,0:T(8,128)(2,1)}, bf16[320,7168]{1,0:T(8,128)(2,1)}, u32[]{:S(2)}, u32[]{:S(2)}) collective-permute-start(bf16[320,7168]{1,0:T(8,128)(2,1)} %first), channel_id=1, source_target_pairs={{0,1},{1,0},{2,3},{3,2},{4,5},{5,4},{6,7},{7,6},{8,9},{9,8},{10,11... | collective-permute-start | bytes 13762568 | tf_op jit(solution)/shard_map/ppermute | solution.py:27
  0.1 34.7 %copy-start = (f32[7168]{0:T(1024)S(1)}, f32[7168]{0:T(1024)}, u32[]{:S(2)}) copy-start(f32[7168]{0:T(1024)} %param.22) | copy-start | bytes 86020
  6.9 2.7 %collective-permute-start = (bf16[4,6144]{1,0:T(4,128)(2,1)S(1)}, bf16[4,6144]{1,0:T(4,128)(2,1)S(1)}, u32[]{:S(2)}, u32[]{:S(2)}) collective-permute-start(bf16[4,6144]{1,0:T(4,128)(2,1)S(1)} %get-tuple-element.49), channel_id=1, source_target_pairs={{0,1},{1,0},{2,3},{3,2},{4,5},{5,4},{6,7},{7,6},{8,9},{9,8},{10,11... | collective-permute-start | bytes 147464 | tf_op jit(solution)/shard_map/ppermute | solution.py:44
  7.5 4.1 %collective-permute-start.1 = (bf16[4,6144]{1,0:T(4,128)(2,1)S(1)}, bf16[4,6144]{1,0:T(4,128)(2,1)S(1)}, u32[]{:S(2)}, u32[]{:S(2)}) collective-permute-start(bf16[4,6144]{1,0:T(4,128)(2,1)S(1)} %get-tuple-element.50), channel_id=1, source_target_pairs={{0,2},{1,3},{2,0},{3,1},{4,6},{5,7},{6,4},{7,5},{8,10},{9,11},{10,... | collective-permute-start | bytes 147464 | tf_op jit(solution)/shard_map/ppermute | solution.py:44
  9.1 4.0 %collective-permute-start.2 = (bf16[4,6144]{1,0:T(4,128)(2,1)S(1)}, bf16[4,6144]{1,0:T(4,128)(2,1)S(1)}, u32[]{:S(2)}, u32[]{:S(2)}) collective-permute-start(bf16[4,6144]{1,0:T(4,128)(2,1)S(1)} %get-tuple-element.51), channel_id=1, source_target_pairs={{0,3},{1,2},{2,1},{3,0},{4,7},{5,6},{6,5},{7,4},{8,11},{9,10},{10,... | collective-permute-start | bytes 147464 | tf_op jit(solution)/shard_map/ppermute | solution.py:44
  9.1 4.4 %collective-permute-start.6 = (bf16[112,4096]{1,0:T(8,128)(2,1)}, bf16[112,4096]{1,0:T(8,128)(2,1)S(1)}, u32[]{:S(2)}, u32[]{:S(2)}) collective-permute-start(bf16[112,4096]{1,0:T(8,128)(2,1)} %get-tuple-element.58), channel_id=1, source_target_pairs={{0,1},{1,0},{2,3},{3,2},{4,5},{5,4},{6,7},{7,6},{8,9},{9,8},{10,11... | collective-permute-start | bytes 2752520 | tf_op jit(solution)/shard_map/ppermute | solution.py:27
  13.5 32.9 %collective-permute-start.11 = (bf16[112,4096]{1,0:T(8,128)(2,1)S(1)}, bf16[112,4096]{1,0:T(8,128)(2,1)S(1)}, u32[]{:S(2)}, u32[]{:S(2)}) collective-permute-start(bf16[112,4096]{1,0:T(8,128)(2,1)S(1)} %get-tuple-element.74), channel_id=1, source_target_pairs={{0,2},{1,3},{2,64},{3,65},{64,66},{65,67},{66,0},{67,1},{4,6},{5,7... | collective-permute-start | bytes 2752520 | tf_op jit(solution)/shard_map/ppermute | solution.py:40
  14.0 32.5 %collective-permute-start.12 = (bf16[112,4096]{1,0:T(8,128)(2,1)S(1)}, bf16[112,4096]{1,0:T(8,128)(2,1)S(1)}, u32[]{:S(2)}, u32[]{:S(2)}) collective-permute-start(bf16[112,4096]{1,0:T(8,128)(2,1)S(1)} %get-tuple-element.75), channel_id=1, source_target_pairs={{0,67},{1,66},{2,1},{3,0},{64,3},{65,2},{66,65},{67,64},{4,71},{5,... | collective-permute-start | bytes 2752520 | tf_op jit(solution)/shard_map/ppermute | solution.py:40
  16.3 6.8 %collective-permute-start.5 = (bf16[16,4608]{1,0:T(8,128)(2,1)S(1)}, bf16[16,4608]{1,0:T(8,128)(2,1)S(1)}, u32[]{:S(2)}, u32[]{:S(2)}) collective-permute-start(bf16[16,4608]{1,0:T(8,128)(2,1)S(1)} %get-tuple-element.95), channel_id=1, source_target_pairs={{0,48},{1,13},{4,52},{5,1},{8,56},{9,5},{12,60},{13,9},{16,0},{17,... | collective-permute-start | bytes 442376 | tf_op jit(solution)/shard_map/ppermute | solution.py:55
  20.4 7.9 %collective-permute-start.3 = (bf16[16,4608]{1,0:T(8,128)(2,1)S(1)}, bf16[16,4608]{1,0:T(8,128)(2,1)S(1)}, u32[]{:S(2)}, u32[]{:S(2)}) collective-permute-start(bf16[16,4608]{1,0:T(8,128)(2,1)S(1)} %get-tuple-element.96), channel_id=1, source_target_pairs={{0,16},{1,5},{4,20},{5,9},{8,24},{9,13},{12,28},{13,1},{16,32},{17... | collective-permute-start | bytes 442376 | tf_op jit(solution)/shard_map/ppermute | solution.py:55
  20.4 7.9 %collective-permute-start.4 = (bf16[16,4608]{1,0:T(8,128)(2,1)S(1)}, bf16[16,4608]{1,0:T(8,128)(2,1)S(1)}, u32[]{:S(2)}, u32[]{:S(2)}) collective-permute-start(bf16[16,4608]{1,0:T(8,128)(2,1)S(1)} %get-tuple-element.97), channel_id=1, source_target_pairs={{0,32},{1,9},{4,36},{5,13},{8,40},{9,1},{12,44},{13,5},{16,48},{17... | collective-permute-start | bytes 442376 | tf_op jit(solution)/shard_map/ppermute | solution.py:55
  29.0 11.4 %collective-permute-start.8 = (bf16[64,4224]{1,0:T(8,128)(2,1)S(1)}, bf16[64,4224]{1,0:T(8,128)(2,1)S(1)}, u32[]{:S(2)}, u32[]{:S(2)}) collective-permute-start(bf16[64,4224]{1,0:T(8,128)(2,1)S(1)} %get-tuple-element.61), channel_id=1, source_target_pairs={{0,4},{1,17},{4,8},{5,21},{8,12},{9,25},{12,0},{13,29},{16,20},{17... | collective-permute-start | bytes 1622024 | tf_op jit(solution)/shard_map/ppermute | solution.py:55
  30.6 15.9 %collective-permute-start.9 = (bf16[64,4224]{1,0:T(8,128)(2,1)S(1)}, bf16[64,4224]{1,0:T(8,128)(2,1)S(1)}, u32[]{:S(2)}, u32[]{:S(2)}) collective-permute-start(bf16[64,4224]{1,0:T(8,128)(2,1)S(1)} %get-tuple-element.62), channel_id=1, source_target_pairs={{0,8},{1,33},{4,12},{5,37},{8,0},{9,41},{12,4},{13,45},{16,24},{17... | collective-permute-start | bytes 1622024 | tf_op jit(solution)/shard_map/ppermute | solution.py:55
  33.3 13.1 %collective-permute-start.10 = (bf16[64,4224]{1,0:T(8,128)(2,1)S(1)}, bf16[64,4224]{1,0:T(8,128)(2,1)S(1)}, u32[]{:S(2)}, u32[]{:S(2)}) collective-permute-start(bf16[64,4224]{1,0:T(8,128)(2,1)S(1)} %get-tuple-element.63), channel_id=1, source_target_pairs={{0,12},{1,49},{4,0},{5,53},{8,4},{9,57},{12,8},{13,61},{16,28},{17... | collective-permute-start | bytes 1622024 | tf_op jit(solution)/shard_map/ppermute | solution.py:55
  48.3 2.0 %collective-permute-start.13 = (bf16[112,256]{1,0:T(8,128)(2,1)S(1)}, bf16[112,256]{1,0:T(8,128)(2,1)S(1)}, u32[]{:S(2)}, u32[]{:S(2)}) collective-permute-start(bf16[112,256]{1,0:T(8,128)(2,1)S(1)} %get-tuple-element.77), channel_id=1, source_target_pairs={{0,1},{1,0},{2,3},{3,2},{4,5},{5,4},{6,7},{7,6},{8,9},{9,8},{10,11... | collective-permute-start | bytes 172040 | tf_op jit(solution)/shard_map/ppermute | solution.py:44
  48.4 4.8 %collective-permute-start.14 = (bf16[112,256]{1,0:T(8,128)(2,1)S(1)}, bf16[112,256]{1,0:T(8,128)(2,1)S(1)}, u32[]{:S(2)}, u32[]{:S(2)}) collective-permute-start(bf16[112,256]{1,0:T(8,128)(2,1)S(1)} %get-tuple-element.78), channel_id=1, source_target_pairs={{0,2},{1,3},{2,0},{3,1},{4,6},{5,7},{6,4},{7,5},{8,10},{9,11},{10,... | collective-permute-start | bytes 172040 | tf_op jit(solution)/shard_map/ppermute | solution.py:44
  48.7 4.8 %collective-permute-start.15 = (bf16[112,256]{1,0:T(8,128)(2,1)S(1)}, bf16[112,256]{1,0:T(8,128)(2,1)S(1)}, u32[]{:S(2)}, u32[]{:S(2)}) collective-permute-start(bf16[112,256]{1,0:T(8,128)(2,1)S(1)} %get-tuple-element.79), channel_id=1, source_target_pairs={{0,3},{1,2},{2,1},{3,0},{4,7},{5,6},{6,5},{7,4},{8,11},{9,10},{10,... | collective-permute-start | bytes 172040 | tf_op jit(solution)/shard_map/ppermute | solution.py:44
  89.0 6.2 %collective-permute-start.16 = (bf16[64,112,128]{2,1,0:T(8,128)(2,1)S(1)}, bf16[64,112,128]{2,1,0:T(8,128)(2,1)S(1)}, u32[]{:S(2)}, u32[]{:S(2)}) collective-permute-start(bf16[64,112,128]{2,1,0:T(8,128)(2,1)S(1)} %all_to_all.10.arrived), channel_id=1, source_target_pairs={{0,1},{1,0},{2,3},{3,2},{4,5},{5,4},{6,7},{7,6},{8,9},{9,8},{10,11... | collective-permute-start | bytes 5505032 | tf_op jit(solution)/shard_map/ppermute | solution.py:27
  94.5 4.6 %collective-permute-start.18 = (bf16[16,7168]{1,0:T(8,128)(2,1)S(1)}, bf16[16,7168]{1,0:T(8,128)(2,1)S(1)}, u32[]{:S(2)}, u32[]{:S(2)}) collective-permute-start(bf16[16,7168]{1,0:T(8,128)(2,1)S(1)} %get-tuple-element.89), channel_id=1, source_target_pairs={{0,1},{1,0},{2,3},{3,2},{4,5},{5,4},{6,7},{7,6},{8,9},{9,8},{10,11... | collective-permute-start | bytes 688136 | tf_op jit(solution)/shard_map/ppermute | solution.py:27
  99.1 1.4 %collective-permute-start.17 = (bf16[128,320]{1,0:T(8,128)(2,1)S(1)}, bf16[128,320]{1,0:T(8,128)(2,1)S(1)}, u32[]{:S(2)}, u32[]{:S(2)}) collective-permute-start(bf16[128,320]{1,0:T(8,128)(2,1)S(1)} %get-tuple-element.86), channel_id=1, source_target_pairs={{0,1},{1,0},{2,3},{3,2},{4,5},{5,4},{6,7},{7,6},{8,9},{9,8},{10,11... | collective-permute-start | bytes 245768 | tf_op jit(solution)/shard_map/ppermute | solution.py:27

commit v6 on v5

--- a/solution.py
+++ b/solution.py
@@ -489,20 +489,19 @@
 def lower_kernel(place, own, other, weights, kept, taken, gain, out, act):
     x, y = place[1], place[2]
     act[:, :HID_DEV] = own[...]
-    act[:, HID_DEV:] = other[...]
-    row = lax.broadcasted_iota(jnp.int32, (128, 16), 0)
-    column = lax.broadcasted_iota(jnp.int32, (128, 16), 1)
+    act[:, HID_DEV : 2 * HID_DEV] = other[...]
+    row = lax.broadcasted_iota(jnp.int32, (128, 32), 0)
+    column = lax.broadcasted_iota(jnp.int32, (128, 32), 1) % 16
     here = (row // 2 % 8 == x * 2 + y) & (row // 16 * 2 + row % 2 == column)
-    place_in = jnp.where(here, 1.0, 0.0).astype(BF)
+    act[:, 2 * HID_DEV :] = jnp.where(here, 1.0, 0.0).astype(BF)
     width = D // 4
     for k in range(4):
         lanes = slice(k * width, (k + 1) * width)
-        part = jnp.dot(act[...], weights[:, lanes], preferred_element_type=F32)
         residual = (kept[:, lanes] + taken[:, lanes]).astype(F32) / gain[:, lanes]
         high = residual.astype(BF)
         low = (residual - high.astype(F32)).astype(BF)
-        part = part + jnp.dot(place_in, high, preferred_element_type=F32)
-        part = part + jnp.dot(place_in, low, preferred_element_type=F32)
+        depth = jnp.concatenate([weights[:, lanes], high, low], axis=0)
+        part = jnp.dot(act[...], depth, preferred_element_type=F32)
         out[:, :, lanes] = part.astype(BF).reshape(64, 2, width)
 
 
@@ -512,7 +511,7 @@
         out_shape=jax.ShapeDtypeStruct((64, 2, D), BF),
         in_specs=[SMEM] + [VMEM] * 6,
         out_specs=VMEM,
-        scratch_shapes=[pltpu.VMEM((128, 2 * HID_DEV), BF)],
+        scratch_shapes=[pltpu.VMEM((128, 2 * HID_DEV + 32), BF)],
         compiler_params=pltpu.CompilerParams(vmem_limit_bytes=16 << 20),
         name="lower",
     )(place, own, other, weights, kept, taken, gain)

time: 137 us -> 136 us (level)
  transfers between devices with their start and end apart: 19 -> 19, of which waited for: 8 -> 8; matrix products, arithmetic and copies ran while one was open for 0% -> 0% of each run, Pallas kernels for 16% -> 17%
where the time goes in v6:
time: 136 us
  blocking collectives  66.8 us (49%)
  Pallas kernels  28.9 us (21%)
  waiting for transfers between devices  20.1 us (15%)
  starting transfers between devices  19.8 us (15%)
    all_to_all x1, blocking collectives, per_device(): arrived = lax.all_to_all(dispatched, ('g', 'z', 'x', 'y'), 0, 0, tiled=True)  34.4 us
    all_to_all x1, blocking collectives, per_device(): returned = lax.all_to_all(summed, ('g', 'z', 'x', 'y'), 0, 0, tiled=True)  32.4 us
    ppermute x6, waiting for transfers between devices, crossed(): return lax.ppermute(array, ('z', 'x', 'c'), pairs)  12.1 us
    ppermute x6, starting transfers between devices, crossed(): return lax.ppermute(array, ('z', 'x', 'c'), pairs)  11.7 us
    pallas_call x1, Pallas kernels, attend(): pl.pallas_call(attend_kernel, out_shape=(*(jax.ShapeDtypeStruct((rows, KQ...  6.78 us
    ppermute x6, waiting for transfers between devices, around(): return lax.ppermute(array, ('y', 'c'), [(i, i ^ k) for i in range(4)])  6.7 us
    pallas_call x1, Pallas kernels, receive(): pl.pallas_call(receive_kernel, out_shape=(jax.ShapeDtypeStruct((D, 256),...  5.57 us
    ppermute x6, starting transfers between devices, around(): return lax.ppermute(array, ('y', 'c'), [(i, i ^ k) for i in range(4)])  4.19 us
  transfers between devices with their start and end apart: 19, of which 8 were waited for; matrix products, arithmetic and copies ran while one was open for 0% of the time, Pallas kernels for 17%

profile of v6, /device:TPU:0, one launch (start us, length us, event | category | flops | bytes accessed | tf_op | source)
XLA Modules:
  0.0 136.2 jit_solution(2199759857926851473)
XLA Ops:
  0.1 6.8 %attend.1 = (bf16[4,6144]{1,0:T(4,128)(2,1)S(1)}, bf16[4,6144]{1,0:T(4,128)(2,1)S(1)}, bf16[4,6144]{1,0:T(4,128)(2,1)S(1)}, bf16[4,6144]{1,0:T(4,128)(2,1)S(1)},...) custom-call(s32[4]{0:T(128)} %lengths.1, ...), custom_call_target="tpu_custom_call" | custom-call | flops 536870912 | bytes 8388608 | tf_op jit(solution)/shard_map/attend/pallas_call | solution.py:189
  6.9 0.6 collective-permute-start
  7.5 1.7 %collective-permute-start.1 = (bf16[4,6144]{1,0:T(4,128)(2,1)S(1)}, bf16[4,6144]{1,0:T(4,128)(2,1)S(1)}, u32[]{:S(2)}, u32[]{:S(2)}) collective-permute-start(bf16[4,6144]{1,0:T(4,128)(2,1)S(1)} %get-tuple-element.50), channel_id=1, source_target_pairs={{0,2},{1,3},{2,0},{3,1},{4,6},{5,7},{6,4},{7,5},{8,10},{9,11},{10,... | collective-permute-start | bytes 147464 | tf_op jit(solution)/shard_map/ppermute | solution.py:44
  9.1 0.5 collective-permute-start.6
  9.7 1.9 %collective-permute-done.1 = bf16[4,6144]{1,0:T(4,128)(2,1)S(1)} collective-permute-done((bf16[4,6144]{1,0:T(4,128)(2,1)S(1)}, bf16[4,6144]{1,0:T(4,128)(2,1)S(1)}, u32[]{:S(2)}, u32[]{:S(2)}) %collective-permute-start.1) | collective-permute-done | bytes 49184 | tf_op jit(solution)/shard_map/ppermute | solution.py:44
  11.5 1.6 %collective-permute-done.2 = bf16[4,6144]{1,0:T(4,128)(2,1)S(1)} collective-permute-done((bf16[4,6144]{1,0:T(4,128)(2,1)S(1)}, bf16[4,6144]{1,0:T(4,128)(2,1)S(1)}, u32[]{:S(2)}, u32[]{:S(2)}) %collective-permute-start.2) | collective-permute-done | bytes 49184 | tf_op jit(solution)/shard_map/ppermute | solution.py:44
  13.5 0.4 collective-permute-start.11
  14.0 2.3 %collective-permute-start.12 = (bf16[112,4096]{1,0:T(8,128)(2,1)S(1)}, bf16[112,4096]{1,0:T(8,128)(2,1)S(1)}, u32[]{:S(2)}, u32[]{:S(2)}) collective-permute-start(bf16[112,4096]{1,0:T(8,128)(2,1)S(1)} %get-tuple-element.75), channel_id=1, source_target_pairs={{0,67},{1,66},{2,1},{3,0},{64,3},{65,2},{66,65},{67,64},{4,71},{5,... | collective-permute-start | bytes 2752520 | tf_op jit(solution)/shard_map/ppermute | solution.py:40
  16.3 4.1 %collective-permute-start.5 = (bf16[16,4608]{1,0:T(8,128)(2,1)S(1)}, bf16[16,4608]{1,0:T(8,128)(2,1)S(1)}, u32[]{:S(2)}, u32[]{:S(2)}) collective-permute-start(bf16[16,4608]{1,0:T(8,128)(2,1)S(1)} %get-tuple-element.95), channel_id=1, source_target_pairs={{0,48},{1,13},{4,52},{5,1},{8,56},{9,5},{12,60},{13,9},{16,0},{17,... | collective-permute-start | bytes 442376 | tf_op jit(solution)/shard_map/ppermute | solution.py:55
  20.4 1.9 %collective-permute-start.4 = (bf16[16,4608]{1,0:T(8,128)(2,1)S(1)}, bf16[16,4608]{1,0:T(8,128)(2,1)S(1)}, u32[]{:S(2)}, u32[]{:S(2)}) collective-permute-start(bf16[16,4608]{1,0:T(8,128)(2,1)S(1)} %get-tuple-element.97), channel_id=1, source_target_pairs={{0,32},{1,9},{4,36},{5,13},{8,40},{9,1},{12,44},{13,5},{16,48},{17... | collective-permute-start | bytes 442376 | tf_op jit(solution)/shard_map/ppermute | solution.py:55
  22.3 0.8 collective-permute-done.5.b3
  23.1 5.3 %collective-permute-done.3.b1 = bf16[16,4608]{1,0:T(8,128)(2,1)S(1)} collective-permute-done((bf16[16,4608]{1,0:T(8,128)(2,1)S(1)}, bf16[16,4608]{1,0:T(8,128)(2,1)S(1)}, u32[]{:S(2)}, u32[]{:S(2)}) %collective-permute-start.3) | collective-permute-done | bytes 147488 | tf_op jit(solution)/shard_map/ppermute | solution.py:55
  28.3 0.7 spread.1
  29.0 1.6 %collective-permute-start.8 = (bf16[64,4224]{1,0:T(8,128)(2,1)S(1)}, bf16[64,4224]{1,0:T(8,128)(2,1)S(1)}, u32[]{:S(2)}, u32[]{:S(2)}) collective-permute-start(bf16[64,4224]{1,0:T(8,128)(2,1)S(1)} %get-tuple-element.61), channel_id=1, source_target_pairs={{0,4},{1,17},{4,8},{5,21},{8,12},{9,25},{12,0},{13,29},{16,20},{17... | collective-permute-start | bytes 1622024 | tf_op jit(solution)/shard_map/ppermute | solution.py:55
  30.6 2.7 %collective-permute-start.9 = (bf16[64,4224]{1,0:T(8,128)(2,1)S(1)}, bf16[64,4224]{1,0:T(8,128)(2,1)S(1)}, u32[]{:S(2)}, u32[]{:S(2)}) collective-permute-start(bf16[64,4224]{1,0:T(8,128)(2,1)S(1)} %get-tuple-element.62), channel_id=1, source_target_pairs={{0,8},{1,33},{4,12},{5,37},{8,0},{9,41},{12,4},{13,45},{16,24},{17... | collective-permute-start | bytes 1622024 | tf_op jit(solution)/shard_map/ppermute | solution.py:55
  33.3 1.4 %collective-permute-start.10 = (bf16[64,4224]{1,0:T(8,128)(2,1)S(1)}, bf16[64,4224]{1,0:T(8,128)(2,1)S(1)}, u32[]{:S(2)}, u32[]{:S(2)}) collective-permute-start(bf16[64,4224]{1,0:T(8,128)(2,1)S(1)} %get-tuple-element.63), channel_id=1, source_target_pairs={{0,12},{1,49},{4,0},{5,53},{8,4},{9,57},{12,8},{13,61},{16,28},{17... | collective-permute-start | bytes 1622024 | tf_op jit(solution)/shard_map/ppermute | solution.py:55
  34.9 1.7 %own_quarter.1.own = bf16[112,4096]{1,0:T(8,128)(2,1)S(1)} custom-call(s32[4]{0:T(128)S(1)} %pad_add_fusion.place, bf16[112,16384]{1,0:T(8,128)(2,1)} %bitcast.16), custom_call_target="tpu_custom_call" | custom-call | tf_op jit(solution)/shard_map/own_quarter/pallas_call | solution.py:265
  36.7 3.7 %load_lower.1.weights = bf16[640,7168]{1,0:T(8,128)(2,1)S(1)} custom-call(bf16[320,7168]{1,0:T(8,128)(2,1)} %first, bf16[320,7168]{1,0:T(8,128)(2,1)} %collective-permute-done.7.second), custom_call_target="tpu_custom_call" | custom-call | bytes 18350080 | tf_op jit(solution)/shard_map/load_lower/pallas_call | solution.py:376
  40.4 6.0 %collective-permute-done.9.r2 = bf16[64,4224]{1,0:T(8,128)(2,1)S(1)} collective-permute-done((bf16[64,4224]{1,0:T(8,128)(2,1)S(1)}, bf16[64,4224]{1,0:T(8,128)(2,1)S(1)}, u32[]{:S(2)}, u32[]{:S(2)}) %collective-permute-start.9) | collective-permute-done | bytes 540704 | tf_op jit(solution)/shard_map/ppermute | solution.py:55
  46.4 1.9 %project.1 = (f32[112,256]{1,0:T(8,128)S(1)}, bf16[112,256]{1,0:T(8,128)(2,1)S(1)}, bf16[112,256]{1,0:T(8,128)(2,1)S(1)}, bf16[112,256]{1,0:T(8,128)(2,1)S(1)}, bf16[256,128]{1,0:T(8,128)(2,1)S(1)}) custom-call(s32[4]{0:T(128)S(1)} %pad_add_fusion.place, bf16[64,4224]{1,0:T(8,128)(2,1)S(1)} %get-tuple-element.68.r0, ...), custom_call_target="tpu_custom_call" | custom-call | tf_op jit(solution)/shard_map/project/pallas_call | solution.py:297
  48.7 1.6 %collective-permute-start.15 = (bf16[112,256]{1,0:T(8,128)(2,1)S(1)}, bf16[112,256]{1,0:T(8,128)(2,1)S(1)}, u32[]{:S(2)}, u32[]{:S(2)}) collective-permute-start(bf16[112,256]{1,0:T(8,128)(2,1)S(1)} %get-tuple-element.79), channel_id=1, source_target_pairs={{0,3},{1,2},{2,1},{3,0},{4,7},{5,6},{6,5},{7,4},{8,11},{9,10},{10,... | collective-permute-start | bytes 172040 | tf_op jit(solution)/shard_map/ppermute | solution.py:44
  50.3 2.9 %collective-permute-done.14.r2 = bf16[112,256]{1,0:T(8,128)(2,1)S(1)} collective-permute-done((bf16[112,256]{1,0:T(8,128)(2,1)S(1)}, bf16[112,256]{1,0:T(8,128)(2,1)S(1)}, u32[]{:S(2)}, u32[]{:S(2)}) %collective-permute-start.14) | collective-permute-done | bytes 57376 | tf_op jit(solution)/shard_map/ppermute | solution.py:44
  53.2 0.3 collective-permute-done.15.r3
  53.5 1.1 mix.1
  54.6 34.4 %all_to_all.10.arrived = bf16[64,112,128]{2,1,0:T(8,128)(2,1)S(1)} all-to-all(bf16[64,112,128]{2,1,0:T(8,128)(2,1)S(1)} %mix.1), channel_id=1, replica_groups=mesh['g'=2,'z'=4,'x'=4,'y'=2,'c'=2] {'g','z','x','y'}, dimensions={0} | all-to-all | bytes 3670016 | tf_op jit(solution)/shard_map/all_to_all | solution.py:597
  89.0 5.6 %receive.1 = (bf16[7168,256]{1,0:T(8,128)(2,1)S(1)}, f32[8,256]{1,0:T(8,128)S(1)}, bf16[16,7168]{1,0:T(8,128)(2,1)S(1)}, bf16[16,7168]{1,0:T(8,128)(2,1)S(1)}, bf16[640,7168]{1,0:T(8,128)(2,1)S(1)}) custom-call(s32[4]{0:T(128)S(1)} %pad_add_fusion.place, bf16[64,112,128]{2,1,0:T(8,128)(2,1)S(1)} %all_to_all.10.arrived, f32[64,112]{1,0:T(8,128)S(1)} %chunked.1.gains, ...), custom_call_target="tpu_custom_call" | custom-call | tf_op jit(solution)/shard_map/receive/pallas_call | solution.py:436
  94.5 0.6 collective-permute-start.18
  95.1 3.9 %expert.1 = (bf16[128,320]{1,0:T(8,128)(2,1)S(1)}, bf16[128,320]{1,0:T(8,128)(2,1)S(1)}) custom-call(s32[4]{0:T(128)S(1)} %pad_add_fusion.place, bf16[7168,256]{1,0:T(8,128)(2,1)S(1)} %get-tuple-element.82.seen, bf16[64,112,128]{2,1,0:T(8,128)(2,1)S(1)} %collective-permute-done.16.other, f32[8,256]{1,0:T(8,128)S(1)} %get-tuple-element.83.own_squares, ...), custom_call_target="tpu_custom_call" | custom-call | tf_op jit(solution)/shard_map/expert/pallas_call | solution.py:478
  99.2 1.3 collective-permute-done.17.other
  100.5 2.3 %lower.1 = bf16[64,2,7168]{2,1,0:T(2,128)(2,1)S(1)} custom-call(s32[4]{0:T(128)S(1)} %pad_add_fusion.place, bf16[128,320]{1,0:T(8,128)(2,1)S(1)} %get-tuple-element.85.own, bf16[128,320]{1,0:T(8,128)(2,1)S(1)} %collective-permute-done.17.other, bf16[640,7168]{1,0:T(8,128)(2,1)S(1)} %load_lower.1.weights, bf16[16,7168]{1,0:T(8,128)(2,1)S(1)} %get-tuple-element.88.kept, ...), custom_call_target="tpu_custom_call" | custom-call | tf_op jit(solution)/shard_map/lower/pallas_call | solution.py:509
  102.8 32.4 %all_to_all.11.returned = bf16[64,2,7168]{2,1,0:T(2,128)(2,1)S(1)} all-to-all(bf16[64,2,7168]{2,1,0:T(2,128)(2,1)S(1)} %lower.1), channel_id=1, replica_groups=mesh['g'=2,'z'=4,'x'=4,'y'=2,'c'=2] {'g','z','x','y'}, dimensions={0} | all-to-all | bytes 3670016 | tf_op jit(solution)/shard_map/all_to_all | solution.py:605
  135.2 1.0 combine.1
  (29 shorter events, 1.2 us)
Async XLA Ops:
  0.0 13.5 %collective-permute-start.7 = (bf16[320,7168]{1,0:T(8,128)(2,1)}, bf16[320,7168]{1,0:T(8,128)(2,1)}, u32[]{:S(2)}, u32[]{:S(2)}) collective-permute-start(bf16[320,7168]{1,0:T(8,128)(2,1)} %first), channel_id=1, source_target_pairs={{0,1},{1,0},{2,3},{3,2},{4,5},{5,4},{6,7},{7,6},{8,9},{9,8},{10,11... | collective-permute-start | bytes 13762568 | tf_op jit(solution)/shard_map/ppermute | solution.py:27
  0.1 34.7 %copy-start = (f32[7168]{0:T(1024)S(1)}, f32[7168]{0:T(1024)}, u32[]{:S(2)}) copy-start(f32[7168]{0:T(1024)} %param.22) | copy-start | bytes 86020
  6.9 2.7 %collective-permute-start = (bf16[4,6144]{1,0:T(4,128)(2,1)S(1)}, bf16[4,6144]{1,0:T(4,128)(2,1)S(1)}, u32[]{:S(2)}, u32[]{:S(2)}) collective-permute-start(bf16[4,6144]{1,0:T(4,128)(2,1)S(1)} %get-tuple-element.49), channel_id=1, source_target_pairs={{0,1},{1,0},{2,3},{3,2},{4,5},{5,4},{6,7},{7,6},{8,9},{9,8},{10,11... | collective-permute-start | bytes 147464 | tf_op jit(solution)/shard_map/ppermute | solution.py:44
  7.5 4.1 %collective-permute-start.1 = (bf16[4,6144]{1,0:T(4,128)(2,1)S(1)}, bf16[4,6144]{1,0:T(4,128)(2,1)S(1)}, u32[]{:S(2)}, u32[]{:S(2)}) collective-permute-start(bf16[4,6144]{1,0:T(4,128)(2,1)S(1)} %get-tuple-element.50), channel_id=1, source_target_pairs={{0,2},{1,3},{2,0},{3,1},{4,6},{5,7},{6,4},{7,5},{8,10},{9,11},{10,... | collective-permute-start | bytes 147464 | tf_op jit(solution)/shard_map/ppermute | solution.py:44
  9.1 4.0 %collective-permute-start.2 = (bf16[4,6144]{1,0:T(4,128)(2,1)S(1)}, bf16[4,6144]{1,0:T(4,128)(2,1)S(1)}, u32[]{:S(2)}, u32[]{:S(2)}) collective-permute-start(bf16[4,6144]{1,0:T(4,128)(2,1)S(1)} %get-tuple-element.51), channel_id=1, source_target_pairs={{0,3},{1,2},{2,1},{3,0},{4,7},{5,6},{6,5},{7,4},{8,11},{9,10},{10,... | collective-permute-start | bytes 147464 | tf_op jit(solution)/shard_map/ppermute | solution.py:44
  9.1 4.4 %collective-permute-start.6 = (bf16[112,4096]{1,0:T(8,128)(2,1)}, bf16[112,4096]{1,0:T(8,128)(2,1)S(1)}, u32[]{:S(2)}, u32[]{:S(2)}) collective-permute-start(bf16[112,4096]{1,0:T(8,128)(2,1)} %get-tuple-element.58), channel_id=1, source_target_pairs={{0,1},{1,0},{2,3},{3,2},{4,5},{5,4},{6,7},{7,6},{8,9},{9,8},{10,11... | collective-permute-start | bytes 2752520 | tf_op jit(solution)/shard_map/ppermute | solution.py:27
  13.5 32.9 %collective-permute-start.11 = (bf16[112,4096]{1,0:T(8,128)(2,1)S(1)}, bf16[112,4096]{1,0:T(8,128)(2,1)S(1)}, u32[]{:S(2)}, u32[]{:S(2)}) collective-permute-start(bf16[112,4096]{1,0:T(8,128)(2,1)S(1)} %get-tuple-element.74), channel_id=1, source_target_pairs={{0,2},{1,3},{2,64},{3,65},{64,66},{65,67},{66,0},{67,1},{4,6},{5,7... | collective-permute-start | bytes 2752520 | tf_op jit(solution)/shard_map/ppermute | solution.py:40
  14.0 32.5 %collective-permute-start.12 = (bf16[112,4096]{1,0:T(8,128)(2,1)S(1)}, bf16[112,4096]{1,0:T(8,128)(2,1)S(1)}, u32[]{:S(2)}, u32[]{:S(2)}) collective-permute-start(bf16[112,4096]{1,0:T(8,128)(2,1)S(1)} %get-tuple-element.75), channel_id=1, source_target_pairs={{0,67},{1,66},{2,1},{3,0},{64,3},{65,2},{66,65},{67,64},{4,71},{5,... | collective-permute-start | bytes 2752520 | tf_op jit(solution)/shard_map/ppermute | solution.py:40
  16.3 6.8 %collective-permute-start.5 = (bf16[16,4608]{1,0:T(8,128)(2,1)S(1)}, bf16[16,4608]{1,0:T(8,128)(2,1)S(1)}, u32[]{:S(2)}, u32[]{:S(2)}) collective-permute-start(bf16[16,4608]{1,0:T(8,128)(2,1)S(1)} %get-tuple-element.95), channel_id=1, source_target_pairs={{0,48},{1,13},{4,52},{5,1},{8,56},{9,5},{12,60},{13,9},{16,0},{17,... | collective-permute-start | bytes 442376 | tf_op jit(solution)/shard_map/ppermute | solution.py:55
  20.4 7.9 %collective-permute-start.3 = (bf16[16,4608]{1,0:T(8,128)(2,1)S(1)}, bf16[16,4608]{1,0:T(8,128)(2,1)S(1)}, u32[]{:S(2)}, u32[]{:S(2)}) collective-permute-start(bf16[16,4608]{1,0:T(8,128)(2,1)S(1)} %get-tuple-element.96), channel_id=1, source_target_pairs={{0,16},{1,5},{4,20},{5,9},{8,24},{9,13},{12,28},{13,1},{16,32},{17... | collective-permute-start | bytes 442376 | tf_op jit(solution)/shard_map/ppermute | solution.py:55
  20.4 7.9 %collective-permute-start.4 = (bf16[16,4608]{1,0:T(8,128)(2,1)S(1)}, bf16[16,4608]{1,0:T(8,128)(2,1)S(1)}, u32[]{:S(2)}, u32[]{:S(2)}) collective-permute-start(bf16[16,4608]{1,0:T(8,128)(2,1)S(1)} %get-tuple-element.97), channel_id=1, source_target_pairs={{0,32},{1,9},{4,36},{5,13},{8,40},{9,1},{12,44},{13,5},{16,48},{17... | collective-permute-start | bytes 442376 | tf_op jit(solution)/shard_map/ppermute | solution.py:55
  29.0 11.4 %collective-permute-start.8 = (bf16[64,4224]{1,0:T(8,128)(2,1)S(1)}, bf16[64,4224]{1,0:T(8,128)(2,1)S(1)}, u32[]{:S(2)}, u32[]{:S(2)}) collective-permute-start(bf16[64,4224]{1,0:T(8,128)(2,1)S(1)} %get-tuple-element.61), channel_id=1, source_target_pairs={{0,4},{1,17},{4,8},{5,21},{8,12},{9,25},{12,0},{13,29},{16,20},{17... | collective-permute-start | bytes 1622024 | tf_op jit(solution)/shard_map/ppermute | solution.py:55
  30.6 15.9 %collective-permute-start.9 = (bf16[64,4224]{1,0:T(8,128)(2,1)S(1)}, bf16[64,4224]{1,0:T(8,128)(2,1)S(1)}, u32[]{:S(2)}, u32[]{:S(2)}) collective-permute-start(bf16[64,4224]{1,0:T(8,128)(2,1)S(1)} %get-tuple-element.62), channel_id=1, source_target_pairs={{0,8},{1,33},{4,12},{5,37},{8,0},{9,41},{12,4},{13,45},{16,24},{17... | collective-permute-start | bytes 1622024 | tf_op jit(solution)/shard_map/ppermute | solution.py:55
  33.3 13.1 %collective-permute-start.10 = (bf16[64,4224]{1,0:T(8,128)(2,1)S(1)}, bf16[64,4224]{1,0:T(8,128)(2,1)S(1)}, u32[]{:S(2)}, u32[]{:S(2)}) collective-permute-start(bf16[64,4224]{1,0:T(8,128)(2,1)S(1)} %get-tuple-element.63), channel_id=1, source_target_pairs={{0,12},{1,49},{4,0},{5,53},{8,4},{9,57},{12,8},{13,61},{16,28},{17... | collective-permute-start | bytes 1622024 | tf_op jit(solution)/shard_map/ppermute | solution.py:55
  48.3 2.0 %collective-permute-start.13 = (bf16[112,256]{1,0:T(8,128)(2,1)S(1)}, bf16[112,256]{1,0:T(8,128)(2,1)S(1)}, u32[]{:S(2)}, u32[]{:S(2)}) collective-permute-start(bf16[112,256]{1,0:T(8,128)(2,1)S(1)} %get-tuple-element.77), channel_id=1, source_target_pairs={{0,1},{1,0},{2,3},{3,2},{4,5},{5,4},{6,7},{7,6},{8,9},{9,8},{10,11... | collective-permute-start | bytes 172040 | tf_op jit(solution)/shard_map/ppermute | solution.py:44
  48.4 4.8 %collective-permute-start.14 = (bf16[112,256]{1,0:T(8,128)(2,1)S(1)}, bf16[112,256]{1,0:T(8,128)(2,1)S(1)}, u32[]{:S(2)}, u32[]{:S(2)}) collective-permute-start(bf16[112,256]{1,0:T(8,128)(2,1)S(1)} %get-tuple-element.78), channel_id=1, source_target_pairs={{0,2},{1,3},{2,0},{3,1},{4,6},{5,7},{6,4},{7,5},{8,10},{9,11},{10,... | collective-permute-start | bytes 172040 | tf_op jit(solution)/shard_map/ppermute | solution.py:44
  48.7 4.8 %collective-permute-start.15 = (bf16[112,256]{1,0:T(8,128)(2,1)S(1)}, bf16[112,256]{1,0:T(8,128)(2,1)S(1)}, u32[]{:S(2)}, u32[]{:S(2)}) collective-permute-start(bf16[112,256]{1,0:T(8,128)(2,1)S(1)} %get-tuple-element.79), channel_id=1, source_target_pairs={{0,3},{1,2},{2,1},{3,0},{4,7},{5,6},{6,5},{7,4},{8,11},{9,10},{10,... | collective-permute-start | bytes 172040 | tf_op jit(solution)/shard_map/ppermute | solution.py:44
  89.0 6.2 %collective-permute-start.16 = (bf16[64,112,128]{2,1,0:T(8,128)(2,1)S(1)}, bf16[64,112,128]{2,1,0:T(8,128)(2,1)S(1)}, u32[]{:S(2)}, u32[]{:S(2)}) collective-permute-start(bf16[64,112,128]{2,1,0:T(8,128)(2,1)S(1)} %all_to_all.10.arrived), channel_id=1, source_target_pairs={{0,1},{1,0},{2,3},{3,2},{4,5},{5,4},{6,7},{7,6},{8,9},{9,8},{10,11... | collective-permute-start | bytes 5505032 | tf_op jit(solution)/shard_map/ppermute | solution.py:27
  94.5 4.6 %collective-permute-start.18 = (bf16[16,7168]{1,0:T(8,128)(2,1)S(1)}, bf16[16,7168]{1,0:T(8,128)(2,1)S(1)}, u32[]{:S(2)}, u32[]{:S(2)}) collective-permute-start(bf16[16,7168]{1,0:T(8,128)(2,1)S(1)} %get-tuple-element.89), channel_id=1, source_target_pairs={{0,1},{1,0},{2,3},{3,2},{4,5},{5,4},{6,7},{7,6},{8,9},{9,8},{10,11... | collective-permute-start | bytes 688136 | tf_op jit(solution)/shard_map/ppermute | solution.py:27
  99.1 1.4 %collective-permute-start.17 = (bf16[128,320]{1,0:T(8,128)(2,1)S(1)}, bf16[128,320]{1,0:T(8,128)(2,1)S(1)}, u32[]{:S(2)}, u32[]{:S(2)}) collective-permute-start(bf16[128,320]{1,0:T(8,128)(2,1)S(1)} %get-tuple-element.86), channel_id=1, source_target_pairs={{0,1},{1,0},{2,3},{3,2},{4,5},{5,4},{6,7},{7,6},{8,9},{9,8},{10,11... | collective-permute-start | bytes 245768 | tf_op jit(solution)/shard_map/ppermute | solution.py:27
